TPU v7x, 32 devices: a whole 2x2x4 slice. The times are simulated.
32 devices in a mesh: wide: 16 (over z, y, core), tensor: 2 (over x).
Axes of the slice: x: 2, y: 2, z: 4, core: 2. Of those that a mesh axis runs over, the one named last changes fastest.
Arguments:
- tokens_in: bfloat16 [18432, 512], P('wide'), may hold values from -6 to 6
- pre_gain: float32 [512], replicated, may hold values from 0.5 to 1.5
- pre_shift: float32 [512], replicated, may hold values from -0.5 to 0.5
- qkv_weight: bfloat16 [512, 3, 512], P(None, None, 'tensor'), may hold values from -0.25 to 0.25
- qv_bias: float32 [2, 512], P(None, 'tensor'), may hold values from -0.5 to 0.5
- proj_weight: bfloat16 [512, 512], P('tensor'), may hold values from -1.5 to 1.5
- proj_bias: float32 [512], replicated, may hold values from -0.5 to 0.5
- mid_gain: float32 [512], replicated, may hold values from 0.5 to 1.5
- mid_shift: float32 [512], replicated, may hold values from -0.5 to 0.5
- hidden_weight: bfloat16 [512, 2048], P(None, 'tensor'), may hold values from -0.25 to 0.25
- hidden_bias: float32 [2048], P('tensor'), may hold values from -0.5 to 0.5
- output_weight: bfloat16 [2048, 512], P('tensor'), may hold values from -0.125 to 0.125
- output_bias: float32 [512], replicated, may hold values from -0.5 to 0.5
- moe_gain: float32 [512], replicated, may hold values from 0.5 to 1.5
- moe_shift: float32 [512], replicated, may hold values from -0.5 to 0.5
- router_weight: float32 [512, 16], replicated, may hold values from -0.1875 to 0.1875
- expert_in: bfloat16 [16, 512, 2048], P('wide', None, 'tensor'), may hold values from -0.25 to 0.25
- expert_in_bias: float32 [16, 2048], P('wide', 'tensor'), may hold values from -0.5 to 0.5
- expert_out: bfloat16 [16, 2048, 512], P('wide', 'tensor'), may hold values from -2 to 2
- expert_out_bias: float32 [16, 512], P('wide'), may hold values from -5 to 5
- expert_ids: int32 [18432, 2], P('wide'), may hold values from 0 to 15, all different within a row
- priority: int32 [16, 1152], P('wide'), may hold values from 0 to 1151, each once within a row
- cotangent: float32 [18432, 512], P('wide'), may hold values from -6 to 6
Outputs:
- block_out: bfloat16 [18432, 512], P('wide')
- tokens_grad: float32 [18432, 512], P('wide')
- pre_gain_grad: float32 [512], replicated
- pre_shift_grad: float32 [512], replicated
- qkv_weight_grad: float32 [512, 3, 512], P(None, None, 'tensor')
- qv_bias_grad: float32 [2, 512], P(None, 'tensor')
- proj_weight_grad: float32 [512, 512], P('tensor')
- proj_bias_grad: float32 [512], replicated
- mid_gain_grad: float32 [512], replicated
- mid_shift_grad: float32 [512], replicated
- hidden_weight_grad: float32 [512, 2048], P(None, 'tensor')
- hidden_bias_grad: float32 [2048], P('tensor')
- output_weight_grad: float32 [2048, 512], P('tensor')
- output_bias_grad: float32 [512], replicated
- moe_gain_grad: float32 [512], replicated
- moe_shift_grad: float32 [512], replicated
- router_weight_grad: float32 [512, 16], replicated
- expert_in_grad: float32 [16, 512, 2048], P('wide', None, 'tensor')
- expert_in_bias_grad: float32 [16, 2048], P('wide', 'tensor')
- expert_out_grad: float32 [16, 2048, 512], P('wide', 'tensor')
- expert_out_bias_grad: float32 [16, 512], P('wide')
Inputs may be any that keep to these rules, and one draw needn't show every extreme that they name: `priority`: each row is a permutation of the 1152 ranks: the order in which one index's tokens claim expert slots. `expert_ids`: a token's two experts differ.
All inputs are finite; a program needn't handle non-finite values.
Results may differ from a plain program's by a relative error of at most 0.022.
Values may be sent and summed in bfloat16 or wider, within the bound.
A program may use at most 128 MiB of HBM per device.

v0:
```python
import jax
import jax.numpy as jnp
from jax import lax
from jax.sharding import PartitionSpec as P

HEAD_DIM = 64
PATCHES = 144


def layer_norm(values, gain, shift):
    centered = values - jnp.mean(values, axis=-1, keepdims=True)
    variance = jnp.mean(centered * centered, axis=-1, keepdims=True)
    return centered * lax.rsqrt(variance + 1e-06) * gain + shift


def norm_grad(values, gain, shift, upstream):
    _, pullback = jax.vjp(layer_norm, values, gain, shift)
    return pullback(upstream)


def gelu_grad(inner, upstream):
    _, pullback = jax.vjp(jax.nn.gelu, inner)
    return pullback(upstream)[0]


def slot_tables(choice_ids, ranks, capacity, experts):
    count = choice_ids.shape[0]
    order_keys = jnp.concatenate([ranks, ranks + count])
    flat_ids = jnp.concatenate([choice_ids[:, 0], choice_ids[:, 1]])
    earlier = (order_keys[None, :] < order_keys[:, None]) & (flat_ids[None, :] == flat_ids[:, None])
    position = jnp.sum(earlier.astype(jnp.int32), axis=1)
    kept = position < capacity
    position = position.reshape(2, count)
    kept = kept.reshape(2, count)
    columns = jnp.arange(experts * capacity, dtype=jnp.int32)
    target = choice_ids.T * capacity + position
    tables = (target[:, :, None] == columns[None, None, :]) & kept[:, :, None]
    return (tables, kept)


def shards(
    tokens_in,
    pre_gain,
    pre_shift,
    qkv_weight,
    qv_bias,
    proj_weight,
    proj_bias,
    mid_gain,
    mid_shift,
    hidden_weight,
    hidden_bias,
    output_weight,
    output_bias,
    moe_gain,
    moe_shift,
    router_weight,
    expert_in,
    expert_in_bias,
    expert_out,
    expert_out_bias,
    expert_ids,
    priority,
    cotangent,
):
    tokens = tokens_in.shape[0]
    model_width = tokens_in.shape[1]
    local_heads = qkv_weight.shape[2] // HEAD_DIM
    images = tokens // PATCHES
    experts = router_weight.shape[1]
    capacity = tokens // experts
    score_scale = float(HEAD_DIM) ** (-0.5)
    highest = lax.Precision.HIGHEST
    residual = tokens_in.astype(jnp.float32)
    normed_pre = layer_norm(residual, pre_gain, pre_shift)
    lowered_pre = normed_pre.astype(jnp.bfloat16)
    blank = jnp.zeros_like(qv_bias[0])
    qkv_shift = jnp.stack([qv_bias[0], blank, qv_bias[1]])
    qkv = (
        jnp.einsum("td,dsk->tsk", lowered_pre, qkv_weight, preferred_element_type=jnp.float32)
        + qkv_shift
    ).astype(jnp.bfloat16)
    grid = qkv.reshape(images, PATCHES, 3, local_heads, HEAD_DIM)
    query, keys, values = (grid[:, :, 0], grid[:, :, 1], grid[:, :, 2])
    scores = (
        jnp.einsum("bqhd,bkhd->bhqk", query, keys, preferred_element_type=jnp.float32) * score_scale
    )
    log_total = jax.nn.logsumexp(scores, axis=-1, keepdims=True)
    weights = jnp.exp(scores - log_total).astype(jnp.bfloat16)
    context = jnp.einsum("bhqk,bkhd->bqhd", weights, values, preferred_element_type=jnp.float32)
    context = context.astype(jnp.bfloat16).reshape(tokens, local_heads * HEAD_DIM)
    branch = lax.psum(jnp.dot(context, proj_weight, preferred_element_type=jnp.float32), "tensor")
    first = residual + branch + proj_bias
    normed_mid = layer_norm(first, mid_gain, mid_shift)
    lowered_mid = normed_mid.astype(jnp.bfloat16)
    inner = jnp.dot(lowered_mid, hidden_weight, preferred_element_type=jnp.float32) + hidden_bias
    activated = jax.nn.gelu(inner).astype(jnp.bfloat16)
    partial_out = jnp.dot(activated, output_weight, preferred_element_type=jnp.float32)
    second = first + lax.psum(partial_out, "tensor") + output_bias
    normed_moe = layer_norm(second, moe_gain, moe_shift)
    lowered_moe = normed_moe.astype(jnp.bfloat16)
    route = jax.nn.softmax(jnp.dot(normed_moe, router_weight, precision=highest), axis=-1)
    tables, kept = slot_tables(expert_ids, priority[0], capacity, experts)
    tables = tables.astype(jnp.bfloat16)
    dispatch = tables[0] + tables[1]
    buffers = jnp.einsum("tk,td->kd", dispatch, lowered_moe, preferred_element_type=jnp.float32)
    buffers = buffers.astype(jnp.bfloat16).reshape(experts, capacity, model_width)
    arrived = lax.all_to_all(buffers, "wide", split_axis=0, concat_axis=1, tiled=True)
    expert_inner = (
        jnp.einsum("erd,edf->erf", arrived, expert_in, preferred_element_type=jnp.float32)
        + expert_in_bias[:, None, :]
    )
    expert_act = jax.nn.gelu(expert_inner).astype(jnp.bfloat16)
    expert_partial = jnp.einsum(
        "erf,efd->erd", expert_act, expert_out, preferred_element_type=jnp.float32
    )
    expert_result = (
        lax.psum(expert_partial.astype(jnp.bfloat16), "tensor").astype(jnp.float32)
        + expert_out_bias[:, None, :]
    ).astype(jnp.bfloat16)
    returned = lax.all_to_all(
        expert_result, "wide", split_axis=1, concat_axis=0, tiled=True
    ).reshape(experts * capacity, model_width)
    picked = jnp.einsum("jtk,kd->jtd", tables, returned, preferred_element_type=jnp.float32)
    expert_range = jnp.arange(experts, dtype=jnp.int32)
    chosen = (expert_ids.T[:, :, None] == expert_range[None, None, :]).astype(jnp.float32) * kept[
        :, :, None
    ].astype(jnp.float32)
    gates = jnp.sum(chosen * route[None], axis=-1)
    mixture = jnp.sum(gates[:, :, None] * picked, axis=0)
    block_out = (second + mixture).astype(jnp.bfloat16)
    gate_grad = jnp.sum(picked * cotangent[None], axis=-1)
    weighted = (gates[:, :, None] * cotangent[None]).astype(jnp.bfloat16)
    slot_grad = jnp.einsum("jtk,jtd->kd", tables, weighted, preferred_element_type=jnp.float32)
    slot_grad = slot_grad.astype(jnp.bfloat16).reshape(experts, capacity, model_width)
    result_grad = lax.all_to_all(slot_grad, "wide", split_axis=0, concat_axis=1, tiled=True)
    expert_out_bias_grad = jnp.sum(result_grad.astype(jnp.float32), axis=1)
    expert_out_grad = jnp.einsum(
        "erf,erd->efd", expert_act, result_grad, preferred_element_type=jnp.float32
    )
    act_grad = jnp.einsum(
        "erd,efd->erf", result_grad, expert_out, preferred_element_type=jnp.float32
    )
    expert_inner_grad = gelu_grad(expert_inner, act_grad).astype(jnp.bfloat16)
    expert_in_bias_grad = jnp.sum(expert_inner_grad.astype(jnp.float32), axis=1)
    expert_in_grad = jnp.einsum(
        "erd,erf->edf", arrived, expert_inner_grad, preferred_element_type=jnp.float32
    )
    arrived_partial = jnp.einsum(
        "erf,edf->erd", expert_inner_grad, expert_in, preferred_element_type=jnp.float32
    )
    arrived_grad = lax.psum(arrived_partial.astype(jnp.bfloat16), "tensor")
    buffer_grad = lax.all_to_all(
        arrived_grad, "wide", split_axis=1, concat_axis=0, tiled=True
    ).reshape(experts * capacity, model_width)
    moe_input_grad = jnp.dot(dispatch, buffer_grad, preferred_element_type=jnp.float32)
    route_grad = jnp.sum(gate_grad[:, :, None] * chosen, axis=0)
    logit_grad = route * (route_grad - jnp.sum(route * route_grad, axis=-1, keepdims=True))
    router_grad = jnp.einsum("td,te->de", normed_moe, logit_grad, precision=highest)
    moe_input_grad = moe_input_grad + jnp.einsum(
        "te,de->td", logit_grad, router_weight, precision=highest
    )
    second_part, moe_gain_grad, moe_shift_grad = norm_grad(
        second, moe_gain, moe_shift, moe_input_grad
    )
    second_grad = cotangent + second_part
    lowered_second = second_grad.astype(jnp.bfloat16)
    output_bias_grad = jnp.sum(second_grad, axis=0)
    output_weight_grad = jnp.einsum(
        "tf,td->fd", activated, lowered_second, preferred_element_type=jnp.float32
    )
    activated_grad = jnp.einsum(
        "td,fd->tf", lowered_second, output_weight, preferred_element_type=jnp.float32
    )
    inner_grad = gelu_grad(inner, activated_grad).astype(jnp.bfloat16)
    hidden_bias_grad = jnp.sum(inner_grad.astype(jnp.float32), axis=0)
    hidden_weight_grad = jnp.einsum(
        "td,tf->df", lowered_mid, inner_grad, preferred_element_type=jnp.float32
    )
    mid_partial = jnp.einsum(
        "tf,df->td", inner_grad, hidden_weight, preferred_element_type=jnp.float32
    )
    mid_grad = lax.psum(mid_partial, "tensor")
    first_part, mid_gain_grad, mid_shift_grad = norm_grad(first, mid_gain, mid_shift, mid_grad)
    first_grad = second_grad + first_part
    proj_bias_grad = jnp.sum(first_grad, axis=0)
    branch_grad = first_grad.astype(jnp.bfloat16)
    proj_weight_grad = jnp.einsum(
        "tk,td->kd", context, branch_grad, preferred_element_type=jnp.float32
    )
    context_grad = jnp.einsum(
        "td,kd->tk", branch_grad, proj_weight, preferred_element_type=jnp.float32
    )
    context_grad = context_grad.astype(jnp.bfloat16).reshape(images, PATCHES, local_heads, HEAD_DIM)
    scores = (
        jnp.einsum("bqhd,bkhd->bhqk", query, keys, preferred_element_type=jnp.float32) * score_scale
    )
    probs = jnp.exp(scores - log_total)
    weights = probs.astype(jnp.bfloat16)
    value_grad = jnp.einsum(
        "bhqk,bqhd->bkhd", weights, context_grad, preferred_element_type=jnp.float32
    )
    prob_grad = jnp.einsum(
        "bqhd,bkhd->bhqk", context_grad, values, preferred_element_type=jnp.float32
    )
    score_grad = (probs * (prob_grad - jnp.sum(probs * prob_grad, axis=-1, keepdims=True))).astype(
        jnp.bfloat16
    )
    query_grad = (
        jnp.einsum("bhqk,bkhd->bqhd", score_grad, keys, preferred_element_type=jnp.float32)
        * score_scale
    )
    key_grad = (
        jnp.einsum("bhqk,bqhd->bkhd", score_grad, query, preferred_element_type=jnp.float32)
        * score_scale
    )
    qkv_grad = jnp.stack([query_grad, key_grad, value_grad], axis=2).astype(jnp.bfloat16)
    qkv_grad = qkv_grad.reshape(tokens, 3, local_heads * HEAD_DIM)
    qkv_sums = jnp.sum(qkv_grad.astype(jnp.float32), axis=0)
    qv_bias_grad = jnp.stack([qkv_sums[0], qkv_sums[2]])
    qkv_weight_grad = jnp.einsum(
        "td,tsk->dsk", lowered_pre, qkv_grad, preferred_element_type=jnp.float32
    )
    pre_partial = jnp.einsum(
        "tsk,dsk->td", qkv_grad, qkv_weight, preferred_element_type=jnp.float32
    )
    pre_grad = lax.psum(pre_partial.astype(jnp.bfloat16), "tensor").astype(jnp.float32)
    input_part, pre_gain_grad, pre_shift_grad = norm_grad(residual, pre_gain, pre_shift, pre_grad)
    tokens_grad = first_grad + input_part
    shared = (
        lax.psum(pre_gain_grad.astype(jnp.bfloat16), "wide").astype(jnp.float32),
        lax.psum(pre_shift_grad.astype(jnp.bfloat16), "wide").astype(jnp.float32),
        lax.psum(qkv_weight_grad.astype(jnp.bfloat16), "wide").astype(jnp.float32),
        lax.psum(qv_bias_grad.astype(jnp.bfloat16), "wide").astype(jnp.float32),
        lax.psum(proj_weight_grad.astype(jnp.bfloat16), "wide").astype(jnp.float32),
        lax.psum(proj_bias_grad.astype(jnp.bfloat16), "wide").astype(jnp.float32),
        lax.psum(mid_gain_grad.astype(jnp.bfloat16), "wide").astype(jnp.float32),
        lax.psum(mid_shift_grad.astype(jnp.bfloat16), "wide").astype(jnp.float32),
        lax.psum(hidden_weight_grad.astype(jnp.bfloat16), "wide").astype(jnp.float32),
        lax.psum(hidden_bias_grad.astype(jnp.bfloat16), "wide").astype(jnp.float32),
        lax.psum(output_weight_grad.astype(jnp.bfloat16), "wide").astype(jnp.float32),
        lax.psum(output_bias_grad.astype(jnp.bfloat16), "wide").astype(jnp.float32),
        lax.psum(moe_gain_grad.astype(jnp.bfloat16), "wide").astype(jnp.float32),
        lax.psum(moe_shift_grad.astype(jnp.bfloat16), "wide").astype(jnp.float32),
        lax.psum(router_grad.astype(jnp.bfloat16), "wide").astype(jnp.float32),
    )
    return (
        (block_out, tokens_grad)
        + tuple(shared)
        + (expert_in_grad, expert_in_bias_grad, expert_out_grad, expert_out_bias_grad)
    )


def solution(mesh):
    return jax.shard_map(
        shards,
        mesh=mesh,
        in_specs=(
            P("wide", None),
            P(),
            P(),
            P(None, None, "tensor"),
            P(None, "tensor"),
            P("tensor", None),
            P(),
            P(),
            P(),
            P(None, "tensor"),
            P("tensor"),
            P("tensor", None),
            P(),
            P(),
            P(),
            P(),
            P("wide", None, "tensor"),
            P("wide", "tensor"),
            P("wide", "tensor", None),
            P("wide", None),
            P("wide", None),
            P("wide", None),
            P("wide", None),
        ),
        out_specs=(
            P("wide", None),
            P("wide", None),
            P(),
            P(),
            P(None, None, "tensor"),
            P(None, "tensor"),
            P("tensor", None),
            P(),
            P(),
            P(),
            P(None, "tensor"),
            P("tensor"),
            P("tensor", None),
            P(),
            P(),
            P(),
            P(),
            P("wide", None, "tensor"),
            P("wide", "tensor"),
            P("wide", "tensor", None),
            P("wide", None),
        ),
        check_vma=False,
    )
```

profile of v0, /device:TPU:0, one launch (start us, length us, event | category | flops | bytes accessed | tf_op | source)
XLA Modules:
  0.0 756.1 jit_solution(15224801418845153822)
XLA Ops:
  12.7 2.5 fusion.28
  15.3 6.4 reshape.323
  21.7 4.6 fusion.117
  26.3 2.7 copy.183
  29.1 3.7 copy.182
  32.8 3.4 copy.184
  47.6 71.1 %all-reduce.10.cloned.1.call-done = f32[1152,512]{1,0:T(8,128)} async-done(((f32[1152,512]{1,0:T(8,128)}), f32[1152,512]{1,0:T(8,128)}) %all-reduce.10.cloned.1.call-update) | async-done | bytes 2359312 | tf_op jit(solution)/shard_map/psum | solution.py:92
  126.5 3.1 fusion.108
  129.6 4.4 convert_reduce_fusion
  134.1 4.5 fusion.5
  138.6 59.8 %all-reduce.12.cloned.1.call-done = f32[1152,512]{1,0:T(8,128)} async-done(((f32[1152,512]{1,0:T(8,128)}), f32[1152,512]{1,0:T(8,128)}) %all-reduce.12.cloned.1.call-update) | async-done | bytes 2359312 | tf_op jit(solution)/shard_map/psum | solution.py:99
  198.4 2.9 fusion.114
  202.4 2.8 convolution_convert_fusion.2
  205.2 6.1 all-to-all-start
  211.3 3.1 copy.147
  214.4 2.5 fusion.120
  218.2 4.0 fusion.34
  222.2 14.3 %all-to-all-done = bf16[16,72,512]{2,1,0:T(8,128)(2,1)} async-done(((bf16[16,72,512]{2,1,0:T(8,128)(2,1)}), bf16[16,72,512]{2,1,0:T(8,128)(2,1)}, u32[]{:S(2)}, u32[]{:S(2)}) %all-to-all-start) | async-done | bytes 1179680 | tf_op jit(solution)/shard_map/all_to_all | solution.py:108
  236.5 7.5 all-to-all-start.2
  244.1 3.0 convolution_add_fusion
  249.2 2.7 fusion.38
  251.9 17.3 %all-to-all-done.2 = bf16[16,72,512]{2,1,0:T(8,128)(2,1)} async-done(((bf16[16,72,512]{2,1,0:T(8,128)(2,1)}), bf16[16,72,512]{2,1,0:T(8,128)(2,1)}, u32[]{:S(2)}, u32[]{:S(2)}) %all-to-all-start.2) | async-done | bytes 1179680 | tf_op jit(solution)/shard_map/all_to_all | solution.py:136
  269.2 7.1 convert_reduce_fusion.1
  277.8 2.4 fusion.39
  280.3 70.8 %all-reduce.20.cloned.1.call-done = (bf16[1,1152,512]{2,1,0:T(8,128)(2,1)}, bf16[1,1152,512]{2,1,0:T(8,128)(2,1)}) async-done(((bf16[1,1152,512]{2,1,0:T(8,128)(2,1)}, bf16[1,1152,512]{2,1,0:T(8,128)(2,1)}), (bf16[1,1152,512]{2,1,0:T(8,128)(2,1)}, bf16[1,1152,512]{2,1,0:T(8,128)(2,1)})) %all-reduce.20.cloned.1.call-update) | async-done | bytes 2359312 | tf_op jit(solution)/shard_map/psum | solution.py:118
  352.6 10.8 %copy.192 = bf16[1,1152,512]{2,0,1:T(2,128)(2,1)} copy(bf16[1,1152,512]{2,1,0:T(8,128)(2,1)S(1)} %add_convert_fusion.1) | data formatting | bytes 2359296 | tf_op jit(solution)/shard_map/convert_element_type | solution.py:120
  363.9 9.7 %reduce.12 = bf16[1152,512]{1,0:T(8,128)(2,1)} reduce(bf16[1152,1,512]{2,1,0:T(2,128)(2,1)} %bitcast.128, bf16[]{:T(256)} %broadcast.278), dimensions={1}, to_apply=%bitcast.125.reduce_sub_computation | reduce | bytes 2359298
  373.6 4.0 reshape.329
  377.6 5.7 all-to-all-start.1
  383.3 7.3 copy.191
  390.6 9.7 %reduce.11 = bf16[1152,512]{1,0:T(8,128)(2,1)} reduce(bf16[1152,1,512]{2,1,0:T(2,128)(2,1)} %bitcast.129, bf16[]{:T(256)} %broadcast.278), dimensions={1}, to_apply=%bitcast.124.reduce_sub_computation | reduce | bytes 2359298
  400.3 4.0 reshape.331
  404.3 4.2 all-to-all-done.1
  408.5 7.5 all-to-all-start.3
  416.1 6.4 reshape.330
  422.4 6.0 copy.144
  428.5 7.6 %multiply_reduce_fusion.1 = (f32[2,1152]{1,0:T(2,128)S(1)}, f32[1152,512]{0,1:T(8,128)}) fusion(f32[1152,512]{0,1:T(8,128)} %copy.147, f32[2,1152]{1,0:T(2,128)S(1)} %fusion.99, bf16[1,1152,512]{1,2,0:T(8,128)(2,1)} %copy.144, s32[2,1152]{1,0:T(2,128)S(1)} %multiply_add_fusion.5, pred[2,1152]{1,0:T(4,128)(4,1)S(1)} %get-tuple-element.59), kind=kOutput, calls=%fused_computation.33 | convolution fusion | flops 2727343872 | bytes 5928192 | tf_op jit(solution)/shard_map/jtk,kd->jtd/dot_general | solution.py:124
  436.1 3.2 copy.146
  441.2 6.0 reshape.332
  447.2 5.0 fusion.60
  452.3 3.5 multiply_reduce_fusion.4
  459.1 5.0 fusion.121
  465.6 2.8 fusion.123
  470.6 5.0 convolution_bitcast_fusion.2
  475.6 6.4 convolution_bitcast_fusion.1
  482.1 2.8 convolution_convert_fusion.5
  484.9 3.0 convolution_convert_fusion.4
  487.9 51.1 %all-reduce.14.cloned.1.call-done = f32[1152,512]{1,0:T(8,128)} async-done(((f32[1152,512]{1,0:T(8,128)}), f32[1152,512]{1,0:T(8,128)}) %all-reduce.14.cloned.1.call-update) | async-done | bytes 2359312 | tf_op jit(solution)/shard_map/psum | solution.py:183
  539.1 3.9 multiply_reduce_fusion.5
  549.0 3.6 copy.151
  552.6 4.8 fusion.52
  557.4 3.8 multiply_reduce_fusion
  565.8 2.4 copy.172
  568.3 2.9 reshape.322
  571.2 3.5 copy.170
  574.6 2.9 reshape.320
  577.5 2.4 copy.171
  579.9 3.0 reshape.321
  592.7 3.2 convolution_convert_fusion.9
  598.4 33.4 %all-reduce.16.cloned.1.call-done = bf16[1152,512]{1,0:T(8,128)(2,1)} async-done(((bf16[1152,512]{1,0:T(8,128)(2,1)}), bf16[1152,512]{1,0:T(8,128)(2,1)}) %all-reduce.16.cloned.1.call-update) | async-done | bytes 1179664 | tf_op jit(solution)/shard_map/psum | solution.py:227
  635.5 62.1 %all-reduce = (bf16[512]{0:T(512)(128)(2,1)S(1)}, bf16[512]{0:T(512)(128)(2,1)S(1)}, bf16[2,256]{1,0:T(2,128)(2,1)S(1)}, bf16[512]{0:T(512)(128)(2,1)S(1)}, bf16...) all-reduce(bf16[512]{0:T(512)(128)(2,1)S(1)} %get-tuple-element.27,, ...), channel_id=1, replica_groups=mesh['wide'=16,'tensor'=2] {'wide'}, use_global_device_ids=true, to_apply=%region_30.0 | all-reduce | flops 13824 | bytes 55296 | tf_op jit(solution)/shard_map/psum | solution.py:231
  704.0 3.5 add_add_fusion.3
  707.4 33.8 %all-reduce.18.cloned.1.call-done = (bf16[512,3,256]{2,0,1:T(8,128)(2,1)}, bf16[256,512]{1,0:T(8,128)(2,1)}, bf16[512,1024]{1,0:T(8,128)(2,1)}, bf16[1024,512]{1,0:T(8,128)(2,1)}) async-done(((bf16[512,3,256]{2,0,1:T(8,128)(2,1)}, bf16[256,512]{1,0:T(8,128)(2,1)}, bf16[512,1024]{1,0:T(8,128)(2,1)}, bf16[1024,512]{1,0:T(8,128)(2,1)}), (bf16[512,3,256]{2,0,1:T(8,128)(2,1)}, bf16[256,512]{1,0:T(8,128)(2,1)}, ...) | async-done | bytes 3145744 | tf_op jit(solution)/shard_map/psum | solution.py:233
  743.1 2.5 convert_element_type.237
  (325 shorter events, 79.0 us)
Async XLA Ops:
  7.2 242.0 %copy-start = (bf16[1,1024,512]{2,1,0:T(8,128)(2,1)S(1)}, bf16[1,1024,512]{2,1,0:T(8,128)(2,1)}, u32[]{:S(2)}) copy-start(bf16[1,1024,512]{2,1,0:T(8,128)(2,1)} %param.41) | copy-start | bytes 3145732
  7.2 5.5 copy-start.6
  7.2 5.5 copy-start.75
  7.2 5.5 copy-start.97
  7.2 5.5 copy-start.103
  7.3 111.4 %all-reduce.10.cloned.1.call-start = ((), (), s32[]{:S(2)}) async-start(), calls=%async_computation.4 | async-start | bytes 4718592 | tf_op jit(solution)/shard_map/psum | solution.py:92
  29.1 9.2 %copy-start.14 = (bf16[8,144,1,4,64]{1,4,3,0,2:T(8,128)(2,1)}, bf16[8,144,1,4,64]{1,4,3,0,2:T(8,128)(2,1)S(1)}, u32[]{:S(2)}) copy-start(bf16[8,144,1,4,64]{1,4,3,0,2:T(8,128)(2,1)S(1)} %copy.183) | copy-start | bytes 1769476
  41.5 3.7 copy-start.36
  45.2 73.4 %copy-start.88 = (f32[512]{0:T(512)S(1)}, f32[512]{0:T(512)}, u32[]{:S(2)}) copy-start(f32[512]{0:T(512)} %param.29) | copy-start | bytes 6148
  47.2 151.2 %all-reduce.12.cloned.1.call-start = ((), (), s32[]{:S(2)}) async-start(), calls=%async_computation.5 | async-start | bytes 4718592 | tf_op jit(solution)/shard_map/psum | solution.py:99
  122.8 3.8 copy-start.93
  134.1 84.0 %copy-start.56 = (f32[2,1152]{1,0:T(2,128)}, f32[2,1152]{1,0:T(2,128)S(1)}, u32[]{:S(2)}) copy-start(f32[2,1152]{1,0:T(2,128)S(1)} %get-tuple-element.58) | copy-start | bytes 27652
  134.1 64.3 %copy-start.89 = (f32[512]{0:T(512)S(1)}, f32[512]{0:T(512)}, u32[]{:S(2)}) copy-start(f32[512]{0:T(512)} %param.35) | copy-start | bytes 6148
  198.4 3.9 copy-start.22
  201.3 13.0 %copy-start.40 = (f32[1152]{0:T(1024)}, f32[1152]{0:T(1024)S(1)}, u32[]{:S(2)}) copy-start(f32[1152]{0:T(1024)S(1)} %broadcast_multiply_fusion) | copy-start | bytes 13828
  202.4 12.0 %copy-start.45 = (f32[1152]{0:T(1024)}, f32[1152]{0:T(1024)S(1)}, u32[]{:S(2)}) copy-start(f32[1152]{0:T(1024)S(1)} %fusion.105) | copy-start | bytes 13828
  205.2 31.3 %all-to-all-start = ((bf16[16,72,512]{2,1,0:T(8,128)(2,1)}), bf16[16,72,512]{2,1,0:T(8,128)(2,1)}, u32[]{:S(2)}, u32[]{:S(2)}) async-start(bf16[16,72,512]{2,1,0:T(8,128)(2,1)} %bitcast.132), calls=%async_computation | async-start | bytes 2359296 | tf_op jit(solution)/shard_map/all_to_all | solution.py:108
  214.4 3.8 copy-start.30
  222.2 21.9 %copy-start.100 = (f32[1,1024]{1,0:T(1,128)S(1)}, f32[1,1024]{1,0:T(1,128)}, u32[]{:S(2)}) copy-start(f32[1,1024]{1,0:T(1,128)} %param.40) | copy-start | bytes 12292
  236.5 32.7 %all-to-all-start.2 = ((bf16[16,72,512]{2,1,0:T(8,128)(2,1)}), bf16[16,72,512]{2,1,0:T(8,128)(2,1)}, u32[]{:S(2)}, u32[]{:S(2)}) async-start(bf16[16,72,512]{2,1,0:T(8,128)(2,1)} %bitcast.133), calls=%async_computation.2 | async-start | bytes 2359296 | tf_op jit(solution)/shard_map/all_to_all | solution.py:136
  244.0 107.1 %all-reduce.20.cloned.1.call-start = ((), (), s32[]{:S(2)}) async-start(), calls=%async_computation.9 | async-start | bytes 4718592 | tf_op jit(solution)/shard_map/psum | solution.py:118
  269.2 8.6 %copy-start.92 = (bf16[1,512,1024]{2,1,0:T(8,128)(2,1)S(1)}, bf16[1,512,1024]{2,1,0:T(8,128)(2,1)}, u32[]{:S(2)}) copy-start(bf16[1,512,1024]{2,1,0:T(8,128)(2,1)} %param.39) | copy-start | bytes 3145732
  280.2 70.9 %copy-start.91 = (f32[1,512]{1,0:T(1,128)S(1)}, f32[1,512]{1,0:T(1,128)}, u32[]{:S(2)}) copy-start(f32[1,512]{1,0:T(1,128)} %param.42) | copy-start | bytes 6148
  377.6 30.9 %all-to-all-start.1 = ((bf16[16,2,18432]{2,1,0:T(2,128)(2,1)}), bf16[16,2,18432]{2,1,0:T(2,128)(2,1)}, u32[]{:S(2)}, u32[]{:S(2)}) async-start(bf16[16,2,18432]{2,1,0:T(2,128)(2,1)} %reshape.329), calls=%async_computation.1 | async-start | bytes 2359296 | tf_op jit(solution)/shard_map/all_to_all | solution.py:121
  408.5 32.7 %all-to-all-start.3 = ((bf16[16,2,18432]{2,1,0:T(2,128)(2,1)}), bf16[16,2,18432]{2,1,0:T(2,128)(2,1)}, u32[]{:S(2)}, u32[]{:S(2)}) async-start(bf16[16,2,18432]{2,1,0:T(2,128)(2,1)} %reshape.331), calls=%async_computation.3 | async-start | bytes 2359296 | tf_op jit(solution)/shard_map/all_to_all | solution.py:153
  416.0 123.1 %all-reduce.14.cloned.1.call-start = ((), (), s32[]{:S(2)}) async-start(), calls=%async_computation.6 | async-start | bytes 4718592 | tf_op jit(solution)/shard_map/psum | solution.py:183
  439.3 12.9 %copy-start.58 = (f32[1152]{0:T(1024)}, f32[1152]{0:T(1024)S(1)}, u32[]{:S(2)}) copy-start(f32[1152]{0:T(1024)S(1)} %multiply_reduce_fusion.10) | copy-start | bytes 13828
  447.2 5.1 copy-start.41
  447.2 5.1 copy-start.46
  447.2 5.1 copy-start.51
  447.2 5.1 copy-start.73
  452.3 3.6 copy-start.17
  452.3 6.5 slice-start.2
  458.8 5.3 copy-start.10
  459.1 6.5 copy-start.96
  468.4 163.3 %all-reduce.16.cloned.1.call-start = ((), (), s32[]{:S(2)}) async-start(), calls=%async_computation.7 | async-start | bytes 2359296 | tf_op jit(solution)/shard_map/psum | solution.py:227
  470.6 14.3 %slice-start.4 = ((s8[4718592]{0:T(1024)(128)(4,1)}), s8[4194304]{0:T(1024)(128)(4,1)S(1)}, s32[]{:S(2)}) async-start(s8[4718592]{0:T(1024)(128)(4,1)} %bitcast.142), calls=%async_computation.14 | async-start | bytes 8388608
  475.6 6.5 copy-start.4
  475.6 6.5 copy-start.55
  475.6 6.5 copy-start.71
  475.6 6.5 copy-start.80
  475.6 6.5 copy-start.102
  475.6 6.5 copy-start.107
  475.6 9.3 %slice-start.5 = ((s8[4718592]{0:T(1024)(128)(4,1)}), s8[524288]{0:T(1024)(128)(4,1)S(1)}, s32[]{:S(2)}) async-start(s8[4718592]{0:T(1024)(128)(4,1)} %bitcast.142), calls=%async_computation.15 | async-start | bytes 1048576
  487.9 55.1 %copy-start.63 = (f32[1152]{0:T(1024)S(1)}, f32[1152]{0:T(1024)}, u32[]{:S(2)}) copy-start(f32[1152]{0:T(1024)} %copy-done.62) | copy-start | bytes 13828
  539.1 4.0 copy-start.5
  539.1 4.0 copy-start.18
  552.6 4.8 copy-start.20
  552.6 4.8 copy-start.21
  552.6 4.8 copy-start.39
  552.6 8.6 %slice-start = ((s8[4718592]{0:T(1024)(128)(4,1)}), s8[4194304]{0:T(1024)(128)(4,1)S(1)}, s32[]{:S(2)}) async-start(s8[4718592]{0:T(1024)(128)(4,1)} %bitcast.126), calls=%async_computation.10 | async-start | bytes 8388608
  557.4 3.8 slice-start.1
  571.2 6.4 copy-start.25
  579.9 5.2 copy-start.29
  588.7 4.0 copy-start.24
  588.7 152.6 %all-reduce.18.cloned.1.call-start = ((), (), s32[]{:S(2)}) async-start(), calls=%async_computation.8 | async-start | bytes 6291456 | tf_op jit(solution)/shard_map/psum | solution.py:233
  590.7 5.1 copy-start.7
  590.7 5.1 copy-start.44
  590.7 5.1 copy-start.69
  590.7 5.1 copy-start.76
  590.8 5.1 copy-start.104
  598.3 35.7 %copy-start.61 = (f32[1152]{0:T(1024)S(1)}, f32[1152]{0:T(1024)}, u32[]{:S(2)}) copy-start(f32[1152]{0:T(1024)} %copy-done.60) | copy-start | bytes 13828
  741.2 4.4 copy-start.35
  743.1 4.1 copy-start.34
  (61 other events, 127.8 us)
Sparse Core Ops, SparseCore 0:
  47.3 71.3 all-reduce.9
  129.8 68.6 all-reduce.11
  280.4 70.6 all-reduce.19
  468.5 70.4 all-reduce.13
  588.8 42.8 all-reduce.15
  637.1 104.0 all-reduce.17
where the time goes:
time: 765 us; the launch traced here: 756 us
  waiting for transfers between devices  358 us (47%)
  local copies, waits for them, and re-layouts  118 us (15%)
  matrix products  99.8 us (13%)
  other arithmetic  75.2 us (10%)
  blocking collectives  62.1 us (8%)
  starting transfers between devices  27.5 us (4%)
  between operations  15.9 us (2%)
    psum x1, waiting for transfers between devices, shards(): lax.psum(jnp.dot(context, proj_weight, preferred_element_type=jnp.float32...  71.1 us
    psum x1, waiting for transfers between devices, shards(): lax.psum(expert_partial.astype(jnp.bfloat16), 'tensor').astype(jnp.float32)  70.8 us
    psum x1, blocking collectives, shards(): lax.psum(pre_gain_grad.astype(jnp.bfloat16), 'wide').astype(jnp.float32)  62.1 us
    psum x1, waiting for transfers between devices, shards(): second = first + lax.psum(partial_out, 'tensor') + output_bias  59.8 us
    unnamed x241, local copies, waits for them, and re-layouts  52.7 us
    psum x1, waiting for transfers between devices, shards(): mid_grad = lax.psum(mid_partial, 'tensor')  51.1 us
    psum x1, waiting for transfers between devices, shards(): lax.psum(qkv_weight_grad.astype(jnp.bfloat16), 'wide').astype(jnp.float32)  33.8 us
    psum x1, waiting for transfers between devices, shards(): lax.psum(pre_partial.astype(jnp.bfloat16), 'tensor').astype(jnp.float32)  33.4 us
  transfers between devices with their start and end apart: 10, of which 10 were waited for; matrix products, arithmetic and copies ran while one was open for 15% of the time, Pallas kernels for 0%

commit v1 on v0

--- a/solution.py
+++ b/solution.py
@@ -1,10 +1,918 @@
+import functools
+
 import jax
 import jax.numpy as jnp
 from jax import lax
+from jax.experimental import pallas as pl
+from jax.experimental.pallas import tpu as pltpu
 from jax.sharding import PartitionSpec as P
 
 HEAD_DIM = 64
 PATCHES = 144
+BF16 = jnp.bfloat16
+F32 = jnp.float32
+HIGHEST = lax.Precision.HIGHEST
+MESH = pl.DeviceIdType.MESH
+VMEM_BYTES = 60 * 1024 * 1024
+
+
+def dot(left, right):
+    return jnp.dot(left, right, preferred_element_type=F32)
+
+
+def dot_rows(left, right):
+    return lax.dot_general(left, right, (((1,), (1,)), ((), ())), preferred_element_type=F32)
+
+
+def dot_columns(left, right, precision=None):
+    return lax.dot_general(
+        left, right, (((0,), (0,)), ((), ())), precision=precision, preferred_element_type=F32
+    )
+
+
+def normalized(values):
+    centered = values - jnp.mean(values, axis=-1, keepdims=True)
+    variance = jnp.mean(centered * centered, axis=-1, keepdims=True)
+    scale = lax.rsqrt(variance + 1e-06)
+    return centered * scale, scale
+
+
+def norm_back(rows, scale, gain, upstream):
+    scaled = upstream * gain
+    inward = jnp.mean(scaled, axis=-1, keepdims=True)
+    along = jnp.mean(scaled * rows, axis=-1, keepdims=True)
+    return scale * (scaled - inward - rows * along)
+
+
+def gelu_parts(inner):
+    square = inner * inner
+    bend = jnp.tanh(0.7978845608028654 * inner * (1.0 + 0.044715 * square))
+    half = 0.5 * (1.0 + bend)
+    slope = half + (0.5 * 0.7978845608028654) * inner * (1.0 - bend * bend) * (
+        1.0 + 0.134145 * square
+    )
+    return inner * half, slope
+
+
+def gelu(inner):
+    return inner * (0.5 * (1.0 + jnp.tanh(0.7978845608028654 * inner * (1.0 + 0.044715 * inner * inner))))
+
+
+def softmax_rows(scores, scale):
+    peak = jnp.max(scores, axis=-1, keepdims=True)
+    weights = jnp.exp((scores - peak) * scale)
+    return weights * (1.0 / jnp.sum(weights, axis=-1, keepdims=True))
+
+
+def spots(places):
+    lane = lax.broadcasted_iota(jnp.int32, (places.shape[0], 128), 1)
+    return [(lane == places[:, j : j + 1]).astype(F32) for j in range(2)]
+
+
+def bits_of(index, wide):
+    return [lax.rem(lax.div(index, 1 << k), 2) for k in range(wide.bit_length() - 1)]
+
+
+class Sums:
+    def __init__(self, wide, orders, totals, sends, lands, gathers, send_sems, recv_sems):
+        me, self.plane = lax.axis_index("wide"), lax.axis_index("tensor")
+        self.bits = bits_of(me, wide)
+        self.partners = [me + (1 - 2 * bit) * (1 << k) for k, bit in enumerate(self.bits)]
+        self.steps = len(self.bits)
+        self.orders, self.totals, self.sends, self.lands, self.gathers = orders, totals, sends, lands, gathers
+        self.send_sems, self.recv_sems = send_sems, recv_sems
+
+    def piece(self, i, step):
+        rows = self.gathers[i].shape[0]
+        base = 0
+        for s in range(step):
+            base = base + self.bits[self.orders[i][s]] * (rows >> (s + 1))
+        length = rows >> (step + 1)
+        bit = self.bits[self.orders[i][step]]
+        return pl.multiple_of(base + bit * length, 16), pl.multiple_of(base + (1 - bit) * length, 16), length
+
+    def staged(self, i, step):
+        rows = self.gathers[i].shape[0]
+        return rows - (rows >> step)
+
+    def transfer(self, i, k):
+        step = k if k < self.steps else 2 * self.steps - 1 - k
+        kept, _, length = self.piece(i, step)
+        if k < self.steps:
+            at = self.staged(i, step)
+            source, target = self.sends[i].at[pl.ds(at, length)], self.lands[i].at[pl.ds(at, length)]
+        else:
+            source = target = self.gathers[i].at[pl.ds(kept, length)]
+        return pltpu.make_async_remote_copy(
+            source, target, self.send_sems.at[i, k], self.recv_sems.at[i, k],
+            device_id=(self.partners[self.orders[i][step]], self.plane), device_id_type=MESH,
+        )
+
+    def begin(self, i, k):
+        if k < self.steps:
+            _, other, length = self.piece(i, k)
+            at = self.staged(i, k)
+            self.sends[i][at : at + length, :] = self.totals[i][pl.ds(other, length), :].astype(BF16)
+        self.transfer(i, k).start()
+
+    def advance(self, i, k):
+        self.transfer(i, k).wait()
+        if k < self.steps:
+            kept, _, length = self.piece(i, k)
+            at = self.staged(i, k)
+            value = self.totals[i][pl.ds(kept, length), :] + self.lands[i][at : at + length, :].astype(F32)
+            if k + 1 < self.steps:
+                self.totals[i][pl.ds(kept, length), :] = value
+            else:
+                self.gathers[i][pl.ds(kept, length), :] = value.astype(BF16)
+        if k + 1 < 2 * self.steps:
+            self.begin(i, k + 1)
+
+
+def greet(wide):
+    me, plane = lax.axis_index("wide"), lax.axis_index("tensor")
+    barrier = pltpu.get_barrier_semaphore()
+
+    def hail(d, carry):
+        pl.semaphore_signal(barrier, inc=1, device_id=(lax.rem(me + d, wide), plane), device_id_type=MESH)
+        return carry
+
+    lax.fori_loop(1, wide, hail, 0)
+    pl.semaphore_signal(barrier, inc=1, device_id=(me, 1 - plane), device_id_type=MESH)
+    pl.semaphore_wait(barrier, wide)
+
+
+def put_row(small, at, row):
+    for c in range(row.shape[1] // 128):
+        small[at + c : at + c + 1, :] = row[:, 128 * c : 128 * (c + 1)]
+    return at + row.shape[1] // 128
+
+
+def get_row(small, at, width):
+    return jnp.concatenate([small[at + c : at + c + 1, :] for c in range(width // 128)], axis=1)
+
+
+def image_back(heads, qkv, context_grad):
+    width = heads * HEAD_DIM
+    scale = HEAD_DIM**-0.5
+    parts = [[], [], []]
+    for head in range(heads):
+        h = head * HEAD_DIM
+        query = qkv[:, h : h + HEAD_DIM]
+        keys = qkv[:, width + h : width + h + HEAD_DIM]
+        values = qkv[:, 2 * width + h : 2 * width + h + HEAD_DIM]
+        upstream = context_grad[:, h : h + HEAD_DIM]
+        probs = softmax_rows(dot_rows(query, keys), scale)
+        prob_grad = dot_rows(upstream, values)
+        inward = jnp.sum(probs * prob_grad, axis=-1, keepdims=True)
+        score_grad = (probs * (prob_grad - inward)).astype(BF16)
+        parts[0].append(dot(score_grad, keys) * scale)
+        parts[1].append(dot_columns(score_grad, query) * scale)
+        parts[2].append(dot_columns(probs.astype(BF16), upstream))
+    return jnp.concatenate(parts[0] + parts[1] + parts[2], axis=1).astype(BF16)
+
+
+def column_dots(left, right, put, tile=256):
+    def body(i, carry):
+        at = pl.multiple_of(i * tile, tile)
+        put(at, tile, dot_columns(left[:, pl.ds(at, tile)], right[...]))
+        return carry
+
+    lax.fori_loop(0, left.shape[1] // tile, body, 0)
+
+
+def image_forward(heads, qkv):
+    width = heads * HEAD_DIM
+    parts = []
+    for head in range(heads):
+        h = head * HEAD_DIM
+        probs = softmax_rows(
+            dot_rows(qkv[:, h : h + HEAD_DIM], qkv[:, width + h : width + h + HEAD_DIM]), HEAD_DIM**-0.5
+        )
+        parts.append(dot(probs.astype(BF16), qkv[:, 2 * width + h : 2 * width + h + HEAD_DIM]))
+    return jnp.concatenate(parts, axis=1).astype(BF16)
+
+
+def token_hits(choices, slots):
+    slot = lax.broadcasted_iota(jnp.int32, (choices.shape[0], slots), 1)
+    return [slot == choices[:, j : j + 1] for j in range(2)]
+
+
+def slot_hits(first, count, targets):
+    slot = first + lax.broadcasted_iota(jnp.int32, (count, targets.shape[1]), 0)
+    return ((slot == targets[0:1, :]) | (slot == targets[1:2, :])).astype(BF16)
+
+
+def slot_targets(choice_ids, ranks, capacity, room):
+    count = choice_ids.shape[1]
+    order_keys = jnp.concatenate([ranks, ranks + count])
+    flat_ids = choice_ids.reshape(2 * count)
+    earlier = (order_keys[None, :] < order_keys[:, None]) & (flat_ids[None, :] == flat_ids[:, None])
+    position = jnp.sum(earlier.astype(jnp.int32), axis=1).reshape(2, count)
+    kept = position < capacity
+    targets = jnp.where(kept, choice_ids * room + position, -1)
+    marks = jnp.where(kept, choice_ids, -1)
+    places = jnp.where(kept, position, -1)
+    return targets, jnp.concatenate([targets, marks, places]).T
+
+
+def forward(
+    wide, room, group, heads, rows,
+    tokens, cotangent, targets, choices, pre_gain, pre_shift, weight_qkv, qv_bias, projection, proj_bias,
+    mid_gain, mid_shift, hidden, hidden_bias, output, output_bias, moe_gain, moe_shift, router,
+    qkv_out, context_out, first_out, second_out, lowered_out, route_out, gates_out, table_out, upstream_out,
+    placed, projection_peer, context_peer, partial_own, partial_peer, sems,
+):
+    me, plane = lax.axis_index("wide"), lax.axis_index("tensor")
+    chunks, groups = tokens.shape[0] // rows, wide // group
+    mine = lax.div(me, group)
+    block = group * room
+    width = heads * HEAD_DIM
+    row_at, context_at, partial_at, last_at = 0, wide, wide + chunks, wide + 2 * chunks
+    greet(wide)
+
+    def rows_of(index):
+        return pl.ds(pl.multiple_of(index * room, 16), room)
+
+    def chunk_of(index):
+        return pl.ds(pl.multiple_of(index * rows, 16), rows)
+
+    def move(source, target, base, sent, landed, device):
+        return pltpu.make_async_remote_copy(
+            source, target, sems.at[0, base + sent], sems.at[1, base + landed], device_id=device, device_id_type=MESH
+        )
+
+    def across(source, target, base, index):
+        there = chunk_of(index)
+        return move(source.at[there], target.at[there], base, index, index, (me, 1 - plane))
+
+    def row_copy(other, sender):
+        return move(placed.at[rows_of(other)], upstream_out.at[rows_of(sender)], row_at, other, sender, (other, plane))
+
+    weights = move(projection, projection_peer, last_at, 0, 0, (me, 1 - plane))
+    weights.start()
+    table_out[...] = jnp.zeros_like(table_out)
+
+    def attend_chunk(c):
+        there = chunk_of(c)
+        normed, _ = normalized(tokens[there, :].astype(F32))
+        lowered = (normed * pre_gain[...] + pre_shift[...]).astype(BF16)
+        parts = [dot(lowered, weight_qkv[s]) for s in range(3)]
+        parts = [parts[0] + qv_bias[0:1, :], parts[1], parts[2] + qv_bias[1:2, :]]
+        qkv = jnp.concatenate(parts, axis=1).astype(BF16)
+        qkv_out[there, :] = qkv
+        contexts = [
+            image_forward(heads, qkv[image * PATCHES : (image + 1) * PATCHES]) for image in range(rows // PATCHES)
+        ]
+        context_out[there, :] = jnp.concatenate(contexts, axis=0)
+        across(context_out, context_peer, context_at, c).start()
+
+    def place_group(k):
+        q = lax.rem(mine + k, groups)
+        hits = slot_hits(q * block, block, targets)
+        here = pl.ds(pl.multiple_of(q * block, 16), block)
+        placed[here, :] = dot(hits, cotangent[...].astype(BF16)).astype(BF16)
+        for j in range(group):
+            e = q * group + j
+
+            @pl.when(e != me)
+            def _(e=e):
+                row_copy(e, me).start()
+
+            @pl.when(e == me)
+            def _(e=e):
+                upstream_out[rows_of(e), :] = placed[rows_of(e), :]
+
+    def feed_chunk(c):
+        there = chunk_of(c)
+        across(context_out, context_peer, context_at, c).wait()
+        branch = dot(context_out[there, :], projection[...]) + dot(context_peer[there, :], projection_peer[...])
+        first = tokens[there, :].astype(F32) + branch + proj_bias[...]
+        first_out[there, :] = first
+        normed, _ = normalized(first)
+        lowered = (normed * mid_gain[...] + mid_shift[...]).astype(BF16)
+        activated = gelu(dot(lowered, hidden[...]) + hidden_bias[...]).astype(BF16)
+        partial_own[there, :] = dot(activated, output[...]).astype(BF16)
+        across(partial_own, partial_peer, partial_at, c).start()
+
+    def route_chunk(c):
+        there = chunk_of(c)
+        across(partial_own, partial_peer, partial_at, c).wait()
+        partial = partial_own[there, :].astype(F32) + partial_peer[there, :].astype(F32)
+        second = first_out[there, :] + partial + output_bias[...]
+        second_out[there, :] = second
+        normed, _ = normalized(second)
+        normed = normed * moe_gain[...] + moe_shift[...]
+        lowered_out[there, :] = normed.astype(BF16)
+        logits = lax.dot_general(
+            normed, router[...], (((1,), (1,)), ((), ())), precision=HIGHEST, preferred_element_type=F32
+        )
+        grown = jnp.exp(logits - jnp.max(logits, axis=-1, keepdims=True))
+        route = grown / jnp.sum(grown, axis=-1, keepdims=True)
+        route_out[there, :] = route
+        number = lax.broadcasted_iota(jnp.int32, route.shape, 1)
+        picks = choices[there, :]
+        chosen = [jnp.where(number == picks[:, 2 + j : 3 + j], route, 0.0) for j in range(2)]
+        gates_out[there, :] = jnp.concatenate([jnp.sum(part, axis=1, keepdims=True) for part in chosen], axis=1)
+        for part, spot in zip(chosen, spots(picks[:, 4:6])):
+            table_out[...] += dot_columns(part, spot, HIGHEST)
+
+    def turn(c, carry):
+        @pl.when(c < chunks)
+        def _():
+            attend_chunk(c)
+
+        @pl.when(c < groups)
+        def _():
+            place_group(c)
+
+        @pl.when(c == 1)
+        def _():
+            weights.wait()
+
+        @pl.when((c >= 1) & (c <= chunks))
+        def _():
+            feed_chunk(c - 1)
+
+        @pl.when(c >= 2)
+        def _():
+            route_chunk(c - 2)
+
+        return carry
+
+    lax.fori_loop(0, chunks + 2, turn, 0)
+
+    def take_rows(d, carry):
+        other = lax.rem(me + d, wide)
+        row_copy(other, other).wait_recv()
+        row_copy(other, me).wait_send()
+        return carry
+
+    lax.fori_loop(1, wide, take_rows, 0)
+
+
+def experts(
+    wide, room, group,
+    lowered, targets, table, upstream, weight_in, bias_in, weight_out, bias_out,
+    own_home, peer_home, gate_home, result_out, in_grad, out_grad, in_bias_grad, out_bias_grad,
+    placed, arrived, act, inner_grad, slot_grad, grad_kept, grad_sent, grad_landed, result_kept, result_sent,
+    result_landed, grad_back, gate_sent, gate_arrived, gate_back, gate_own, gate_peer, sems,
+):
+    me, plane = lax.axis_index("wide"), lax.axis_index("tensor")
+    groups = wide // group
+    mine = lax.div(me, group)
+    half = own_home.shape[1]
+    block = group * room
+    row_at, gate_at, home_at, back_at = 0, wide, 2 * wide, 3 * wide
+    grad_at, result_at, share_at, table_at = 4 * wide, 4 * wide + groups, 4 * wide + 2 * groups, 4 * wide + 3 * groups
+
+    greet(wide)
+
+    def rows_of(index):
+        return pl.ds(pl.multiple_of(index * room, 16), room)
+
+    def rows_of_group(index):
+        return pl.ds(pl.multiple_of(index * block, 16), block)
+
+    def move(source, target, base, sent, landed, device):
+        return pltpu.make_async_remote_copy(
+            source, target, sems.at[0, base + sent], sems.at[1, base + landed], device_id=device, device_id_type=MESH
+        )
+
+    def row_copy(other, sender):
+        return move(placed.at[rows_of(other)], arrived.at[rows_of(sender)], row_at, other, sender, (other, plane))
+
+    def gate_copy(other, sender):
+        return move(gate_sent.at[other], gate_arrived.at[sender], gate_at, other, sender, (other, plane))
+
+    def home_copy(other, sender):
+        return move(grad_back.at[rows_of(other)], own_home.at[rows_of(sender)], home_at, other, sender, (other, plane))
+
+    def back_copy(other, sender):
+        return move(gate_back.at[other], gate_own.at[sender], back_at, other, sender, (other, plane))
+
+    def across(source, target, base, index):
+        there = rows_of_group(index)
+        return move(source.at[there], target.at[there], base, index, index, (me, 1 - plane))
+
+    for e in range(wide):
+        gate_sent[e] = jnp.broadcast_to(table[e : e + 1, :], gate_sent.shape[1:])
+    in_bias_grad[...] = jnp.zeros_like(in_bias_grad)
+    out_bias_grad[...] = jnp.zeros_like(out_bias_grad)
+
+    def place_group(k, carry):
+        q = lax.rem(mine + k, groups)
+        slot = q * block + lax.broadcasted_iota(jnp.int32, (block, targets.shape[1]), 0)
+        hits = ((slot == targets[0:1, :]) | (slot == targets[1:2, :])).astype(BF16)
+        placed[rows_of_group(q), :] = dot(hits, lowered[...]).astype(BF16)
+        for j in range(group):
+            e = q * group + j
+
+            @pl.when(e != me)
+            def _(e=e):
+                row_copy(e, me).start()
+                gate_copy(e, me).start()
+
+            @pl.when(e == me)
+            def _(e=e):
+                arrived[rows_of(e), :] = placed[rows_of(e), :]
+                gate_arrived[e] = gate_sent[e]
+
+        return carry
+
+    lax.fori_loop(0, groups, place_group, 0)
+    diagonal = lax.broadcasted_iota(jnp.int32, (room, 128), 0) == lax.broadcasted_iota(jnp.int32, (room, 128), 1)
+    first_plane = plane == 0
+
+    def give_back(p):
+        across(grad_sent, grad_landed, grad_at, p).wait()
+        there = rows_of_group(p)
+        grad_back[there, :] = (grad_kept[there, :] + grad_landed[there, :].astype(F32)).astype(BF16)
+        for j in range(group):
+            w = p * group + j
+
+            @pl.when(w != me)
+            def _(w=w):
+                home_copy(w, me).start()
+
+            @pl.when(w == me)
+            def _(w=w):
+                own_home[rows_of(w), :] = grad_back[rows_of(w), :]
+
+    def expert_group(k, carry):
+        p = lax.rem(mine + groups - k, groups)
+        there = rows_of_group(p)
+        columns = []
+        for j in range(group):
+            w = p * group + j
+
+            @pl.when(w != me)
+            def _(w=w):
+                row_copy(w, w).wait_recv()
+                gate_copy(w, w).wait_recv()
+
+            columns.append(jnp.sum(jnp.where(diagonal, gate_arrived[w][0:1, :], 0.0), axis=1, keepdims=True))
+        gates = jnp.concatenate(columns, axis=0)
+        inner = dot(arrived[there, :], weight_in[...]) + bias_in[...]
+        acted, slope = gelu_parts(inner)
+        acted = acted.astype(BF16)
+        act[there, :] = acted
+        result = dot(acted, weight_out[...])
+        raised = upstream[there, :].astype(F32)
+        slot = (raised * gates).astype(BF16)
+        slot_grad[there, :] = slot
+        out_bias_grad[0:1, :] += jnp.sum(slot.astype(F32), axis=0, keepdims=True)
+        inward = (dot_rows(slot, weight_out[...]) * slope).astype(BF16)
+        inner_grad[there, :] = inward
+        in_bias_grad[0:1, :] += jnp.sum(inward.astype(F32), axis=0, keepdims=True)
+        grad = dot_rows(inward, weight_in[...])
+        low, high = grad[:, :half], grad[:, half:]
+        grad_sent[there, :] = jnp.where(first_plane, high, low).astype(BF16)
+        across(grad_sent, grad_landed, grad_at, p).start()
+        grad_kept[there, :] = jnp.where(first_plane, low, high)
+        biased = result + bias_out[...]
+        low, high = biased[:, :half], biased[:, half:]
+        result_kept[there, :] = jnp.where(first_plane, low, high)
+        low, high = result[:, :half], result[:, half:]
+        result_sent[there, :] = jnp.where(first_plane, high, low).astype(BF16)
+        across(result_sent, result_landed, result_at, p).start()
+        slopes = jnp.sum(raised * jnp.where(first_plane, biased, result), axis=1, keepdims=True)
+        for j in range(group):
+            w = p * group + j
+            row = jnp.sum(
+                jnp.where(diagonal, slopes[j * room : (j + 1) * room], 0.0), axis=0, keepdims=True
+            )
+            gate_back[w] = jnp.broadcast_to(row, gate_back.shape[1:])
+
+            @pl.when(w != me)
+            def _(w=w):
+                back_copy(w, me).start()
+
+            @pl.when(w == me)
+            def _(w=w):
+                gate_own[w] = gate_back[w]
+
+        @pl.when(k > 0)
+        def _():
+            give_back(lax.rem(mine + groups - k + 1, groups))
+
+        return carry
+
+    lax.fori_loop(0, groups, expert_group, 0)
+    give_back(lax.rem(mine + 1, groups))
+
+    tile = act.shape[1] // groups
+
+    def share_group(k, carry):
+        at = pl.multiple_of(k * tile, 128)
+        out_grad[pl.ds(at, tile), :] = dot_columns(act[:, pl.ds(at, tile)], slot_grad[...]).astype(BF16)
+        q = lax.rem(mine + k, groups)
+        for j in range(group):
+            e = q * group + j
+
+            @pl.when(e != me)
+            def _(e=e):
+                home_copy(e, e).wait_recv()
+
+        across(own_home, peer_home, share_at, q).start()
+        return carry
+
+    lax.fori_loop(0, groups, share_group, 0)
+
+    def take_gates(d, carry):
+        back_copy(lax.rem(me + d, wide), lax.rem(me + d, wide)).wait_recv()
+        return carry
+
+    lax.fori_loop(1, wide, take_gates, 0)
+    tables = move(gate_own, gate_peer, table_at, 0, 0, (me, 1 - plane))
+    tables.start()
+
+    def put(at, tile, value):
+        in_grad[pl.ds(at, tile), :] = value.astype(BF16)
+
+    column_dots(arrived, inner_grad, put)
+
+    def take_result(p, carry):
+        across(result_sent, result_landed, result_at, p).wait()
+        there = rows_of_group(p)
+        result_out[there, :] = (result_kept[there, :] + result_landed[there, :].astype(F32)).astype(BF16)
+        return carry
+
+    lax.fori_loop(0, groups, take_result, 0)
+
+    def end_sends(d, carry):
+        other = lax.rem(me + d, wide)
+        row_copy(other, me).wait_send()
+        gate_copy(other, me).wait_send()
+        home_copy(other, me).wait_send()
+        back_copy(other, me).wait_send()
+        return carry
+
+    lax.fori_loop(1, wide, end_sends, 0)
+    tables.wait()
+    for e in range(wide):
+        gate_home[e : e + 1, :] = gate_own[e][0:1, :] + gate_peer[e][0:1, :]
+
+    def end_share(q, carry):
+        across(own_home, peer_home, share_at, q).wait()
+        return carry
+
+    lax.fori_loop(0, groups, end_share, 0)
+
+
+def backward(
+    wide, room, heads, layout, orders, rows,
+    second, cotangent, route, choices, gates, moe_gain, moe_shift, router, gate_grads, row_own, row_peer, result,
+    first, tokens, qkv, context, mid_gain, mid_shift, pre_gain, pre_shift, hidden, hidden_bias, output, projection,
+    weight_qkv,
+    block_out, grad_out, hidden_out, output_out, qkv_out, proj_out, *rest,
+):
+    vectors_out, rest = rest[: len(layout)], rest[len(layout) :]
+    (lowered_mid, act, inner_grad, mid_own, mid_peer, branch, qkv_grad, lowered_pre, pre_peer, result_own, result_peer,
+     moe_sums, router_sums, mid_sums, hidden_sums, qkv_sums, pre_sums, small_sums) = rest[:18]
+    hidden_total, output_total, qkv_total, proj_total, small = rest[18:23]
+    sends, lands = rest[23:29], rest[29:35]
+    mid_sems, pre_sems, result_sems, send_sems, recv_sems = rest[35:]
+    me, plane = lax.axis_index("wide"), lax.axis_index("tensor")
+    chunks = tokens.shape[0] // rows
+    model = tokens.shape[1]
+    width = heads * HEAD_DIM
+    split = qkv_total.shape[0] // 2
+    totals = (
+        hidden_total, output_total, qkv_total.at[pl.ds(0, split)], qkv_total.at[pl.ds(split, split)], proj_total, small
+    )
+    gathers = (
+        hidden_out, output_out, qkv_out.at[pl.ds(0, split)], qkv_out.at[pl.ds(split, split)], proj_out, small_sums
+    )
+    greet(wide)
+    sums = Sums(wide, orders, totals, sends, lands, gathers, send_sems, recv_sems)
+
+    def rows_of(index):
+        return pl.ds(pl.multiple_of(index * room, 16), room)
+
+    def result_copy(other, sender):
+        return pltpu.make_async_remote_copy(
+            result.at[rows_of(other)], result_own.at[rows_of(sender)], result_sems.at[0, other],
+            result_sems.at[1, sender], device_id=(other, plane), device_id_type=MESH,
+        )
+
+    def send_result(d, carry):
+        result_copy(lax.rem(me + d, wide), me).start()
+        return carry
+
+    lax.fori_loop(1, wide, send_result, 0)
+    result_own[rows_of(me), :] = result[rows_of(me), :]
+
+    def across(own, peer, sems, chunk):
+        at = pl.multiple_of(chunk * rows, rows)
+        return pltpu.make_async_remote_copy(
+            own.at[pl.ds(at, rows)], peer.at[pl.ds(at, rows)], sems.at[0, chunk], sems.at[1, chunk],
+            device_id=(me, 1 - plane), device_id_type=MESH,
+        )
+
+    for vector in (moe_sums, router_sums, mid_sums, hidden_sums, qkv_sums, pre_sums):
+        vector[...] = jnp.zeros_like(vector)
+    first_plane = plane == 0
+
+    def ordered(own, peer):
+        return jnp.concatenate([jnp.where(first_plane, own, peer), jnp.where(first_plane, peer, own)], axis=1)
+
+    def settle(here):
+        picks = choices[here, :]
+        hits = token_hits(picks, row_own.shape[0])
+        table = (hits[0] | hits[1]).astype(BF16)
+        moe_grad = ordered(dot(table, row_own[...]), dot(table, row_peer[...]))
+        chances = route[here, :]
+        number = lax.broadcasted_iota(jnp.int32, chances.shape, 1)
+        route_grad = jnp.zeros_like(chances)
+        for j, spot in enumerate(spots(picks[:, 4:6])):
+            at_place = lax.dot_general(
+                spot, gate_grads[...], (((1,), (1,)), ((), ())), precision=HIGHEST, preferred_element_type=F32
+            )
+            route_grad = route_grad + jnp.where(number == picks[:, 2 + j : 3 + j], at_place, 0.0)
+        logit_grad = chances * (route_grad - jnp.sum(chances * route_grad, axis=1, keepdims=True))
+        normed, scale = normalized(second[here, :])
+        router_sums[...] += dot_columns(logit_grad, normed * moe_gain[...] + moe_shift[...], HIGHEST)
+        moe_grad = moe_grad + jnp.dot(logit_grad, router[...], precision=HIGHEST, preferred_element_type=F32)
+        grad = cotangent[here, :] + norm_back(normed, scale, moe_gain[...], moe_grad)
+        grad_out[here, :] = grad
+        branch[here, :] = grad.astype(BF16)
+        moe_sums[0:1, :] += jnp.sum(moe_grad * normed, axis=0, keepdims=True)
+        moe_sums[1:2, :] += jnp.sum(moe_grad, axis=0, keepdims=True)
+        moe_sums[2:3, :] += jnp.sum(grad, axis=0, keepdims=True)
+
+    def feed_chunk(chunk, carry):
+        here = pl.ds(pl.multiple_of(chunk * rows, rows), rows)
+        settle(here)
+        normed, _ = normalized(first[here, :])
+        lowered = (normed * mid_gain[...] + mid_shift[...]).astype(BF16)
+        lowered_mid[here, :] = lowered
+        acted, slope = gelu_parts(dot(lowered, hidden[...]) + hidden_bias[...])
+        act[here, :] = acted.astype(BF16)
+        inward = (dot_rows(branch[here, :], output[...]) * slope).astype(BF16)
+        inner_grad[here, :] = inward
+        hidden_sums[0:1, :] += jnp.sum(inward.astype(F32), axis=0, keepdims=True)
+        mid_own[here, :] = dot_rows(inward, hidden[...]).astype(BF16)
+        across(mid_own, mid_peer, mid_sems, chunk).start()
+        return carry
+
+    lax.fori_loop(0, chunks, feed_chunk, 0)
+
+    def put_in(total):
+        def put(at, tile, value):
+            total[pl.ds(at, tile), :] = value
+
+        return put
+
+    column_dots(lowered_mid, inner_grad, put_in(hidden_total))
+    sums.begin(0, 0)
+    column_dots(act, branch, put_in(output_total))
+    sums.begin(1, 0)
+
+    def attend_chunk(chunk, carry):
+        here = pl.ds(pl.multiple_of(chunk * rows, rows), rows)
+        across(mid_own, mid_peer, mid_sems, chunk).wait()
+        mid_grad = mid_own[here, :].astype(F32) + mid_peer[here, :].astype(F32)
+        normed, scale = normalized(first[here, :])
+        first_grad = grad_out[here, :] + norm_back(normed, scale, mid_gain[...], mid_grad)
+        grad_out[here, :] = first_grad
+        lowered_grad = first_grad.astype(BF16)
+        branch[here, :] = lowered_grad
+        mid_sums[0:1, :] += jnp.sum(mid_grad * normed, axis=0, keepdims=True)
+        mid_sums[1:2, :] += jnp.sum(mid_grad, axis=0, keepdims=True)
+        mid_sums[2:3, :] += jnp.sum(first_grad, axis=0, keepdims=True)
+        normed, _ = normalized(tokens[here, :].astype(F32))
+        lowered_pre[here, :] = (normed * pre_gain[...] + pre_shift[...]).astype(BF16)
+        context_grad = dot_rows(lowered_grad, projection[...]).astype(BF16)
+        for image in range(rows // PATCHES):
+            at = pl.multiple_of(chunk * rows + image * PATCHES, PATCHES)
+            block = qkv[pl.ds(at, PATCHES), :]
+            grad = image_back(heads, block, context_grad[image * PATCHES : (image + 1) * PATCHES])
+            qkv_grad[pl.ds(at, PATCHES), :] = grad
+            pre = sum(dot_rows(grad[:, s * width : (s + 1) * width], weight_qkv[s]) for s in range(3))
+            mid_own[pl.ds(at, PATCHES), :] = pre.astype(BF16)
+            qkv_sums[0:1, :] += jnp.sum(grad.astype(F32), axis=0, keepdims=True)
+            for k in range(sums.steps):
+
+                @pl.when(chunk == k)
+                def _(i=image, k=k):
+                    if i < 2:
+                        sums.advance(i, k)
+
+        across(mid_own, pre_peer, pre_sems, chunk).start()
+        return carry
+
+    lax.fori_loop(0, chunks, attend_chunk, 0)
+
+    def take_result(d, carry):
+        other = lax.rem(me + d, wide)
+        result_copy(other, other).wait_recv()
+        result_copy(other, me).wait_send()
+        return carry
+
+    lax.fori_loop(1, wide, take_result, 0)
+    share = pltpu.make_async_remote_copy(
+        result_own, result_peer, result_sems.at[0, wide], result_sems.at[1, wide],
+        device_id=(me, 1 - plane), device_id_type=MESH,
+    )
+    share.start()
+    column_dots(context, branch, put_in(proj_total))
+    sums.begin(4, 0)
+
+    def put_thirds(at, tile, value):
+        for s in range(3):
+            there = pl.ds(pl.multiple_of(s * model + at, 16), tile)
+            qkv_total[there, :] = value[:, s * width : (s + 1) * width]
+
+    column_dots(lowered_pre, qkv_grad, put_thirds)
+    sums.begin(2, 0)
+    sums.begin(3, 0)
+
+    def finish_chunk(chunk, carry):
+        here = pl.ds(pl.multiple_of(chunk * rows, rows), rows)
+        across(mid_own, pre_peer, pre_sems, chunk).wait()
+        upstream = mid_own[here, :].astype(F32) + pre_peer[here, :].astype(F32)
+        normed, scale = normalized(tokens[here, :].astype(F32))
+        grad_out[here, :] += norm_back(normed, scale, pre_gain[...], upstream)
+        pre_sums[0:1, :] += jnp.sum(upstream * normed, axis=0, keepdims=True)
+        pre_sums[1:2, :] += jnp.sum(upstream, axis=0, keepdims=True)
+        return carry
+
+    lax.fori_loop(0, chunks, finish_chunk, 0)
+    small[...] = jnp.zeros_like(small)
+    at = 0
+    for vector, picked in zip((pre_sums, mid_sums, moe_sums, hidden_sums, qkv_sums, router_sums), layout):
+        for r in picked:
+            at = put_row(small, at, vector[r : r + 1, :])
+    sums.begin(5, 0)
+
+    def blend(chunk, carry):
+        here = pl.ds(pl.multiple_of(chunk * rows, rows), rows)
+        mixture = second[here, :]
+        for j, hit in enumerate(token_hits(choices[here, :], result_own.shape[0])):
+            table = hit.astype(BF16)
+            picked = ordered(dot(table, result_own[...]), dot(table, result_peer[...]))
+            mixture = mixture + gates[here, j : j + 1] * picked
+        block_out[here, :] = mixture.astype(BF16)
+        return carry
+
+    for k in range(2 * sums.steps):
+        if k < sums.steps:
+            for i in (0, 1):
+                sums.advance(i, sums.steps + k)
+        for i in (4, 2, 3, 5):
+            sums.advance(i, k)
+        if k == sums.steps - 1:
+            share.wait()
+        if k >= sums.steps - 1:
+            first_chunk = (k - sums.steps + 1) * chunks // (sums.steps + 1)
+            lax.fori_loop(first_chunk, (k - sums.steps + 2) * chunks // (sums.steps + 1), blend, 0)
+    at = 0
+    for out, picked in zip(vectors_out, layout):
+        for i in range(len(picked)):
+            out[i : i + 1, :] = get_row(small_sums, at, out.shape[1]).astype(F32)
+            at += out.shape[1] // 128
+
+
+def widen(pairs, layout, *refs):
+    ins, outs = refs[: pairs + len(layout)], refs[pairs + len(layout) :]
+    for source, out in zip(ins[:pairs], outs[:pairs]):
+        out[...] = source[...].astype(out.dtype)
+    outs = iter(outs[pairs:])
+    for source, picked in zip(ins[pairs:], layout):
+        for r in picked:
+            out = next(outs)
+            out[...] = source[r : r + out.shape[0], : out.shape[1]]
+
+
+def shards(
+    wide,
+    tokens_in, pre_gain, pre_shift, qkv_weight, qv_bias, proj_weight, proj_bias, mid_gain, mid_shift,
+    hidden_weight, hidden_bias, output_weight, output_bias, moe_gain, moe_shift, router_weight,
+    expert_in, expert_in_bias, expert_out, expert_out_bias, expert_ids, priority, cotangent,
+):
+    tokens, model = tokens_in.shape
+    width = qkv_weight.shape[2]
+    heads = width // HEAD_DIM
+    hidden = hidden_weight.shape[1]
+    count = router_weight.shape[1]
+    capacity = tokens // count
+    room = -(-capacity // 16) * 16
+    slots = count * room
+    half = model // 2
+    lanes = 3 * width
+    rows = 2 * PATCHES
+    chunks = tokens // rows
+    group = 4
+    steps = wide.bit_length() - 1
+
+    def row(vector):
+        return vector.reshape(1, -1)
+
+    def remote(kernel, name, identity, ins, outs, scratch):
+        return pl.pallas_call(
+            kernel,
+            out_shape=[jax.ShapeDtypeStruct(shape, dtype) for shape, dtype in outs],
+            in_specs=[pl.BlockSpec(memory_space=pltpu.VMEM)] * len(ins),
+            out_specs=[pl.BlockSpec(memory_space=pltpu.VMEM)] * len(outs),
+            scratch_shapes=scratch,
+            compiler_params=pltpu.CompilerParams(
+                vmem_limit_bytes=VMEM_BYTES, collective_id=identity, has_side_effects=True
+            ),
+            name=name,
+        )(*ins)
+
+    def room_for(local):
+        return [pltpu.VMEM(shape, dtype) for shape, dtype in local]
+
+    pre_gain, pre_shift, proj_bias = row(pre_gain), row(pre_shift), row(proj_bias)
+    mid_gain, mid_shift, hidden_bias = row(mid_gain), row(mid_shift), row(hidden_bias)
+    output_bias, moe_gain, moe_shift = row(output_bias), row(moe_gain), row(moe_shift)
+    weight_qkv = qkv_weight.transpose(1, 0, 2)
+    router = router_weight.T
+    targets, choices = slot_targets(expert_ids.T, priority[0], capacity, room)
+
+    qkv, context, first, second, lowered, route, gates, table, upstream = remote(
+        functools.partial(forward, wide, room, group, heads, rows), "forward", 1,
+        [tokens_in, cotangent, targets, choices, pre_gain, pre_shift, weight_qkv, qv_bias, proj_weight, proj_bias,
+         mid_gain, mid_shift, hidden_weight, hidden_bias, output_weight, output_bias, moe_gain, moe_shift, router],
+        [((tokens, lanes), BF16), ((tokens, width), BF16), ((tokens, model), F32), ((tokens, model), F32),
+         ((tokens, model), BF16), ((tokens, count), F32), ((tokens, 2), F32), ((count, 128), F32), ((slots, model), BF16)],
+        room_for([((slots, model), BF16), ((width, model), BF16), ((tokens, width), BF16), ((tokens, model), BF16),
+                  ((tokens, model), BF16)]) + [pltpu.SemaphoreType.DMA((2, wide + 2 * chunks + 1))],
+    )
+
+    tables = [((count, 8, 128), F32)] * 5
+    row_own, row_peer, gate_grads, result, in_grad, out_grad, in_bias, out_bias = remote(
+        functools.partial(experts, wide, room, group), "experts", 2,
+        [lowered, targets, table, upstream, expert_in[0], expert_in_bias, expert_out[0], expert_out_bias],
+        [((slots, half), BF16), ((slots, half), BF16), ((count, 128), F32), ((slots, half), BF16),
+         ((model, hidden), BF16), ((hidden, model), BF16), ((8, hidden), F32), ((8, model), F32)],
+        room_for([((slots, model), BF16), ((slots, model), BF16), ((slots, hidden), BF16), ((slots, hidden), BF16),
+                  ((slots, model), BF16), ((slots, half), F32), ((slots, half), BF16), ((slots, half), BF16),
+                  ((slots, half), F32), ((slots, half), BF16), ((slots, half), BF16), ((slots, half), BF16)] + tables)
+        + [pltpu.SemaphoreType.DMA((2, 4 * wide + 3 * (wide // group) + 1))],
+    )
+
+    layout = [(0, 1), (0, 1, 2), (0, 1, 2), (0,), (0,), tuple(range(count))]
+    vectors = [((8, model), F32), ((8, model), F32), ((8, model), F32), ((8, hidden), F32), ((8, lanes), F32), ((count, model), F32)]
+    near, far = tuple(range(steps)), (0,) + tuple(range(2, steps)) + (1,)
+    summed = [(model, hidden), (hidden, model), (3 * model // 2, width), (3 * model // 2, width), (width, model), (16 * wide, 128)]
+    block_out, grad, hidden_g, output_g, qkv_g, proj_g, *sums = remote(
+        functools.partial(backward, wide, room, heads, layout, (near, far, near, far, near, far), rows), "backward", 3,
+        [second, cotangent, route, choices, gates, moe_gain, moe_shift, router, gate_grads, row_own, row_peer, result,
+         first, tokens_in, qkv, context, mid_gain, mid_shift, pre_gain, pre_shift, hidden_weight, hidden_bias,
+         output_weight, proj_weight, weight_qkv],
+        [((tokens, model), BF16), ((tokens, model), F32), ((model, hidden), BF16), ((hidden, model), BF16),
+         ((3 * model, width), BF16), ((width, model), BF16)] + vectors,
+        room_for([((tokens, model), BF16), ((tokens, hidden), BF16), ((tokens, hidden), BF16), ((tokens, model), BF16),
+                  ((tokens, model), BF16), ((tokens, model), BF16), ((tokens, lanes), BF16), ((tokens, model), BF16),
+                  ((tokens, model), BF16), ((slots, half), BF16), ((slots, half), BF16), ((8, model), F32),
+                  ((count, model), F32), ((8, model), F32), ((8, hidden), F32), ((8, lanes), F32), ((8, model), F32),
+                  (summed[-1], BF16), (summed[0], F32), (summed[1], F32), ((3 * model, width), F32), (summed[4], F32),
+                  (summed[5], F32)] + [(shape, BF16) for shape in summed] * 2)
+        + [pltpu.SemaphoreType.DMA((2, chunks))] * 2 + [pltpu.SemaphoreType.DMA((2, wide + 1))]
+        + [pltpu.SemaphoreType.DMA((len(summed), 2 * steps))] * 2,
+    )
+
+    pairs = [
+        (block_out, BF16), (grad, F32), (hidden_g, F32), (output_g, F32), (qkv_g.reshape(3, model, width), F32),
+        (proj_g, F32), (in_grad, F32), (out_grad, F32),
+    ]
+    singles = [(0, 1), (0, 1, 2), (0, 1, 2), (0,), (0,), (0,), (0,), (0,)]
+    sources = list(sums) + [in_bias, out_bias]
+    sizes = [(1, model)] * 8 + [(1, hidden), (1, lanes), (count, model), (1, hidden), (1, model)]
+    parts = 4
+
+    def spec(shape):
+        if len(shape) == 3:
+            return pl.BlockSpec((shape[0], shape[1] // parts, shape[2]), lambda i: (0, i, 0))
+        return pl.BlockSpec((shape[0] // parts, shape[1]), lambda i: (i, 0))
+
+    def whole(shape):
+        return pl.BlockSpec(shape, lambda i: (0, 0))
+
+    outs = pl.pallas_call(
+        functools.partial(widen, len(pairs), singles),
+        grid=(parts,),
+        in_specs=[spec(source.shape) for source, _ in pairs] + [whole(source.shape) for source in sources],
+        out_specs=[spec(source.shape) for source, _ in pairs] + [whole(size) for size in sizes],
+        out_shape=[jax.ShapeDtypeStruct(source.shape, dtype) for source, dtype in pairs]
+        + [jax.ShapeDtypeStruct(size, F32) for size in sizes],
+        compiler_params=pltpu.CompilerParams(vmem_limit_bytes=VMEM_BYTES),
+        name="widen",
+    )(*[source for source, _ in pairs], *sources)
+    block_out, grad, hidden_g, output_g, qkv_g, proj_g, in_grad, out_grad = outs[:8]
+    pre_gain_g, pre_shift_g, mid_gain_g, mid_shift_g, proj_bias_g, moe_gain_g, moe_shift_g, output_bias_g = (
+        vector.reshape(model) for vector in outs[8:16]
+    )
+    hidden_bias_g, qkv_bias_g, router_g, in_bias_g, out_bias_g = outs[16:]
+    return (
+        block_out, grad, pre_gain_g, pre_shift_g, qkv_g.transpose(1, 0, 2),
+        jnp.concatenate([qkv_bias_g[:, :width], qkv_bias_g[:, 2 * width :]]), proj_g, proj_bias_g, mid_gain_g,
+        mid_shift_g, hidden_g, hidden_bias_g.reshape(hidden), output_g, output_bias_g, moe_gain_g, moe_shift_g,
+        router_g.T, in_grad[None], in_bias_g, out_grad[None], out_bias_g,
+    )
 
 
 def layer_norm(values, gain, shift):
@@ -38,7 +946,7 @@
     return (tables, kept)
 
 
-def shards(
+def plain(
     tokens_in,
     pre_gain,
     pre_shift,
@@ -252,56 +1160,20 @@
 
 
 def solution(mesh):
+    body = functools.partial(shards, mesh.shape["wide"]) if mesh.shape["tensor"] == 2 else plain
     return jax.shard_map(
-        shards,
+        body,
         mesh=mesh,
         in_specs=(
-            P("wide", None),
-            P(),
-            P(),
-            P(None, None, "tensor"),
-            P(None, "tensor"),
-            P("tensor", None),
-            P(),
-            P(),
-            P(),
-            P(None, "tensor"),
-            P("tensor"),
-            P("tensor", None),
-            P(),
-            P(),
-            P(),
-            P(),
-            P("wide", None, "tensor"),
-            P("wide", "tensor"),
-            P("wide", "tensor", None),
-            P("wide", None),
-            P("wide", None),
-            P("wide", None),
-            P("wide", None),
+            P("wide", None), P(), P(), P(None, None, "tensor"), P(None, "tensor"), P("tensor", None), P(), P(), P(),
+            P(None, "tensor"), P("tensor"), P("tensor", None), P(), P(), P(), P(),
+            P("wide", None, "tensor"), P("wide", "tensor"), P("wide", "tensor", None), P("wide", None),
+            P("wide", None), P("wide", None), P("wide", None),
         ),
         out_specs=(
-            P("wide", None),
-            P("wide", None),
-            P(),
-            P(),
-            P(None, None, "tensor"),
-            P(None, "tensor"),
-            P("tensor", None),
-            P(),
-            P(),
-            P(),
-            P(None, "tensor"),
-            P("tensor"),
-            P("tensor", None),
-            P(),
-            P(),
-            P(),
-            P(),
-            P("wide", None, "tensor"),
-            P("wide", "tensor"),
-            P("wide", "tensor", None),
-            P("wide", None),
+            P("wide", None), P("wide", None), P(), P(), P(None, None, "tensor"), P(None, "tensor"), P("tensor", None),
+            P(), P(), P(), P(None, "tensor"), P("tensor"), P("tensor", None), P(), P(), P(), P(),
+            P("wide", None, "tensor"), P("wide", "tensor"), P("wide", "tensor", None), P("wide", None),
         ),
         check_vma=False,
     )

time: 765 us -> 265 us (0.35); the launches traced: 756 us -> 264 us
  waiting for transfers between devices: 358 us -> 0 us
  Pallas kernels: 0 us -> 255 us
  local copies, waits for them, and re-layouts: 118 us -> 2.48 us
  matrix products: 99.8 us -> 0 us
  other arithmetic: 75.2 us -> 6.43 us
  blocking collectives: 62.1 us -> 0 us
  starting transfers between devices: 27.5 us -> 0 us
  between operations: 15.9 us -> 0.73 us
    psum x6 -> x0, waiting for transfers between devices: 320 us -> none  [the longest x1 71.1 us: shards(): lax.psum(jnp.dot(context, proj_weight, preferred_element_type=jnp.float32...]
    pallas_call x0 -> x4, Pallas kernels: none -> 255 us  [the longest x3 246 us: remote(): pl.pallas_call(kernel, out_shape=[jax.ShapeDtypeStruct(shape, dtype) for...]
    dot_general x31 -> x0, matrix products: 99.8 us -> none  [the longest x1 7.59 us: shards(): jnp.einsum('jtk,kd->jtd', tables, returned, preferred_element_type=jnp.fl...]
    psum x1 -> x0, blocking collectives: 62.1 us -> none  [shards(): lax.psum(pre_gain_grad.astype(jnp.bfloat16), 'wide').astype(jnp.float32)]
    unnamed x241 -> x2, local copies, waits for them, and re-layouts: 52.7 us -> 0.01 us
    all_to_all x4 -> x0, waiting for transfers between devices: 37.7 us -> none  [the longest x1 17.3 us: shards(): lax.all_to_all(slot_grad, 'wide', split_axis=0, concat_axis=1, tiled=True)]
    all_to_all x4 -> x0, starting transfers between devices: 26.8 us -> none  [the longest x1 7.53 us: shards(): lax.all_to_all(arrived_grad, 'wide', split_axis=1, concat_axis=0, tiled=T...]
    reduce_sum x22 -> x1, other arithmetic: 30.8 us -> 4.38 us  [slot_targets(): position = jnp.sum(earlier.astype(jnp.int32), axis=1).reshape(2, count)]
  transfers between devices with their start and end apart: 10 -> 0, of which waited for: 10 -> 0; matrix products, arithmetic and copies ran while one was open for 15% -> 0% of each run, Pallas kernels for 0% -> 0%
where the time goes in v1:
time: 265 us; the launch traced here: 264 us
  Pallas kernels  255 us (96%)
  other arithmetic  6.43 us (2%)
    pallas_call x3, Pallas kernels, remote(): pl.pallas_call(kernel, out_shape=[jax.ShapeDtypeStruct(shape, dtype) for...  246 us
    pallas_call x1, Pallas kernels, shards(): pl.pallas_call(functools.partial(widen, len(pairs), singles), grid=(parts...  8.87 us

profile of v1, /device:TPU:0, one launch (start us, length us, event | category | flops | bytes accessed | tf_op | source)
XLA Modules:
  0.0 264.2 jit_solution(10268867817517002074)
XLA Ops:
  0.7 0.7 reduce
  1.4 0.7 eq.15
  2.1 4.4 %convert_reduce_fusion = s32[2304]{0:T(1024)S(1)} fusion(s32[2304]{0:T(1024)S(1)} %eq.15, s32[2304]{0:T(1024)S(1)} %pad_add_fusion.1), kind=kLoop, calls=%fused_computation | loop fusion | flops 26539776 | bytes 27648 | tf_op jit(solution)/shard_map/reduce_sum | solution.py:211
  6.5 0.7 broadcast_select_fusion.1
  7.2 0.0 copy-start
  7.3 1.1 copy.55
  8.3 0.0 copy-done
  8.3 61.5 %forward.1 = (bf16[1152,768]{1,0:T(8,128)(2,1)}, bf16[1152,256]{1,0:T(8,128)(2,1)}, f32[1152,512]{1,0:T(8,128)}, f32[1152,512]{1,0:T(8,128)}, bf16[1152,512]{1,0...) custom-call(bf16[1152,512]{1,0:T(8,128)(2,1)} %tokens.3, ...), custom_call_target="tpu_custom_call" | custom-call | tf_op jit(solution)/shard_map/forward/pallas_call | solution.py:813
  69.8 74.1 %experts.1 = (bf16[1280,256]{1,0:T(8,128)(2,1)}, bf16[1280,256]{1,0:T(8,128)(2,1)}, f32[16,128]{1,0:T(8,128)}, bf16[1280,256]{1,0:T(8,128)(2,1)}, bf16[512,1024]...) custom-call(bf16[1152,512]{1,0:T(8,128)(2,1)} %get-tuple-element.74.lowered, ...), custom_call_target="tpu_custom_call" | custom-call | tf_op jit(solution)/shard_map/experts/pallas_call | solution.py:813
  144.0 110.1 %backward.1 = (bf16[1152,512]{1,0:T(8,128)(2,1)}, f32[1152,512]{1,0:T(8,128)}, bf16[512,1024]{1,0:T(8,128)(2,1)}, bf16[1024,512]{1,0:T(8,128)(2,1)}, bf16[1536,2...) custom-call(f32[1152,512]{1,0:T(8,128)} %get-tuple-element.71.second, ...), custom_call_target="tpu_custom_call" | custom-call | tf_op jit(solution)/shard_map/backward/pallas_call | solution.py:813
  254.1 8.9 %widen.1 = (bf16[1152,512]{1,0:T(8,128)(2,1)}, f32[1152,512]{1,0:T(8,128)}, f32[512,1024]{1,0:T(8,128)}, f32[1024,512]{1,0:T(8,128)}, f32[3,512,256]{2,1,0:T(8,1...) custom-call(bf16[1152,512]{1,0:T(8,128)(2,1)} %get-tuple-element.84., ...), custom_call_target="tpu_custom_call" | custom-call | tf_op jit(solution)/shard_map/widen/pallas_call | solution.py:895
  263.0 0.7 fusion
  263.7 0.6 pad_maximum_fusion
  (4 shorter events, 0.0 us)
Async XLA Ops:
  7.2 1.1 copy-start

commit v2 on v1

--- a/solution.py
+++ b/solution.py
@@ -355,8 +355,8 @@
     wide, room, group,
     lowered, targets, table, upstream, weight_in, bias_in, weight_out, bias_out,
     own_home, peer_home, gate_home, result_out, in_grad, out_grad, in_bias_grad, out_bias_grad,
-    placed, arrived, act, inner_grad, slot_grad, grad_kept, grad_sent, grad_landed, result_kept, result_sent,
-    result_landed, grad_back, gate_sent, gate_arrived, gate_back, gate_own, gate_peer, sems,
+    columns, placed, rows_own, rows_peer, act, inner_grad, slot_grad, grad_kept, grad_sent, grad_landed,
+    grad_back, gate_sent, gate_arrived, gate_back, gate_own, gate_peer, sems,
 ):
     me, plane = lax.axis_index("wide"), lax.axis_index("tensor")
     groups = wide // group
@@ -364,8 +364,7 @@
     half = own_home.shape[1]
     block = group * room
     row_at, gate_at, home_at, back_at = 0, wide, 2 * wide, 3 * wide
-    grad_at, result_at, share_at, table_at = 4 * wide, 4 * wide + groups, 4 * wide + 2 * groups, 4 * wide + 3 * groups
-
+    grad_at, share_at, join_at, table_at = 4 * wide, 4 * wide + groups, 4 * wide + 2 * groups, 4 * wide + 3 * groups
     greet(wide)
 
     def rows_of(index):
@@ -380,7 +379,7 @@
         )
 
     def row_copy(other, sender):
-        return move(placed.at[rows_of(other)], arrived.at[rows_of(sender)], row_at, other, sender, (other, plane))
+        return move(placed.at[rows_of(other)], rows_own.at[rows_of(sender)], row_at, other, sender, (other, plane))
 
     def gate_copy(other, sender):
         return move(gate_sent.at[other], gate_arrived.at[sender], gate_at, other, sender, (other, plane))
@@ -395,6 +394,10 @@
         there = rows_of_group(index)
         return move(source.at[there], target.at[there], base, index, index, (me, 1 - plane))
 
+    first_plane = plane == 0
+    columns[...] = jnp.where(first_plane, lowered[:, :half], lowered[:, half:])
+    own_half = pl.ds(pl.multiple_of(plane * half, 16), half)
+    peer_half = pl.ds(pl.multiple_of((1 - plane) * half, 16), half)
     for e in range(wide):
         gate_sent[e] = jnp.broadcast_to(table[e : e + 1, :], gate_sent.shape[1:])
     in_bias_grad[...] = jnp.zeros_like(in_bias_grad)
@@ -402,9 +405,7 @@
 
     def place_group(k, carry):
         q = lax.rem(mine + k, groups)
-        slot = q * block + lax.broadcasted_iota(jnp.int32, (block, targets.shape[1]), 0)
-        hits = ((slot == targets[0:1, :]) | (slot == targets[1:2, :])).astype(BF16)
-        placed[rows_of_group(q), :] = dot(hits, lowered[...]).astype(BF16)
+        placed[rows_of_group(q), :] = dot(slot_hits(q * block, block, targets), columns[...]).astype(BF16)
         for j in range(group):
             e = q * group + j
 
@@ -415,14 +416,66 @@
 
             @pl.when(e == me)
             def _(e=e):
-                arrived[rows_of(e), :] = placed[rows_of(e), :]
+                rows_own[rows_of(e), :] = placed[rows_of(e), :]
                 gate_arrived[e] = gate_sent[e]
 
         return carry
 
     lax.fori_loop(0, groups, place_group, 0)
     diagonal = lax.broadcasted_iota(jnp.int32, (room, 128), 0) == lax.broadcasted_iota(jnp.int32, (room, 128), 1)
-    first_plane = plane == 0
+
+    def join_group(p):
+        for j in range(group):
+            w = p * group + j
+
+            @pl.when(w != me)
+            def _(w=w):
+                row_copy(w, w).wait_recv()
+                gate_copy(w, w).wait_recv()
+
+        across(rows_own, rows_peer, join_at, p).start()
+
+    def expert_group(p):
+        there = rows_of_group(p)
+        across(rows_own, rows_peer, join_at, p).wait()
+        gates = jnp.concatenate(
+            [
+                jnp.sum(jnp.where(diagonal, gate_arrived[p * group + j][0:1, :], 0.0), axis=1, keepdims=True)
+                for j in range(group)
+            ],
+            axis=0,
+        )
+        inner = dot(rows_own[there, :], weight_in[own_half, :]) + dot(rows_peer[there, :], weight_in[peer_half, :])
+        acted, slope = gelu_parts(inner + bias_in[...])
+        acted = acted.astype(BF16)
+        act[there, :] = acted
+        raised = upstream[there, :].astype(F32)
+        slot = (raised * gates).astype(BF16)
+        slot_grad[there, :] = slot
+        inward = (dot_rows(slot, weight_out[...]) * slope).astype(BF16)
+        inner_grad[there, :] = inward
+        grad_sent[there, :] = dot_rows(inward, weight_in[peer_half, :]).astype(BF16)
+        across(grad_sent, grad_landed, grad_at, p).start()
+        grad_kept[there, :] = dot_rows(inward, weight_in[own_half, :])
+        result = dot(acted, weight_out[...]) + bias_out[...] * jnp.where(first_plane, 1.0, 0.0)
+        result_out[there, :] = result.astype(BF16)
+        out_bias_grad[0:1, :] += jnp.sum(slot.astype(F32), axis=0, keepdims=True)
+        in_bias_grad[0:1, :] += jnp.sum(inward.astype(F32), axis=0, keepdims=True)
+        slopes = jnp.sum(raised * result, axis=1, keepdims=True)
+        for j in range(group):
+            w = p * group + j
+            row = jnp.sum(
+                jnp.where(diagonal, slopes[j * room : (j + 1) * room], 0.0), axis=0, keepdims=True
+            )
+            gate_back[w] = jnp.broadcast_to(row, gate_back.shape[1:])
+
+            @pl.when(w != me)
+            def _(w=w):
+                back_copy(w, me).start()
+
+            @pl.when(w == me)
+            def _(w=w):
+                gate_own[w] = gate_back[w]
 
     def give_back(p):
         across(grad_sent, grad_landed, grad_at, p).wait()
@@ -439,68 +492,22 @@
             def _(w=w):
                 own_home[rows_of(w), :] = grad_back[rows_of(w), :]
 
-    def expert_group(k, carry):
-        p = lax.rem(mine + groups - k, groups)
-        there = rows_of_group(p)
-        columns = []
-        for j in range(group):
-            w = p * group + j
-
-            @pl.when(w != me)
-            def _(w=w):
-                row_copy(w, w).wait_recv()
-                gate_copy(w, w).wait_recv()
-
-            columns.append(jnp.sum(jnp.where(diagonal, gate_arrived[w][0:1, :], 0.0), axis=1, keepdims=True))
-        gates = jnp.concatenate(columns, axis=0)
-        inner = dot(arrived[there, :], weight_in[...]) + bias_in[...]
-        acted, slope = gelu_parts(inner)
-        acted = acted.astype(BF16)
-        act[there, :] = acted
-        result = dot(acted, weight_out[...])
-        raised = upstream[there, :].astype(F32)
-        slot = (raised * gates).astype(BF16)
-        slot_grad[there, :] = slot
-        out_bias_grad[0:1, :] += jnp.sum(slot.astype(F32), axis=0, keepdims=True)
-        inward = (dot_rows(slot, weight_out[...]) * slope).astype(BF16)
-        inner_grad[there, :] = inward
-        in_bias_grad[0:1, :] += jnp.sum(inward.astype(F32), axis=0, keepdims=True)
-        grad = dot_rows(inward, weight_in[...])
-        low, high = grad[:, :half], grad[:, half:]
-        grad_sent[there, :] = jnp.where(first_plane, high, low).astype(BF16)
-        across(grad_sent, grad_landed, grad_at, p).start()
-        grad_kept[there, :] = jnp.where(first_plane, low, high)
-        biased = result + bias_out[...]
-        low, high = biased[:, :half], biased[:, half:]
-        result_kept[there, :] = jnp.where(first_plane, low, high)
-        low, high = result[:, :half], result[:, half:]
-        result_sent[there, :] = jnp.where(first_plane, high, low).astype(BF16)
-        across(result_sent, result_landed, result_at, p).start()
-        slopes = jnp.sum(raised * jnp.where(first_plane, biased, result), axis=1, keepdims=True)
-        for j in range(group):
-            w = p * group + j
-            row = jnp.sum(
-                jnp.where(diagonal, slopes[j * room : (j + 1) * room], 0.0), axis=0, keepdims=True
-            )
-            gate_back[w] = jnp.broadcast_to(row, gate_back.shape[1:])
-
-            @pl.when(w != me)
-            def _(w=w):
-                back_copy(w, me).start()
-
-            @pl.when(w == me)
-            def _(w=w):
-                gate_own[w] = gate_back[w]
-
-        @pl.when(k > 0)
+    def turn(k, carry):
+        @pl.when(k < groups)
         def _():
-            give_back(lax.rem(mine + groups - k + 1, groups))
-
-        return carry
-
-    lax.fori_loop(0, groups, expert_group, 0)
-    give_back(lax.rem(mine + 1, groups))
-
+            join_group(lax.rem(mine + groups - k, groups))
+
+        @pl.when((k >= 1) & (k <= groups))
+        def _():
+            expert_group(lax.rem(mine + groups - k + 1, groups))
+
+        @pl.when(k >= 2)
+        def _():
+            give_back(lax.rem(mine + groups - k + 2, groups))
+
+        return carry
+
+    lax.fori_loop(0, groups + 2, turn, 0)
     tile = act.shape[1] // groups
 
     def share_group(k, carry):
@@ -520,25 +527,15 @@
     lax.fori_loop(0, groups, share_group, 0)
 
     def take_gates(d, carry):
-        back_copy(lax.rem(me + d, wide), lax.rem(me + d, wide)).wait_recv()
+        other = lax.rem(me + d, wide)
+        back_copy(other, other).wait_recv()
         return carry
 
     lax.fori_loop(1, wide, take_gates, 0)
     tables = move(gate_own, gate_peer, table_at, 0, 0, (me, 1 - plane))
     tables.start()
-
-    def put(at, tile, value):
-        in_grad[pl.ds(at, tile), :] = value.astype(BF16)
-
-    column_dots(arrived, inner_grad, put)
-
-    def take_result(p, carry):
-        across(result_sent, result_landed, result_at, p).wait()
-        there = rows_of_group(p)
-        result_out[there, :] = (result_kept[there, :] + result_landed[there, :].astype(F32)).astype(BF16)
-        return carry
-
-    lax.fori_loop(0, groups, take_result, 0)
+    in_grad[own_half, :] = dot_columns(rows_own[...], inner_grad[...]).astype(BF16)
+    in_grad[peer_half, :] = dot_columns(rows_peer[...], inner_grad[...]).astype(BF16)
 
     def end_sends(d, carry):
         other = lax.rem(me + d, wide)
@@ -567,12 +564,13 @@
     weight_qkv,
     block_out, grad_out, hidden_out, output_out, qkv_out, proj_out, *rest,
 ):
-    vectors_out, rest = rest[: len(layout)], rest[len(layout) :]
-    (lowered_mid, act, inner_grad, mid_own, mid_peer, branch, qkv_grad, lowered_pre, pre_peer, result_own, result_peer,
-     moe_sums, router_sums, mid_sums, hidden_sums, qkv_sums, pre_sums, small_sums) = rest[:18]
-    hidden_total, output_total, qkv_total, proj_total, small = rest[18:23]
-    sends, lands = rest[23:29], rest[29:35]
-    mid_sems, pre_sems, result_sems, send_sems, recv_sems = rest[35:]
+    vectors_out, pre_out, rest = rest[: len(layout)], rest[len(layout)], rest[len(layout) + 1 :]
+    (lowered_mid, act, inner_grad, mid_own, mid_peer, branch, qkv_grad, lowered_pre, pre_peer, result_own, blend_peer,
+     pre_tile, pre_tiles, pre_total, pre_other, moe_sums, router_sums, mid_sums, hidden_sums, qkv_sums, pre_sums, small_sums) = rest[:22]
+    hidden_total, output_total, qkv_total, proj_total, small = rest[22:27]
+    sends, lands = rest[27:33], rest[33:39]
+    mid_sems, pre_sems, blend_sems, result_sems, send_sems, recv_sems = rest[39:]
+    blend_own = lowered_mid
     me, plane = lax.axis_index("wide"), lax.axis_index("tensor")
     chunks = tokens.shape[0] // rows
     model = tokens.shape[1]
@@ -690,7 +688,11 @@
             grad = image_back(heads, block, context_grad[image * PATCHES : (image + 1) * PATCHES])
             qkv_grad[pl.ds(at, PATCHES), :] = grad
             pre = sum(dot_rows(grad[:, s * width : (s + 1) * width], weight_qkv[s]) for s in range(3))
-            mid_own[pl.ds(at, PATCHES), :] = pre.astype(BF16)
+            pre = pre.astype(BF16)
+            mid_own[pl.ds(at, PATCHES), :] = pre
+            pre = pre.astype(F32)
+            pre_sums[0:1, :] += jnp.sum(pre * normed[image * PATCHES : (image + 1) * PATCHES], axis=0, keepdims=True)
+            pre_sums[1:2, :] += jnp.sum(pre, axis=0, keepdims=True)
             qkv_sums[0:1, :] += jnp.sum(grad.astype(F32), axis=0, keepdims=True)
             for k in range(sums.steps):
 
@@ -704,18 +706,26 @@
 
     lax.fori_loop(0, chunks, attend_chunk, 0)
 
-    def take_result(d, carry):
-        other = lax.rem(me + d, wide)
-        result_copy(other, other).wait_recv()
-        result_copy(other, me).wait_send()
-        return carry
-
-    lax.fori_loop(1, wide, take_result, 0)
-    share = pltpu.make_async_remote_copy(
-        result_own, result_peer, result_sems.at[0, wide], result_sems.at[1, wide],
-        device_id=(me, 1 - plane), device_id_type=MESH,
-    )
-    share.start()
+    small[...] = jnp.zeros_like(small)
+    at = 0
+    for vector, picked in zip((mid_sums, moe_sums, hidden_sums, qkv_sums, router_sums), layout):
+        for r in picked:
+            at = put_row(small, at, vector[r : r + 1, :])
+    sums.begin(5, 0)
+    put_row(pre_tile, put_row(pre_tile, 0, pre_sums[0:1, :]), pre_sums[1:2, :])
+
+    def pre_copy(other, sender):
+        return pltpu.make_async_remote_copy(
+            pre_tile, pre_tiles.at[sender], result_sems.at[0, wide + other], result_sems.at[1, wide + sender],
+            device_id=(other, plane), device_id_type=MESH,
+        )
+
+    def send_pre(d, carry):
+        pre_copy(lax.rem(me + d, wide), me).start()
+        return carry
+
+    lax.fori_loop(1, wide, send_pre, 0)
+    pre_tiles[me] = pre_tile[...]
     column_dots(context, branch, put_in(proj_total))
     sums.begin(4, 0)
 
@@ -734,39 +744,61 @@
         upstream = mid_own[here, :].astype(F32) + pre_peer[here, :].astype(F32)
         normed, scale = normalized(tokens[here, :].astype(F32))
         grad_out[here, :] += norm_back(normed, scale, pre_gain[...], upstream)
-        pre_sums[0:1, :] += jnp.sum(upstream * normed, axis=0, keepdims=True)
-        pre_sums[1:2, :] += jnp.sum(upstream, axis=0, keepdims=True)
-        return carry
-
-    lax.fori_loop(0, chunks, finish_chunk, 0)
-    small[...] = jnp.zeros_like(small)
-    at = 0
-    for vector, picked in zip((pre_sums, mid_sums, moe_sums, hidden_sums, qkv_sums, router_sums), layout):
-        for r in picked:
-            at = put_row(small, at, vector[r : r + 1, :])
-    sums.begin(5, 0)
+        return carry
+
+    def take_result(d, carry):
+        other = lax.rem(me + d, wide)
+        result_copy(other, other).wait_recv()
+        result_copy(other, me).wait_send()
+        return carry
+
+    lax.fori_loop(1, wide, take_result, 0)
 
     def blend(chunk, carry):
         here = pl.ds(pl.multiple_of(chunk * rows, rows), rows)
-        mixture = second[here, :]
-        for j, hit in enumerate(token_hits(choices[here, :], result_own.shape[0])):
-            table = hit.astype(BF16)
-            picked = ordered(dot(table, result_own[...]), dot(table, result_peer[...]))
-            mixture = mixture + gates[here, j : j + 1] * picked
-        block_out[here, :] = mixture.astype(BF16)
-        return carry
-
+        hits = token_hits(choices[here, :], result_own.shape[0])
+        table = jnp.where(hits[0], gates[here, 0:1], jnp.where(hits[1], gates[here, 1:2], 0.0)).astype(BF16)
+        blend_own[here, :] = dot(table, result_own[...]).astype(BF16)
+        across(blend_own, blend_peer, blend_sems, chunk).start()
+        return carry
+
+    def blend_end(chunk, carry):
+        here = pl.ds(pl.multiple_of(chunk * rows, rows), rows)
+        across(blend_own, blend_peer, blend_sems, chunk).wait()
+        mixture = blend_own[here, :].astype(F32) + blend_peer[here, :].astype(F32)
+        block_out[here, :] = (second[here, :] + mixture).astype(BF16)
+        return carry
+
+    def take_pre(d, carry):
+        other = lax.rem(me + d, wide)
+        pre_copy(other, other).wait_recv()
+        pre_copy(other, me).wait_send()
+        return carry
+
+    pre_share = pltpu.make_async_remote_copy(
+        pre_total, pre_other, result_sems.at[0, 2 * wide], result_sems.at[1, 2 * wide],
+        device_id=(me, 1 - plane), device_id_type=MESH,
+    )
     for k in range(2 * sums.steps):
         if k < sums.steps:
             for i in (0, 1):
                 sums.advance(i, sums.steps + k)
-        for i in (4, 2, 3, 5):
+        for i in (5, 4, 2, 3):
             sums.advance(i, k)
+        if k < sums.steps:
+            lax.fori_loop(k * chunks // sums.steps, (k + 1) * chunks // sums.steps, blend, 0)
+            lax.fori_loop(k * chunks // sums.steps, (k + 1) * chunks // sums.steps, finish_chunk, 0)
+        else:
+            first_chunk = (k - sums.steps) * chunks // sums.steps
+            lax.fori_loop(first_chunk, (k - sums.steps + 1) * chunks // sums.steps, blend_end, 0)
         if k == sums.steps - 1:
-            share.wait()
-        if k >= sums.steps - 1:
-            first_chunk = (k - sums.steps + 1) * chunks // (sums.steps + 1)
-            lax.fori_loop(first_chunk, (k - sums.steps + 2) * chunks // (sums.steps + 1), blend, 0)
+            lax.fori_loop(1, wide, take_pre, 0)
+            pre_total[...] = sum(pre_tiles[w] for w in range(wide))
+            pre_share.start()
+    pre_share.wait()
+    pre_tile[...] = pre_total[...] + pre_other[...]
+    pre_out[0:1, :] = get_row(pre_tile, 0, model)
+    pre_out[1:2, :] = get_row(pre_tile, model // 128, model)
     at = 0
     for out, picked in zip(vectors_out, layout):
         for i in range(len(picked)):
@@ -846,16 +878,16 @@
     row_own, row_peer, gate_grads, result, in_grad, out_grad, in_bias, out_bias = remote(
         functools.partial(experts, wide, room, group), "experts", 2,
         [lowered, targets, table, upstream, expert_in[0], expert_in_bias, expert_out[0], expert_out_bias],
-        [((slots, half), BF16), ((slots, half), BF16), ((count, 128), F32), ((slots, half), BF16),
+        [((slots, half), BF16), ((slots, half), BF16), ((count, 128), F32), ((slots, model), BF16),
          ((model, hidden), BF16), ((hidden, model), BF16), ((8, hidden), F32), ((8, model), F32)],
-        room_for([((slots, model), BF16), ((slots, model), BF16), ((slots, hidden), BF16), ((slots, hidden), BF16),
-                  ((slots, model), BF16), ((slots, half), F32), ((slots, half), BF16), ((slots, half), BF16),
-                  ((slots, half), F32), ((slots, half), BF16), ((slots, half), BF16), ((slots, half), BF16)] + tables)
+        room_for([((tokens, half), BF16), ((slots, half), BF16), ((slots, half), BF16), ((slots, half), BF16),
+                  ((slots, hidden), BF16), ((slots, hidden), BF16), ((slots, model), BF16), ((slots, half), F32),
+                  ((slots, half), BF16), ((slots, half), BF16), ((slots, half), BF16)] + tables)
         + [pltpu.SemaphoreType.DMA((2, 4 * wide + 3 * (wide // group) + 1))],
     )
 
-    layout = [(0, 1), (0, 1, 2), (0, 1, 2), (0,), (0,), tuple(range(count))]
-    vectors = [((8, model), F32), ((8, model), F32), ((8, model), F32), ((8, hidden), F32), ((8, lanes), F32), ((count, model), F32)]
+    layout = [(0, 1, 2), (0, 1, 2), (0,), (0,), tuple(range(count))]
+    vectors = [((8, model), F32), ((8, model), F32), ((8, hidden), F32), ((8, lanes), F32), ((count, model), F32)]
     near, far = tuple(range(steps)), (0,) + tuple(range(2, steps)) + (1,)
     summed = [(model, hidden), (hidden, model), (3 * model // 2, width), (3 * model // 2, width), (width, model), (16 * wide, 128)]
     block_out, grad, hidden_g, output_g, qkv_g, proj_g, *sums = remote(
@@ -864,14 +896,15 @@
          first, tokens_in, qkv, context, mid_gain, mid_shift, pre_gain, pre_shift, hidden_weight, hidden_bias,
          output_weight, proj_weight, weight_qkv],
         [((tokens, model), BF16), ((tokens, model), F32), ((model, hidden), BF16), ((hidden, model), BF16),
-         ((3 * model, width), BF16), ((width, model), BF16)] + vectors,
+         ((3 * model, width), BF16), ((width, model), BF16)] + vectors + [((8, model), F32)],
         room_for([((tokens, model), BF16), ((tokens, hidden), BF16), ((tokens, hidden), BF16), ((tokens, model), BF16),
                   ((tokens, model), BF16), ((tokens, model), BF16), ((tokens, lanes), BF16), ((tokens, model), BF16),
-                  ((tokens, model), BF16), ((slots, half), BF16), ((slots, half), BF16), ((8, model), F32),
-                  ((count, model), F32), ((8, model), F32), ((8, hidden), F32), ((8, lanes), F32), ((8, model), F32),
+                  ((tokens, model), BF16), ((slots, model), BF16), ((tokens, model), BF16),
+                  ((2 * model // 128, 128), F32), ((wide, 2 * model // 128, 128), F32), ((2 * model // 128, 128), F32),
+                  ((2 * model // 128, 128), F32), ((8, model), F32), ((count, model), F32), ((8, model), F32), ((8, hidden), F32), ((8, lanes), F32), ((8, model), F32),
                   (summed[-1], BF16), (summed[0], F32), (summed[1], F32), ((3 * model, width), F32), (summed[4], F32),
                   (summed[5], F32)] + [(shape, BF16) for shape in summed] * 2)
-        + [pltpu.SemaphoreType.DMA((2, chunks))] * 2 + [pltpu.SemaphoreType.DMA((2, wide + 1))]
+        + [pltpu.SemaphoreType.DMA((2, chunks))] * 3 + [pltpu.SemaphoreType.DMA((2, 2 * wide + 1))]
         + [pltpu.SemaphoreType.DMA((len(summed), 2 * steps))] * 2,
     )
 
@@ -880,7 +913,7 @@
         (proj_g, F32), (in_grad, F32), (out_grad, F32),
     ]
     singles = [(0, 1), (0, 1, 2), (0, 1, 2), (0,), (0,), (0,), (0,), (0,)]
-    sources = list(sums) + [in_bias, out_bias]
+    sources = [sums[-1]] + list(sums[:-1]) + [in_bias, out_bias]
     sizes = [(1, model)] * 8 + [(1, hidden), (1, lanes), (count, model), (1, hidden), (1, model)]
     parts = 4
 

time: 265 us -> 242 us (0.913)
  Pallas kernels: 255 us -> 232 us
    pallas_call x3, Pallas kernels: 246 us -> 223 us  [remote(): pl.pallas_call(kernel, out_shape=[jax.ShapeDtypeStruct(shape, dtype) for...]
where the time goes in v2:
time: 242 us
  Pallas kernels  232 us (96%)
  other arithmetic  6.43 us (3%)
  local copies, waits for them, and re-layouts  2.48 us (1%)
    pallas_call x3, Pallas kernels, remote(): pl.pallas_call(kernel, out_shape=[jax.ShapeDtypeStruct(shape, dtype) for...  223 us
    pallas_call x1, Pallas kernels, shards(): pl.pallas_call(functools.partial(widen, len(pairs), singles), grid=(parts...  8.87 us

profile of v2, /device:TPU:0, one launch (start us, length us, event | category | flops | bytes accessed | tf_op | source)
XLA Modules:
  0.0 241.7 jit_solution(15272026698008486455)
XLA Ops:
  0.7 0.7 reduce
  1.4 0.7 eq.15
  2.1 4.4 %convert_reduce_fusion = s32[2304]{0:T(1024)S(1)} fusion(s32[2304]{0:T(1024)S(1)} %eq.15, s32[2304]{0:T(1024)S(1)} %pad_add_fusion.1), kind=kLoop, calls=%fused_computation | loop fusion | flops 26539776 | bytes 27648 | tf_op jit(solution)/shard_map/reduce_sum | solution.py:211
  6.5 0.7 broadcast_select_fusion.1
  7.2 0.0 copy-start
  7.3 1.1 copy.55
  8.3 0.0 copy-done
  8.3 61.4 %forward.1 = (bf16[1152,768]{1,0:T(8,128)(2,1)}, bf16[1152,256]{1,0:T(8,128)(2,1)}, f32[1152,512]{1,0:T(8,128)}, f32[1152,512]{1,0:T(8,128)}, bf16[1152,512]{1,0...) custom-call(bf16[1152,512]{1,0:T(8,128)(2,1)} %tokens.3, ...), custom_call_target="tpu_custom_call" | custom-call | tf_op jit(solution)/shard_map/forward/pallas_call | solution.py:845
  69.7 63.4 %experts.1 = (bf16[1280,256]{1,0:T(8,128)(2,1)}, bf16[1280,256]{1,0:T(8,128)(2,1)}, f32[16,128]{1,0:T(8,128)}, bf16[1280,512]{1,0:T(8,128)(2,1)}, bf16[512,1024]...) custom-call(bf16[1152,512]{1,0:T(8,128)(2,1)} %get-tuple-element.74.lowered, ...), custom_call_target="tpu_custom_call" | custom-call | tf_op jit(solution)/shard_map/experts/pallas_call | solution.py:845
  133.1 98.5 %backward.1 = (bf16[1152,512]{1,0:T(8,128)(2,1)}, f32[1152,512]{1,0:T(8,128)}, bf16[512,1024]{1,0:T(8,128)(2,1)}, bf16[1024,512]{1,0:T(8,128)(2,1)}, bf16[1536,2...) custom-call(f32[1152,512]{1,0:T(8,128)} %get-tuple-element.71.second, ...), custom_call_target="tpu_custom_call" | custom-call | tf_op jit(solution)/shard_map/backward/pallas_call | solution.py:845
  231.6 8.9 %widen.1 = (bf16[1152,512]{1,0:T(8,128)(2,1)}, f32[1152,512]{1,0:T(8,128)}, f32[512,1024]{1,0:T(8,128)}, f32[1024,512]{1,0:T(8,128)}, f32[3,512,256]{2,1,0:T(8,1...) custom-call(bf16[1152,512]{1,0:T(8,128)(2,1)} %get-tuple-element.84., ...), custom_call_target="tpu_custom_call" | custom-call | tf_op jit(solution)/shard_map/widen/pallas_call | solution.py:928
  240.5 0.7 fusion
  241.2 0.6 pad_maximum_fusion
  (4 shorter events, 0.0 us)
Async XLA Ops:
  7.2 1.1 copy-start

commit v3 on v2

--- a/solution.py
+++ b/solution.py
@@ -203,132 +203,216 @@
     return ((slot == targets[0:1, :]) | (slot == targets[1:2, :])).astype(BF16)
 
 
-def slot_targets(choice_ids, ranks, capacity, room):
-    count = choice_ids.shape[1]
-    order_keys = jnp.concatenate([ranks, ranks + count])
-    flat_ids = choice_ids.reshape(2 * count)
-    earlier = (order_keys[None, :] < order_keys[:, None]) & (flat_ids[None, :] == flat_ids[:, None])
-    position = jnp.sum(earlier.astype(jnp.int32), axis=1).reshape(2, count)
-    kept = position < capacity
-    targets = jnp.where(kept, choice_ids * room + position, -1)
-    marks = jnp.where(kept, choice_ids, -1)
-    places = jnp.where(kept, position, -1)
-    return targets, jnp.concatenate([targets, marks, places]).T
-
-
-def forward(
-    wide, room, group, heads, rows,
-    tokens, cotangent, targets, choices, pre_gain, pre_shift, weight_qkv, qv_bias, projection, proj_bias,
-    mid_gain, mid_shift, hidden, hidden_bias, output, output_bias, moe_gain, moe_shift, router,
-    qkv_out, context_out, first_out, second_out, lowered_out, route_out, gates_out, table_out, upstream_out,
-    placed, projection_peer, context_peer, partial_own, partial_peer, sems,
+def count_slots(ids, priority, experts, capacity, room):
+    tokens = ids.shape[1]
+    wide_rows = jnp.concatenate([ids, priority, jnp.zeros((5, tokens), jnp.int32)], axis=0)
+    eye = lax.broadcasted_iota(jnp.int32, (8, 8), 0) == lax.broadcasted_iota(jnp.int32, (8, 8), 1)
+    turned = dot_columns(wide_rows.astype(F32), eye.astype(F32), HIGHEST).astype(jnp.int32)
+    rank, ranks = turned[:, 2:3], priority
+
+    def fold(numbers, own, before, axis):
+        later = [jnp.where(numbers == own[0], before, 0.0), jnp.where(numbers == own[1] + experts, before, 0.0)]
+        return [jnp.sum(part, axis=axis, keepdims=True) for part in later]
+
+    def finish(own, counts, firsts):
+        counts = [counts[0], counts[1] + firsts]
+        places = [count.astype(jnp.int32) for count in counts]
+        kept = [place < capacity for place in places]
+        return (
+            [jnp.where(keep, choice * room + place, -1) for keep, choice, place in zip(kept, own, places)],
+            [jnp.where(keep, choice, -1) for keep, choice in zip(kept, own)],
+            [jnp.where(keep, place, -1) for keep, place in zip(kept, places)],
+        )
+
+    number = lax.broadcasted_iota(jnp.int32, (2 * experts, tokens), 0)
+    by_row = [ids[0:1, :], ids[1:2, :]]
+    held = ((number == by_row[0]) | (number == by_row[1] + experts)).astype(BF16)
+    before = dot(held, (rank < ranks).astype(BF16))
+    first_counts = jnp.sum(held.astype(F32), axis=1, keepdims=True)
+    firsts = jnp.sum(jnp.where(number == by_row[1], first_counts, 0.0), axis=0, keepdims=True)
+    targets, _, _ = finish(by_row, fold(number, by_row, before, 0), firsts)
+
+    number = lax.broadcasted_iota(jnp.int32, (tokens, 2 * experts), 1)
+    by_token = [turned[:, 0:1], turned[:, 1:2]]
+    held_by_token = ((number == by_token[0]) | (number == by_token[1] + experts)).astype(BF16)
+    before = dot((ranks < rank).astype(BF16), held_by_token)
+    first_counts = jnp.sum(held_by_token.astype(F32), axis=0, keepdims=True)
+    firsts = jnp.sum(jnp.where(number == by_token[1], first_counts, 0.0), axis=1, keepdims=True)
+    groups = finish(by_token, fold(number, by_token, before, 1), firsts)
+    choices = jnp.concatenate([part for group in groups for part in group], axis=1)
+    return jnp.concatenate(targets, axis=0), choices
+
+
+def front(
+    wide, room, group, heads, rows, experts,
+    tokens_h, cotangent_h, weight_qkv_h, projection_h, hidden_h, output_h, weight_in_h, weight_out_h,
+    ids, priority, pre_gain, pre_shift, qv_bias, proj_bias, mid_gain, mid_shift, hidden_bias, output_bias,
+    moe_gain, moe_shift, router, bias_in, bias_out,
+    qkv_h, context_h, first_h, second_h, info_h, result_h, in_grad_h, out_grad_h, own_home, peer_home,
+    gate_home, in_bias_grad, out_bias_grad,
+    tokens, cotangent, weight_qkv, projection, hidden, output, weight_in, weight_out,
+    qkv, context, first, second, info, result, in_grad, out_grad,
+    targets, table, raised_placed, upstream, projection_peer, context_peer, partial_own, partial_peer,
+    columns, placed, rows_own, rows_peer, act, inner_grad, slot_grad, grad_kept, grad_sent, grad_landed,
+    grad_back, gate_sent, gate_arrived, gate_back, gate_own, gate_peer,
+    sems, load_sems, chunk_sems, store_sems, group_sems,
 ):
     me, plane = lax.axis_index("wide"), lax.axis_index("tensor")
     chunks, groups = tokens.shape[0] // rows, wide // group
     mine = lax.div(me, group)
     block = group * room
     width = heads * HEAD_DIM
-    row_at, context_at, partial_at, last_at = 0, wide, wide + chunks, wide + 2 * chunks
-    greet(wide)
+    half = columns.shape[1]
+    capacity = tokens.shape[0] // experts
+    row_at, gate_at, home_at, back_at, up_at = 0, wide, 2 * wide, 3 * wide, 4 * wide
+    grad_at, share_at, join_at = 5 * wide, 5 * wide + groups, 5 * wide + 2 * groups
+    context_at = 5 * wide + 3 * groups
+    partial_at, last_at = context_at + chunks, context_at + 2 * chunks
 
     def rows_of(index):
         return pl.ds(pl.multiple_of(index * room, 16), room)
 
+    def rows_of_group(index):
+        return pl.ds(pl.multiple_of(index * block, 16), block)
+
     def chunk_of(index):
         return pl.ds(pl.multiple_of(index * rows, 16), rows)
+
+    def load_tokens(c):
+        return pltpu.make_async_copy(tokens_h.at[chunk_of(c)], tokens.at[chunk_of(c)], chunk_sems.at[c])
+
+    def start_tokens(c, carry):
+        load_tokens(c).start()
+        return carry
+
+    loads = [
+        pltpu.make_async_copy(source, target, load_sems.at[i])
+        for i, (source, target) in enumerate(
+            [(weight_qkv_h, weight_qkv), (projection_h, projection), (hidden_h, hidden), (output_h, output),
+             (cotangent_h, cotangent), (weight_in_h, weight_in), (weight_out_h, weight_out)]
+        )
+    ]
+    loads[0].start()
+    lax.fori_loop(0, chunks, start_tokens, 0)
+    for load in loads[1:]:
+        load.start()
+
+    def store(kind, source, target, c):
+        return pltpu.make_async_copy(source.at[chunk_of(c)], target.at[chunk_of(c)], store_sems.at[kind, c])
+
+    stores = [(qkv, qkv_h), (context, context_h), (first, first_h), (second, second_h), (info, info_h)]
+    greet(wide)
 
     def move(source, target, base, sent, landed, device):
         return pltpu.make_async_remote_copy(
             source, target, sems.at[0, base + sent], sems.at[1, base + landed], device_id=device, device_id_type=MESH
         )
 
-    def across(source, target, base, index):
+    def across_chunk(source, target, base, index):
         there = chunk_of(index)
         return move(source.at[there], target.at[there], base, index, index, (me, 1 - plane))
 
-    def row_copy(other, sender):
-        return move(placed.at[rows_of(other)], upstream_out.at[rows_of(sender)], row_at, other, sender, (other, plane))
-
-    weights = move(projection, projection_peer, last_at, 0, 0, (me, 1 - plane))
+    def up_copy(other, sender):
+        return move(raised_placed.at[rows_of(other)], upstream.at[rows_of(sender)], up_at, other, sender, (other, plane))
+
+    weights = move(projection_h, projection_peer, last_at, 0, 0, (me, 1 - plane))
     weights.start()
-    table_out[...] = jnp.zeros_like(table_out)
+    first_plane = plane == 0
+    table[...] = jnp.zeros_like(table)
+    in_bias_grad[...] = jnp.zeros_like(in_bias_grad)
+    out_bias_grad[...] = jnp.zeros_like(out_bias_grad)
 
     def attend_chunk(c):
         there = chunk_of(c)
+        load_tokens(c).wait()
         normed, _ = normalized(tokens[there, :].astype(F32))
         lowered = (normed * pre_gain[...] + pre_shift[...]).astype(BF16)
         parts = [dot(lowered, weight_qkv[s]) for s in range(3)]
         parts = [parts[0] + qv_bias[0:1, :], parts[1], parts[2] + qv_bias[1:2, :]]
-        qkv = jnp.concatenate(parts, axis=1).astype(BF16)
-        qkv_out[there, :] = qkv
+        value = jnp.concatenate(parts, axis=1).astype(BF16)
+        qkv[there, :] = value
         contexts = [
-            image_forward(heads, qkv[image * PATCHES : (image + 1) * PATCHES]) for image in range(rows // PATCHES)
+            image_forward(heads, value[image * PATCHES : (image + 1) * PATCHES]) for image in range(rows // PATCHES)
         ]
-        context_out[there, :] = jnp.concatenate(contexts, axis=0)
-        across(context_out, context_peer, context_at, c).start()
-
-    def place_group(k):
+        context[there, :] = jnp.concatenate(contexts, axis=0)
+        across_chunk(context, context_peer, context_at, c).start()
+        store(0, qkv, qkv_h, c).start()
+        store(1, context, context_h, c).start()
+
+    def find_slots():
+        by_row, choices = count_slots(ids[...], priority[...], experts, capacity, room)
+        targets[0:2, :] = by_row
+        info[:, experts : experts + 6] = choices.astype(F32)
+
+    def raise_group(k):
         q = lax.rem(mine + k, groups)
         hits = slot_hits(q * block, block, targets)
-        here = pl.ds(pl.multiple_of(q * block, 16), block)
-        placed[here, :] = dot(hits, cotangent[...].astype(BF16)).astype(BF16)
+        raised_placed[rows_of_group(q), :] = dot(hits, cotangent[...].astype(BF16)).astype(BF16)
         for j in range(group):
             e = q * group + j
 
             @pl.when(e != me)
             def _(e=e):
-                row_copy(e, me).start()
+                up_copy(e, me).start()
 
             @pl.when(e == me)
             def _(e=e):
-                upstream_out[rows_of(e), :] = placed[rows_of(e), :]
+                upstream[rows_of(e), :] = raised_placed[rows_of(e), :]
 
     def feed_chunk(c):
         there = chunk_of(c)
-        across(context_out, context_peer, context_at, c).wait()
-        branch = dot(context_out[there, :], projection[...]) + dot(context_peer[there, :], projection_peer[...])
-        first = tokens[there, :].astype(F32) + branch + proj_bias[...]
-        first_out[there, :] = first
-        normed, _ = normalized(first)
+        across_chunk(context, context_peer, context_at, c).wait()
+        branch = dot(context[there, :], projection[...]) + dot(context_peer[there, :], projection_peer[...])
+        value = tokens[there, :].astype(F32) + branch + proj_bias[...]
+        first[there, :] = value
+        normed, _ = normalized(value)
         lowered = (normed * mid_gain[...] + mid_shift[...]).astype(BF16)
         activated = gelu(dot(lowered, hidden[...]) + hidden_bias[...]).astype(BF16)
         partial_own[there, :] = dot(activated, output[...]).astype(BF16)
-        across(partial_own, partial_peer, partial_at, c).start()
+        across_chunk(partial_own, partial_peer, partial_at, c).start()
+        store(2, first, first_h, c).start()
 
     def route_chunk(c):
         there = chunk_of(c)
-        across(partial_own, partial_peer, partial_at, c).wait()
+        across_chunk(partial_own, partial_peer, partial_at, c).wait()
         partial = partial_own[there, :].astype(F32) + partial_peer[there, :].astype(F32)
-        second = first_out[there, :] + partial + output_bias[...]
-        second_out[there, :] = second
-        normed, _ = normalized(second)
+        value = first[there, :] + partial + output_bias[...]
+        second[there, :] = value
+        normed, _ = normalized(value)
         normed = normed * moe_gain[...] + moe_shift[...]
-        lowered_out[there, :] = normed.astype(BF16)
+        columns[there, :] = jnp.where(first_plane, normed[:, :half], normed[:, half:]).astype(BF16)
         logits = lax.dot_general(
             normed, router[...], (((1,), (1,)), ((), ())), precision=HIGHEST, preferred_element_type=F32
         )
         grown = jnp.exp(logits - jnp.max(logits, axis=-1, keepdims=True))
         route = grown / jnp.sum(grown, axis=-1, keepdims=True)
-        route_out[there, :] = route
+        info[there, 0:experts] = route
         number = lax.broadcasted_iota(jnp.int32, route.shape, 1)
-        picks = choices[there, :]
-        chosen = [jnp.where(number == picks[:, 2 + j : 3 + j], route, 0.0) for j in range(2)]
-        gates_out[there, :] = jnp.concatenate([jnp.sum(part, axis=1, keepdims=True) for part in chosen], axis=1)
-        for part, spot in zip(chosen, spots(picks[:, 4:6])):
-            table_out[...] += dot_columns(part, spot, HIGHEST)
+        picks = info[there, experts : experts + 6].astype(jnp.int32)
+        for j, spot in enumerate(spots(picks[:, 4:6])):
+            table[...] += dot_columns(jnp.where(number == picks[:, 2 + j : 3 + j], route, 0.0), spot, HIGHEST)
+        store(3, second, second_h, c).start()
+        store(4, info, info_h, c).start()
 
     def turn(c, carry):
         @pl.when(c < chunks)
         def _():
             attend_chunk(c)
 
+        @pl.when(c == 0)
+        def _():
+            loads[4].wait()
+            find_slots()
+
         @pl.when(c < groups)
         def _():
-            place_group(c)
+            raise_group(c)
 
         @pl.when(c == 1)
         def _():
             weights.wait()
+            for load in loads[1:4]:
+                load.wait()
 
         @pl.when((c >= 1) & (c <= chunks))
         def _():
@@ -340,43 +424,9 @@
 
         return carry
 
+    info[...] = jnp.zeros_like(info)
+    loads[0].wait()
     lax.fori_loop(0, chunks + 2, turn, 0)
-
-    def take_rows(d, carry):
-        other = lax.rem(me + d, wide)
-        row_copy(other, other).wait_recv()
-        row_copy(other, me).wait_send()
-        return carry
-
-    lax.fori_loop(1, wide, take_rows, 0)
-
-
-def experts(
-    wide, room, group,
-    lowered, targets, table, upstream, weight_in, bias_in, weight_out, bias_out,
-    own_home, peer_home, gate_home, result_out, in_grad, out_grad, in_bias_grad, out_bias_grad,
-    columns, placed, rows_own, rows_peer, act, inner_grad, slot_grad, grad_kept, grad_sent, grad_landed,
-    grad_back, gate_sent, gate_arrived, gate_back, gate_own, gate_peer, sems,
-):
-    me, plane = lax.axis_index("wide"), lax.axis_index("tensor")
-    groups = wide // group
-    mine = lax.div(me, group)
-    half = own_home.shape[1]
-    block = group * room
-    row_at, gate_at, home_at, back_at = 0, wide, 2 * wide, 3 * wide
-    grad_at, share_at, join_at, table_at = 4 * wide, 4 * wide + groups, 4 * wide + 2 * groups, 4 * wide + 3 * groups
-    greet(wide)
-
-    def rows_of(index):
-        return pl.ds(pl.multiple_of(index * room, 16), room)
-
-    def rows_of_group(index):
-        return pl.ds(pl.multiple_of(index * block, 16), block)
-
-    def move(source, target, base, sent, landed, device):
-        return pltpu.make_async_remote_copy(
-            source, target, sems.at[0, base + sent], sems.at[1, base + landed], device_id=device, device_id_type=MESH
-        )
 
     def row_copy(other, sender):
         return move(placed.at[rows_of(other)], rows_own.at[rows_of(sender)], row_at, other, sender, (other, plane))
@@ -394,14 +444,10 @@
         there = rows_of_group(index)
         return move(source.at[there], target.at[there], base, index, index, (me, 1 - plane))
 
-    first_plane = plane == 0
-    columns[...] = jnp.where(first_plane, lowered[:, :half], lowered[:, half:])
     own_half = pl.ds(pl.multiple_of(plane * half, 16), half)
     peer_half = pl.ds(pl.multiple_of((1 - plane) * half, 16), half)
     for e in range(wide):
         gate_sent[e] = jnp.broadcast_to(table[e : e + 1, :], gate_sent.shape[1:])
-    in_bias_grad[...] = jnp.zeros_like(in_bias_grad)
-    out_bias_grad[...] = jnp.zeros_like(out_bias_grad)
 
     def place_group(k, carry):
         q = lax.rem(mine + k, groups)
@@ -422,7 +468,13 @@
         return carry
 
     lax.fori_loop(0, groups, place_group, 0)
+    loads[5].wait()
+    loads[6].wait()
     diagonal = lax.broadcasted_iota(jnp.int32, (room, 128), 0) == lax.broadcasted_iota(jnp.int32, (room, 128), 1)
+
+    def store_result(p):
+        there = rows_of_group(p)
+        return pltpu.make_async_copy(result.at[there], result_h.at[there], group_sems.at[p])
 
     def join_group(p):
         for j in range(group):
@@ -434,6 +486,12 @@
                 gate_copy(w, w).wait_recv()
 
         across(rows_own, rows_peer, join_at, p).start()
+        for j in range(group):
+            w = p * group + j
+
+            @pl.when(w != me)
+            def _(w=w):
+                up_copy(w, w).wait_recv()
 
     def expert_group(p):
         there = rows_of_group(p)
@@ -457,11 +515,12 @@
         grad_sent[there, :] = dot_rows(inward, weight_in[peer_half, :]).astype(BF16)
         across(grad_sent, grad_landed, grad_at, p).start()
         grad_kept[there, :] = dot_rows(inward, weight_in[own_half, :])
-        result = dot(acted, weight_out[...]) + bias_out[...] * jnp.where(first_plane, 1.0, 0.0)
-        result_out[there, :] = result.astype(BF16)
+        value = dot(acted, weight_out[...]) + bias_out[...] * jnp.where(first_plane, 1.0, 0.0)
+        result[there, :] = value.astype(BF16)
+        store_result(p).start()
         out_bias_grad[0:1, :] += jnp.sum(slot.astype(F32), axis=0, keepdims=True)
         in_bias_grad[0:1, :] += jnp.sum(inward.astype(F32), axis=0, keepdims=True)
-        slopes = jnp.sum(raised * result, axis=1, keepdims=True)
+        slopes = jnp.sum(raised * value, axis=1, keepdims=True)
         for j in range(group):
             w = p * group + j
             row = jnp.sum(
@@ -477,6 +536,8 @@
             def _(w=w):
                 gate_own[w] = gate_back[w]
 
+    own_rows = pltpu.make_async_copy(grad_back.at[rows_of(me)], own_home.at[rows_of(me)], group_sems.at[groups])
+
     def give_back(p):
         across(grad_sent, grad_landed, grad_at, p).wait()
         there = rows_of_group(p)
@@ -490,9 +551,9 @@
 
             @pl.when(w == me)
             def _(w=w):
-                own_home[rows_of(w), :] = grad_back[rows_of(w), :]
-
-    def turn(k, carry):
+                own_rows.start()
+
+    def expert_turn(k, carry):
         @pl.when(k < groups)
         def _():
             join_group(lax.rem(mine + groups - k, groups))
@@ -507,7 +568,8 @@
 
         return carry
 
-    lax.fori_loop(0, groups + 2, turn, 0)
+    lax.fori_loop(0, groups + 2, expert_turn, 0)
+    own_rows.wait()
     tile = act.shape[1] // groups
 
     def share_group(k, carry):
@@ -525,6 +587,8 @@
         return carry
 
     lax.fori_loop(0, groups, share_group, 0)
+    out_store = pltpu.make_async_copy(out_grad, out_grad_h, load_sems.at[7])
+    out_store.start()
 
     def take_gates(d, carry):
         other = lax.rem(me + d, wide)
@@ -532,13 +596,16 @@
         return carry
 
     lax.fori_loop(1, wide, take_gates, 0)
-    tables = move(gate_own, gate_peer, table_at, 0, 0, (me, 1 - plane))
+    tables = move(gate_own, gate_peer, last_at, 1, 1, (me, 1 - plane))
     tables.start()
     in_grad[own_half, :] = dot_columns(rows_own[...], inner_grad[...]).astype(BF16)
     in_grad[peer_half, :] = dot_columns(rows_peer[...], inner_grad[...]).astype(BF16)
+    in_store = pltpu.make_async_copy(in_grad, in_grad_h, load_sems.at[8])
+    in_store.start()
 
     def end_sends(d, carry):
         other = lax.rem(me + d, wide)
+        up_copy(other, me).wait_send()
         row_copy(other, me).wait_send()
         gate_copy(other, me).wait_send()
         home_copy(other, me).wait_send()
@@ -546,25 +613,38 @@
         return carry
 
     lax.fori_loop(1, wide, end_sends, 0)
+
+    def end_stores(c, carry):
+        for kind, (source, target) in enumerate(stores):
+            store(kind, source, target, c).wait()
+        return carry
+
+    lax.fori_loop(0, chunks, end_stores, 0)
     tables.wait()
     for e in range(wide):
         gate_home[e : e + 1, :] = gate_own[e][0:1, :] + gate_peer[e][0:1, :]
 
-    def end_share(q, carry):
+    def end_groups(q, carry):
+        store_result(q).wait()
         across(own_home, peer_home, share_at, q).wait()
         return carry
 
-    lax.fori_loop(0, groups, end_share, 0)
+    lax.fori_loop(0, groups, end_groups, 0)
+    out_store.wait()
+    in_store.wait()
 
 
 def backward(
     wide, room, heads, layout, orders, rows,
-    second, cotangent, route, choices, gates, moe_gain, moe_shift, router, gate_grads, row_own, row_peer, result,
-    first, tokens, qkv, context, mid_gain, mid_shift, pre_gain, pre_shift, hidden, hidden_bias, output, projection,
-    weight_qkv,
-    block_out, grad_out, hidden_out, output_out, qkv_out, proj_out, *rest,
+    second_h, cotangent_h, info_h, first_h, tokens_h, qkv_h, context_h, hidden_h, output_h, projection_h, weight_qkv_h,
+    row_own_h, row_peer_h, result,
+    moe_gain, moe_shift, router, gate_grads, mid_gain, mid_shift, pre_gain, pre_shift, hidden_bias,
+    block_h, grad_h, hidden_out_h, output_out_h, qkv_out_h, proj_out_h, *rest,
 ):
     vectors_out, pre_out, rest = rest[: len(layout)], rest[len(layout)], rest[len(layout) + 1 :]
+    (second, cotangent, info, first, tokens, qkv, context, hidden, output, projection, weight_qkv, row_own, row_peer,
+     block_out, grad_out, hidden_out, output_out, qkv_out, proj_out), rest = rest[:19], rest[19:]
+    load_sems, chunk_sems, store_sems, rest = rest[-3], rest[-2], rest[-1], rest[:-3]
     (lowered_mid, act, inner_grad, mid_own, mid_peer, branch, qkv_grad, lowered_pre, pre_peer, result_own, blend_peer,
      pre_tile, pre_tiles, pre_total, pre_other, moe_sums, router_sums, mid_sums, hidden_sums, qkv_sums, pre_sums, small_sums) = rest[:22]
     hidden_total, output_total, qkv_total, proj_total, small = rest[22:27]
@@ -582,6 +662,52 @@
     gathers = (
         hidden_out, output_out, qkv_out.at[pl.ds(0, split)], qkv_out.at[pl.ds(split, split)], proj_out, small_sums
     )
+
+    def chunk_of(index):
+        return pl.ds(pl.multiple_of(index * rows, 16), rows)
+
+    early = [(info_h, info), (second_h, second), (cotangent_h, cotangent), (first_h, first)]
+    late = [(tokens_h, tokens), (qkv_h, qkv)]
+
+    def load(kind, pair, c):
+        return pltpu.make_async_copy(pair[0].at[chunk_of(c)], pair[1].at[chunk_of(c)], chunk_sems.at[kind, c])
+
+    def start_early(c, carry):
+        for kind, pair in enumerate(early):
+            load(kind, pair, c).start()
+        return carry
+
+    def start_late(c, carry):
+        for kind, pair in enumerate(late):
+            load(len(early) + kind, pair, c).start()
+        return carry
+
+    loads = [
+        pltpu.make_async_copy(source, target, load_sems.at[i])
+        for i, (source, target) in enumerate(
+            [(row_own_h, row_own), (row_peer_h, row_peer), (hidden_h, hidden), (output_h, output),
+             (projection_h, projection), (weight_qkv_h, weight_qkv), (context_h, context)]
+        )
+    ]
+    for part in loads[:2]:
+        part.start()
+    start_early(0, 0)
+    for part in loads[2:4]:
+        part.start()
+    lax.fori_loop(1, chunks, start_early, 0)
+    for part in loads[4:]:
+        part.start()
+    lax.fori_loop(0, chunks, start_late, 0)
+    whole_stores = [
+        pltpu.make_async_copy(source, target, load_sems.at[len(loads) + i])
+        for i, (source, target) in enumerate(
+            [(hidden_out, hidden_out_h), (output_out, output_out_h), (qkv_out, qkv_out_h), (proj_out, proj_out_h)]
+        )
+    ]
+
+    def store(kind, source, target, c):
+        return pltpu.make_async_copy(source.at[chunk_of(c)], target.at[chunk_of(c)], store_sems.at[kind, c])
+
     greet(wide)
     sums = Sums(wide, orders, totals, sends, lands, gathers, send_sems, recv_sems)
 
@@ -599,7 +725,10 @@
         return carry
 
     lax.fori_loop(1, wide, send_result, 0)
-    result_own[rows_of(me), :] = result[rows_of(me), :]
+    own_rows = pltpu.make_async_copy(
+        result.at[rows_of(me)], result_own.at[rows_of(me)], load_sems.at[len(loads) + len(whole_stores)]
+    )
+    own_rows.start()
 
     def across(own, peer, sems, chunk):
         at = pl.multiple_of(chunk * rows, rows)
@@ -616,11 +745,12 @@
         return jnp.concatenate([jnp.where(first_plane, own, peer), jnp.where(first_plane, peer, own)], axis=1)
 
     def settle(here):
-        picks = choices[here, :]
+        experts = router.shape[0]
+        picks = info[here, experts : experts + 6].astype(jnp.int32)
         hits = token_hits(picks, row_own.shape[0])
         table = (hits[0] | hits[1]).astype(BF16)
         moe_grad = ordered(dot(table, row_own[...]), dot(table, row_peer[...]))
-        chances = route[here, :]
+        chances = info[here, 0:experts]
         number = lax.broadcasted_iota(jnp.int32, chances.shape, 1)
         route_grad = jnp.zeros_like(chances)
         for j, spot in enumerate(spots(picks[:, 4:6])):
@@ -640,8 +770,16 @@
         moe_sums[2:3, :] += jnp.sum(grad, axis=0, keepdims=True)
 
     def feed_chunk(chunk, carry):
-        here = pl.ds(pl.multiple_of(chunk * rows, rows), rows)
+        here = chunk_of(chunk)
+        for kind, pair in enumerate(early):
+            load(kind, pair, chunk).wait()
         settle(here)
+
+        @pl.when(chunk == 0)
+        def _():
+            loads[2].wait()
+            loads[3].wait()
+
         normed, _ = normalized(first[here, :])
         lowered = (normed * mid_gain[...] + mid_shift[...]).astype(BF16)
         lowered_mid[here, :] = lowered
@@ -654,6 +792,8 @@
         across(mid_own, mid_peer, mid_sems, chunk).start()
         return carry
 
+    loads[0].wait()
+    loads[1].wait()
     lax.fori_loop(0, chunks, feed_chunk, 0)
 
     def put_in(total):
@@ -669,6 +809,8 @@
 
     def attend_chunk(chunk, carry):
         here = pl.ds(pl.multiple_of(chunk * rows, rows), rows)
+        for kind, pair in enumerate(late):
+            load(len(early) + kind, pair, chunk).wait()
         across(mid_own, mid_peer, mid_sems, chunk).wait()
         mid_grad = mid_own[here, :].astype(F32) + mid_peer[here, :].astype(F32)
         normed, scale = normalized(first[here, :])
@@ -704,7 +846,10 @@
         across(mid_own, pre_peer, pre_sems, chunk).start()
         return carry
 
+    loads[4].wait()
+    loads[5].wait()
     lax.fori_loop(0, chunks, attend_chunk, 0)
+    loads[6].wait()
 
     small[...] = jnp.zeros_like(small)
     at = 0
@@ -744,6 +889,7 @@
         upstream = mid_own[here, :].astype(F32) + pre_peer[here, :].astype(F32)
         normed, scale = normalized(tokens[here, :].astype(F32))
         grad_out[here, :] += norm_back(normed, scale, pre_gain[...], upstream)
+        store(0, grad_out, grad_h, chunk).start()
         return carry
 
     def take_result(d, carry):
@@ -753,11 +899,19 @@
         return carry
 
     lax.fori_loop(1, wide, take_result, 0)
+    own_rows.wait()
 
     def blend(chunk, carry):
         here = pl.ds(pl.multiple_of(chunk * rows, rows), rows)
-        hits = token_hits(choices[here, :], result_own.shape[0])
-        table = jnp.where(hits[0], gates[here, 0:1], jnp.where(hits[1], gates[here, 1:2], 0.0)).astype(BF16)
+        experts = router.shape[0]
+        picks, chances = info[here, experts : experts + 6].astype(jnp.int32), info[here, 0:experts]
+        number = lax.broadcasted_iota(jnp.int32, chances.shape, 1)
+        gates = [
+            jnp.sum(jnp.where(number == picks[:, 2 + j : 3 + j], chances, 0.0), axis=1, keepdims=True)
+            for j in range(2)
+        ]
+        hits = token_hits(picks, result_own.shape[0])
+        table = jnp.where(hits[0], gates[0], jnp.where(hits[1], gates[1], 0.0)).astype(BF16)
         blend_own[here, :] = dot(table, result_own[...]).astype(BF16)
         across(blend_own, blend_peer, blend_sems, chunk).start()
         return carry
@@ -767,6 +921,7 @@
         across(blend_own, blend_peer, blend_sems, chunk).wait()
         mixture = blend_own[here, :].astype(F32) + blend_peer[here, :].astype(F32)
         block_out[here, :] = (second[here, :] + mixture).astype(BF16)
+        store(1, block_out, block_h, chunk).start()
         return carry
 
     def take_pre(d, carry):
@@ -792,9 +947,13 @@
             first_chunk = (k - sums.steps) * chunks // sums.steps
             lax.fori_loop(first_chunk, (k - sums.steps + 1) * chunks // sums.steps, blend_end, 0)
         if k == sums.steps - 1:
+            for part in whole_stores[:2]:
+                part.start()
             lax.fori_loop(1, wide, take_pre, 0)
             pre_total[...] = sum(pre_tiles[w] for w in range(wide))
             pre_share.start()
+    for part in whole_stores[2:]:
+        part.start()
     pre_share.wait()
     pre_tile[...] = pre_total[...] + pre_other[...]
     pre_out[0:1, :] = get_row(pre_tile, 0, model)
@@ -804,6 +963,15 @@
         for i in range(len(picked)):
             out[i : i + 1, :] = get_row(small_sums, at, out.shape[1]).astype(F32)
             at += out.shape[1] // 128
+
+    def end_stores(c, carry):
+        store(0, grad_out, grad_h, c).wait()
+        store(1, block_out, block_h, c).wait()
+        return carry
+
+    lax.fori_loop(0, chunks, end_stores, 0)
+    for part in whole_stores:
+        part.wait()
 
 
 def widen(pairs, layout, *refs):
@@ -841,18 +1009,19 @@
     def row(vector):
         return vector.reshape(1, -1)
 
-    def remote(kernel, name, identity, ins, outs, scratch):
+    def remote(kernel, name, identity, far_ins, ins, far_outs, outs, scratch):
+        far, near = pl.BlockSpec(memory_space=pl.ANY), pl.BlockSpec(memory_space=pltpu.VMEM)
         return pl.pallas_call(
             kernel,
-            out_shape=[jax.ShapeDtypeStruct(shape, dtype) for shape, dtype in outs],
-            in_specs=[pl.BlockSpec(memory_space=pltpu.VMEM)] * len(ins),
-            out_specs=[pl.BlockSpec(memory_space=pltpu.VMEM)] * len(outs),
+            out_shape=[jax.ShapeDtypeStruct(shape, dtype) for shape, dtype in far_outs + outs],
+            in_specs=[far] * len(far_ins) + [near] * len(ins),
+            out_specs=[far] * len(far_outs) + [near] * len(outs),
             scratch_shapes=scratch,
             compiler_params=pltpu.CompilerParams(
                 vmem_limit_bytes=VMEM_BYTES, collective_id=identity, has_side_effects=True
             ),
             name=name,
-        )(*ins)
+        )(*far_ins, *ins)
 
     def room_for(local):
         return [pltpu.VMEM(shape, dtype) for shape, dtype in local]
@@ -862,50 +1031,57 @@
     output_bias, moe_gain, moe_shift = row(output_bias), row(moe_gain), row(moe_shift)
     weight_qkv = qkv_weight.transpose(1, 0, 2)
     router = router_weight.T
-    targets, choices = slot_targets(expert_ids.T, priority[0], capacity, room)
-
-    qkv, context, first, second, lowered, route, gates, table, upstream = remote(
-        functools.partial(forward, wide, room, group, heads, rows), "forward", 1,
-        [tokens_in, cotangent, targets, choices, pre_gain, pre_shift, weight_qkv, qv_bias, proj_weight, proj_bias,
-         mid_gain, mid_shift, hidden_weight, hidden_bias, output_weight, output_bias, moe_gain, moe_shift, router],
-        [((tokens, lanes), BF16), ((tokens, width), BF16), ((tokens, model), F32), ((tokens, model), F32),
-         ((tokens, model), BF16), ((tokens, count), F32), ((tokens, 2), F32), ((count, 128), F32), ((slots, model), BF16)],
-        room_for([((slots, model), BF16), ((width, model), BF16), ((tokens, width), BF16), ((tokens, model), BF16),
-                  ((tokens, model), BF16)]) + [pltpu.SemaphoreType.DMA((2, wide + 2 * chunks + 1))],
-    )
-
+    groups = wide // group
+    kept = [
+        ((tokens, lanes), BF16), ((tokens, width), BF16), ((tokens, model), F32), ((tokens, model), F32),
+        ((tokens, 128), F32), ((slots, model), BF16), ((model, hidden), BF16), ((hidden, model), BF16),
+    ]
+    homes = [((slots, half), BF16), ((slots, half), BF16)]
+    fetched = [tokens_in, cotangent, weight_qkv, proj_weight, hidden_weight, output_weight, expert_in[0], expert_out[0]]
     tables = [((count, 8, 128), F32)] * 5
-    row_own, row_peer, gate_grads, result, in_grad, out_grad, in_bias, out_bias = remote(
-        functools.partial(experts, wide, room, group), "experts", 2,
-        [lowered, targets, table, upstream, expert_in[0], expert_in_bias, expert_out[0], expert_out_bias],
-        [((slots, half), BF16), ((slots, half), BF16), ((count, 128), F32), ((slots, model), BF16),
-         ((model, hidden), BF16), ((hidden, model), BF16), ((8, hidden), F32), ((8, model), F32)],
-        room_for([((tokens, half), BF16), ((slots, half), BF16), ((slots, half), BF16), ((slots, half), BF16),
-                  ((slots, hidden), BF16), ((slots, hidden), BF16), ((slots, model), BF16), ((slots, half), F32),
-                  ((slots, half), BF16), ((slots, half), BF16), ((slots, half), BF16)] + tables)
-        + [pltpu.SemaphoreType.DMA((2, 4 * wide + 3 * (wide // group) + 1))],
+    qkv, context, first, second, info, result, in_grad, out_grad, row_own, row_peer, gate_grads, in_bias, out_bias = remote(
+        functools.partial(front, wide, room, group, heads, rows, count), "front", 1,
+        fetched,
+        [expert_ids.T, priority, pre_gain, pre_shift, qv_bias, proj_bias, mid_gain, mid_shift, hidden_bias, output_bias,
+         moe_gain, moe_shift, router, expert_in_bias, expert_out_bias],
+        kept + homes,
+        [((count, 128), F32), ((8, hidden), F32), ((8, model), F32)],
+        room_for([(array.shape, array.dtype) for array in fetched] + kept
+                 + [((8, tokens), jnp.int32), ((count, 128), F32), ((slots, model), BF16), ((slots, model), BF16),
+                    ((width, model), BF16), ((tokens, width), BF16), ((tokens, model), BF16), ((tokens, model), BF16),
+                    ((tokens, half), BF16), ((slots, half), BF16), ((slots, half), BF16), ((slots, half), BF16),
+                    ((slots, hidden), BF16), ((slots, hidden), BF16), ((slots, model), BF16), ((slots, half), F32),
+                    ((slots, half), BF16), ((slots, half), BF16), ((slots, half), BF16)] + tables)
+        + [pltpu.SemaphoreType.DMA((2, 5 * wide + 3 * groups + 2 * chunks + 2)), pltpu.SemaphoreType.DMA((9,)),
+           pltpu.SemaphoreType.DMA((chunks,)), pltpu.SemaphoreType.DMA((5, chunks)), pltpu.SemaphoreType.DMA((groups + 1,))],
     )
 
     layout = [(0, 1, 2), (0, 1, 2), (0,), (0,), tuple(range(count))]
     vectors = [((8, model), F32), ((8, model), F32), ((8, hidden), F32), ((8, lanes), F32), ((count, model), F32)]
     near, far = tuple(range(steps)), (0,) + tuple(range(2, steps)) + (1,)
     summed = [(model, hidden), (hidden, model), (3 * model // 2, width), (3 * model // 2, width), (width, model), (16 * wide, 128)]
+    fetched = [second, cotangent, info, first, tokens_in, qkv, context, hidden_weight, output_weight, proj_weight, weight_qkv, row_own, row_peer]
+    given = [
+        ((tokens, model), BF16), ((tokens, model), F32), ((model, hidden), BF16), ((hidden, model), BF16),
+        ((3 * model, width), BF16), ((width, model), BF16),
+    ]
+    tile = (2 * model // 128, 128)
     block_out, grad, hidden_g, output_g, qkv_g, proj_g, *sums = remote(
-        functools.partial(backward, wide, room, heads, layout, (near, far, near, far, near, far), rows), "backward", 3,
-        [second, cotangent, route, choices, gates, moe_gain, moe_shift, router, gate_grads, row_own, row_peer, result,
-         first, tokens_in, qkv, context, mid_gain, mid_shift, pre_gain, pre_shift, hidden_weight, hidden_bias,
-         output_weight, proj_weight, weight_qkv],
-        [((tokens, model), BF16), ((tokens, model), F32), ((model, hidden), BF16), ((hidden, model), BF16),
-         ((3 * model, width), BF16), ((width, model), BF16)] + vectors + [((8, model), F32)],
-        room_for([((tokens, model), BF16), ((tokens, hidden), BF16), ((tokens, hidden), BF16), ((tokens, model), BF16),
-                  ((tokens, model), BF16), ((tokens, model), BF16), ((tokens, lanes), BF16), ((tokens, model), BF16),
-                  ((tokens, model), BF16), ((slots, model), BF16), ((tokens, model), BF16),
-                  ((2 * model // 128, 128), F32), ((wide, 2 * model // 128, 128), F32), ((2 * model // 128, 128), F32),
-                  ((2 * model // 128, 128), F32), ((8, model), F32), ((count, model), F32), ((8, model), F32), ((8, hidden), F32), ((8, lanes), F32), ((8, model), F32),
-                  (summed[-1], BF16), (summed[0], F32), (summed[1], F32), ((3 * model, width), F32), (summed[4], F32),
-                  (summed[5], F32)] + [(shape, BF16) for shape in summed] * 2)
+        functools.partial(backward, wide, room, heads, layout, (near, far, near, far, near, far), rows), "backward", 2,
+        fetched + [result],
+        [moe_gain, moe_shift, router, gate_grads, mid_gain, mid_shift, pre_gain, pre_shift, hidden_bias],
+        given, vectors + [((8, model), F32)],
+        room_for([(array.shape, array.dtype) for array in fetched] + given
+                 + [((tokens, model), BF16), ((tokens, hidden), BF16), ((tokens, hidden), BF16), ((tokens, model), BF16),
+                    ((tokens, model), BF16), ((tokens, model), BF16), ((tokens, lanes), BF16), ((tokens, model), BF16),
+                    ((tokens, model), BF16), ((slots, model), BF16), ((tokens, model), BF16),
+                    (tile, F32), ((wide,) + tile, F32), (tile, F32), (tile, F32), ((8, model), F32), ((count, model), F32),
+                    ((8, model), F32), ((8, hidden), F32), ((8, lanes), F32), ((8, model), F32), (summed[-1], BF16),
+                    (summed[0], F32), (summed[1], F32), ((3 * model, width), F32), (summed[4], F32), (summed[5], F32)]
+                 + [(shape, BF16) for shape in summed] * 2)
         + [pltpu.SemaphoreType.DMA((2, chunks))] * 3 + [pltpu.SemaphoreType.DMA((2, 2 * wide + 1))]
-        + [pltpu.SemaphoreType.DMA((len(summed), 2 * steps))] * 2,
+        + [pltpu.SemaphoreType.DMA((len(summed), 2 * steps))] * 2
+        + [pltpu.SemaphoreType.DMA((12,)), pltpu.SemaphoreType.DMA((6, chunks)), pltpu.SemaphoreType.DMA((2, chunks))],
     )
 
     pairs = [

time: 242 us -> 220 us (0.909)
  Pallas kernels: 232 us -> 218 us
  other arithmetic: 6.43 us -> 0.59 us
    pallas_call x3 -> x2, Pallas kernels: 223 us -> 209 us  [remote(): pl.pallas_call(kernel, out_shape=[jax.ShapeDtypeStruct(shape, dtype) for...]
    reduce_sum x1 -> x0, other arithmetic: 4.38 us -> none  [slot_targets(): position = jnp.sum(earlier.astype(jnp.int32), axis=1).reshape(2, count)]
where the time goes in v3:
time: 220 us; the launch traced here: 219 us
  Pallas kernels  218 us (99%)
    pallas_call x2, Pallas kernels, remote(): pl.pallas_call(kernel, out_shape=[jax.ShapeDtypeStruct(shape, dtype) for...  209 us
    pallas_call x1, Pallas kernels, shards(): pl.pallas_call(functools.partial(widen, len(pairs), singles), grid=(parts...  8.87 us

profile of v3, /device:TPU:0, one launch (start us, length us, event | category | flops | bytes accessed | tf_op | source)
XLA Modules:
  0.0 219.4 jit_solution(7953827103598950623)
XLA Ops:
  0.7 114.3 %front.1 = (bf16[1152,768]{1,0:T(8,128)(2,1)}, bf16[1152,256]{1,0:T(8,128)(2,1)}, f32[1152,512]{1,0:T(8,128)}, f32[1152,512]{1,0:T(8,128)}, f32[1152,128]{1,0:T(...) custom-call(bf16[1152,512]{1,0:T(8,128)(2,1)} %tokens_h.3, ...), custom_call_target="tpu_custom_call" | custom-call | tf_op jit(solution)/shard_map/front/pallas_call | solution.py:1014
  115.0 94.3 %backward.1 = (bf16[1152,512]{1,0:T(8,128)(2,1)}, f32[1152,512]{1,0:T(8,128)}, bf16[512,1024]{1,0:T(8,128)(2,1)}, bf16[1024,512]{1,0:T(8,128)(2,1)}, bf16[1536,2...) custom-call(f32[1152,512]{1,0:T(8,128)} %get-tuple-element.67.second, ...), custom_call_target="tpu_custom_call" | custom-call | tf_op jit(solution)/shard_map/backward/pallas_call | solution.py:1014
  209.3 8.9 %widen.1 = (bf16[1152,512]{1,0:T(8,128)(2,1)}, f32[1152,512]{1,0:T(8,128)}, f32[512,1024]{1,0:T(8,128)}, f32[1024,512]{1,0:T(8,128)}, f32[3,512,256]{2,1,0:T(8,1...) custom-call(bf16[1152,512]{1,0:T(8,128)(2,1)} %get-tuple-element.76., ...), custom_call_target="tpu_custom_call" | custom-call | tf_op jit(solution)/shard_map/widen/pallas_call | solution.py:1104
  218.2 0.7 fusion
  218.9 0.6 pad_maximum_fusion

commit v4 on v3

--- a/solution.py
+++ b/solution.py
@@ -162,13 +162,15 @@
         keys = qkv[:, width + h : width + h + HEAD_DIM]
         values = qkv[:, 2 * width + h : 2 * width + h + HEAD_DIM]
         upstream = context_grad[:, h : h + HEAD_DIM]
-        probs = softmax_rows(dot_rows(query, keys), scale)
-        prob_grad = dot_rows(upstream, values)
-        inward = jnp.sum(probs * prob_grad, axis=-1, keepdims=True)
+        scores = dot_rows(keys, query)
+        weights = jnp.exp((scores - jnp.max(scores, axis=0, keepdims=True)) * scale)
+        probs = weights * (1.0 / jnp.sum(weights, axis=0, keepdims=True))
+        prob_grad = dot_rows(values, upstream)
+        inward = jnp.sum(probs * prob_grad, axis=0, keepdims=True)
         score_grad = (probs * (prob_grad - inward)).astype(BF16)
-        parts[0].append(dot(score_grad, keys) * scale)
-        parts[1].append(dot_columns(score_grad, query) * scale)
-        parts[2].append(dot_columns(probs.astype(BF16), upstream))
+        parts[0].append(dot_columns(score_grad, keys) * scale)
+        parts[1].append(dot(score_grad, query) * scale)
+        parts[2].append(dot(probs.astype(BF16), upstream))
     return jnp.concatenate(parts[0] + parts[1] + parts[2], axis=1).astype(BF16)
 
 
@@ -253,7 +255,7 @@
     tokens, cotangent, weight_qkv, projection, hidden, output, weight_in, weight_out,
     qkv, context, first, second, info, result, in_grad, out_grad,
     targets, table, raised_placed, upstream, projection_peer, context_peer, partial_own, partial_peer,
-    columns, placed, rows_own, rows_peer, act, inner_grad, slot_grad, grad_kept, grad_sent, grad_landed,
+    columns, other_columns, placed, other_placed, rows_own, rows_peer, act, inner_grad, slot_grad, grad_kept, grad_sent, grad_landed,
     grad_back, gate_sent, gate_arrived, gate_back, gate_own, gate_peer,
     sems, load_sems, chunk_sems, store_sems, group_sems,
 ):
@@ -268,6 +270,7 @@
     grad_at, share_at, join_at = 5 * wide, 5 * wide + groups, 5 * wide + 2 * groups
     context_at = 5 * wide + 3 * groups
     partial_at, last_at = context_at + chunks, context_at + 2 * chunks
+    other_at = last_at + 2
 
     def rows_of(index):
         return pl.ds(pl.multiple_of(index * room, 16), room)
@@ -381,6 +384,7 @@
         normed, _ = normalized(value)
         normed = normed * moe_gain[...] + moe_shift[...]
         columns[there, :] = jnp.where(first_plane, normed[:, :half], normed[:, half:]).astype(BF16)
+        other_columns[there, :] = jnp.where(first_plane, normed[:, half:], normed[:, :half]).astype(BF16)
         logits = lax.dot_general(
             normed, router[...], (((1,), (1,)), ((), ())), precision=HIGHEST, preferred_element_type=F32
         )
@@ -431,6 +435,14 @@
     def row_copy(other, sender):
         return move(placed.at[rows_of(other)], rows_own.at[rows_of(sender)], row_at, other, sender, (other, plane))
 
+    def other_copy(other, sender):
+        return move(other_placed.at[rows_of(other)], rows_peer.at[rows_of(sender)], other_at, other, sender, (other, plane))
+
+    def turned(k, sign):
+        pairs = groups // 2
+        pair = lax.rem(lax.div(mine, 2) + sign * lax.div(k, 2) + pairs, pairs)
+        return 2 * pair + lax.rem(mine + k, 2), k < 2
+
     def gate_copy(other, sender):
         return move(gate_sent.at[other], gate_arrived.at[sender], gate_at, other, sender, (other, plane))
 
@@ -450,8 +462,14 @@
         gate_sent[e] = jnp.broadcast_to(table[e : e + 1, :], gate_sent.shape[1:])
 
     def place_group(k, carry):
-        q = lax.rem(mine + k, groups)
-        placed[rows_of_group(q), :] = dot(slot_hits(q * block, block, targets), columns[...]).astype(BF16)
+        q, near = turned(k, 1)
+        hits = slot_hits(q * block, block, targets)
+        placed[rows_of_group(q), :] = dot(hits, columns[...]).astype(BF16)
+
+        @pl.when(near)
+        def _():
+            other_placed[rows_of_group(q), :] = dot(hits, other_columns[...]).astype(BF16)
+
         for j in range(group):
             e = q * group + j
 
@@ -460,9 +478,14 @@
                 row_copy(e, me).start()
                 gate_copy(e, me).start()
 
+            @pl.when((e != me) & near)
+            def _(e=e):
+                other_copy(e, me).start()
+
             @pl.when(e == me)
             def _(e=e):
                 rows_own[rows_of(e), :] = placed[rows_of(e), :]
+                rows_peer[rows_of(e), :] = other_placed[rows_of(e), :]
                 gate_arrived[e] = gate_sent[e]
 
         return carry
@@ -476,7 +499,8 @@
         there = rows_of_group(p)
         return pltpu.make_async_copy(result.at[there], result_h.at[there], group_sems.at[p])
 
-    def join_group(p):
+    def join_group(k):
+        p, near = turned(k, -1)
         for j in range(group):
             w = p * group + j
 
@@ -485,17 +509,29 @@
                 row_copy(w, w).wait_recv()
                 gate_copy(w, w).wait_recv()
 
-        across(rows_own, rows_peer, join_at, p).start()
+        @pl.when(jnp.logical_not(near))
+        def _():
+            across(rows_own, rows_peer, join_at, p).start()
+
         for j in range(group):
             w = p * group + j
+
+            @pl.when((w != me) & near)
+            def _(w=w):
+                other_copy(w, w).wait_recv()
 
             @pl.when(w != me)
             def _(w=w):
                 up_copy(w, w).wait_recv()
 
-    def expert_group(p):
+    def expert_group(k):
+        p, near = turned(k, -1)
         there = rows_of_group(p)
-        across(rows_own, rows_peer, join_at, p).wait()
+
+        @pl.when(jnp.logical_not(near))
+        def _():
+            across(rows_own, rows_peer, join_at, p).wait()
+
         gates = jnp.concatenate(
             [
                 jnp.sum(jnp.where(diagonal, gate_arrived[p * group + j][0:1, :], 0.0), axis=1, keepdims=True)
@@ -538,7 +574,8 @@
 
     own_rows = pltpu.make_async_copy(grad_back.at[rows_of(me)], own_home.at[rows_of(me)], group_sems.at[groups])
 
-    def give_back(p):
+    def give_back(k):
+        p, _ = turned(k, -1)
         across(grad_sent, grad_landed, grad_at, p).wait()
         there = rows_of_group(p)
         grad_back[there, :] = (grad_kept[there, :] + grad_landed[there, :].astype(F32)).astype(BF16)
@@ -553,18 +590,26 @@
             def _(w=w):
                 own_rows.start()
 
-    def expert_turn(k, carry):
-        @pl.when(k < groups)
+    def expert_turn(s, carry):
+        @pl.when(s < groups)
         def _():
-            join_group(lax.rem(mine + groups - k, groups))
-
-        @pl.when((k >= 1) & (k <= groups))
+            join_group(s)
+
+        @pl.when(s < 2)
         def _():
-            expert_group(lax.rem(mine + groups - k + 1, groups))
-
-        @pl.when(k >= 2)
+            expert_group(s)
+
+        @pl.when((s >= 3) & (s <= groups))
         def _():
-            give_back(lax.rem(mine + groups - k + 2, groups))
+            expert_group(s - 1)
+
+        @pl.when((s >= 1) & (s <= 2))
+        def _():
+            give_back(s - 1)
+
+        @pl.when(s >= 4)
+        def _():
+            give_back(s - 2)
 
         return carry
 
@@ -575,7 +620,7 @@
     def share_group(k, carry):
         at = pl.multiple_of(k * tile, 128)
         out_grad[pl.ds(at, tile), :] = dot_columns(act[:, pl.ds(at, tile)], slot_grad[...]).astype(BF16)
-        q = lax.rem(mine + k, groups)
+        q, _ = turned(k, 1)
         for j in range(group):
             e = q * group + j
 
@@ -613,6 +658,19 @@
         return carry
 
     lax.fori_loop(1, wide, end_sends, 0)
+
+    def end_others(k, carry):
+        q, _ = turned(k, 1)
+        for j in range(group):
+            e = q * group + j
+
+            @pl.when(e != me)
+            def _(e=e):
+                other_copy(e, me).wait_send()
+
+        return carry
+
+    lax.fori_loop(0, 2, end_others, 0)
 
     def end_stores(c, carry):
         for kind, (source, target) in enumerate(stores):
@@ -754,14 +812,13 @@
         number = lax.broadcasted_iota(jnp.int32, chances.shape, 1)
         route_grad = jnp.zeros_like(chances)
         for j, spot in enumerate(spots(picks[:, 4:6])):
-            at_place = lax.dot_general(
-                spot, gate_grads[...], (((1,), (1,)), ((), ())), precision=HIGHEST, preferred_element_type=F32
-            )
+            at_place = dot_rows(spot.astype(BF16), gate_grads[...].astype(BF16))
             route_grad = route_grad + jnp.where(number == picks[:, 2 + j : 3 + j], at_place, 0.0)
         logit_grad = chances * (route_grad - jnp.sum(chances * route_grad, axis=1, keepdims=True))
         normed, scale = normalized(second[here, :])
-        router_sums[...] += dot_columns(logit_grad, normed * moe_gain[...] + moe_shift[...], HIGHEST)
-        moe_grad = moe_grad + jnp.dot(logit_grad, router[...], precision=HIGHEST, preferred_element_type=F32)
+        logit_grad = logit_grad.astype(BF16)
+        router_sums[...] += dot_columns(logit_grad, (normed * moe_gain[...] + moe_shift[...]).astype(BF16))
+        moe_grad = moe_grad + dot(logit_grad, router[...].astype(BF16))
         grad = cotangent[here, :] + norm_back(normed, scale, moe_gain[...], moe_grad)
         grad_out[here, :] = grad
         branch[here, :] = grad.astype(BF16)
@@ -806,6 +863,9 @@
     sums.begin(0, 0)
     column_dots(act, branch, put_in(output_total))
     sums.begin(1, 0)
+
+    images = rows // PATCHES
+    taken = ((3, 7), (3, 7))
 
     def attend_chunk(chunk, carry):
         here = pl.ds(pl.multiple_of(chunk * rows, rows), rows)
@@ -836,12 +896,13 @@
             pre_sums[0:1, :] += jnp.sum(pre * normed[image * PATCHES : (image + 1) * PATCHES], axis=0, keepdims=True)
             pre_sums[1:2, :] += jnp.sum(pre, axis=0, keepdims=True)
             qkv_sums[0:1, :] += jnp.sum(grad.astype(F32), axis=0, keepdims=True)
-            for k in range(sums.steps):
-
-                @pl.when(chunk == k)
-                def _(i=image, k=k):
-                    if i < 2:
-                        sums.advance(i, k)
+            for i, steps in enumerate(taken):
+                for k, boundary in enumerate(steps):
+                    if boundary % images == image:
+
+                        @pl.when(chunk == boundary // images)
+                        def _(i=i, k=k):
+                            sums.advance(i, k)
 
         across(mid_own, pre_peer, pre_sems, chunk).start()
         return carry
@@ -851,37 +912,37 @@
     lax.fori_loop(0, chunks, attend_chunk, 0)
     loads[6].wait()
 
+    put_row(pre_tile, put_row(pre_tile, 0, pre_sums[0:1, :]), pre_sums[1:2, :])
+
+    def pre_copy(other, sender):
+        return pltpu.make_async_remote_copy(
+            pre_tile, pre_tiles.at[sender], result_sems.at[0, wide + other], result_sems.at[1, wide + sender],
+            device_id=(other, plane), device_id_type=MESH,
+        )
+
+    def send_pre(d, carry):
+        pre_copy(lax.rem(me + d, wide), me).start()
+        return carry
+
+    lax.fori_loop(1, wide, send_pre, 0)
+    pre_tiles[me] = pre_tile[...]
+
+    def put_thirds(at, tile, value):
+        for s in range(3):
+            there = pl.ds(pl.multiple_of(s * model + at, 16), tile)
+            qkv_total[there, :] = value[:, s * width : (s + 1) * width]
+
+    column_dots(lowered_pre, qkv_grad, put_thirds)
+    sums.begin(2, 0)
+    sums.begin(3, 0)
+    column_dots(context, branch, put_in(proj_total))
+    sums.begin(4, 0)
     small[...] = jnp.zeros_like(small)
     at = 0
     for vector, picked in zip((mid_sums, moe_sums, hidden_sums, qkv_sums, router_sums), layout):
         for r in picked:
             at = put_row(small, at, vector[r : r + 1, :])
     sums.begin(5, 0)
-    put_row(pre_tile, put_row(pre_tile, 0, pre_sums[0:1, :]), pre_sums[1:2, :])
-
-    def pre_copy(other, sender):
-        return pltpu.make_async_remote_copy(
-            pre_tile, pre_tiles.at[sender], result_sems.at[0, wide + other], result_sems.at[1, wide + sender],
-            device_id=(other, plane), device_id_type=MESH,
-        )
-
-    def send_pre(d, carry):
-        pre_copy(lax.rem(me + d, wide), me).start()
-        return carry
-
-    lax.fori_loop(1, wide, send_pre, 0)
-    pre_tiles[me] = pre_tile[...]
-    column_dots(context, branch, put_in(proj_total))
-    sums.begin(4, 0)
-
-    def put_thirds(at, tile, value):
-        for s in range(3):
-            there = pl.ds(pl.multiple_of(s * model + at, 16), tile)
-            qkv_total[there, :] = value[:, s * width : (s + 1) * width]
-
-    column_dots(lowered_pre, qkv_grad, put_thirds)
-    sums.begin(2, 0)
-    sums.begin(3, 0)
 
     def finish_chunk(chunk, carry):
         here = pl.ds(pl.multiple_of(chunk * rows, rows), rows)
@@ -934,26 +995,24 @@
         pre_total, pre_other, result_sems.at[0, 2 * wide], result_sems.at[1, 2 * wide],
         device_id=(me, 1 - plane), device_id_type=MESH,
     )
+    ends = (1, 3, 5, 7)
     for k in range(2 * sums.steps):
-        if k < sums.steps:
-            for i in (0, 1):
-                sums.advance(i, sums.steps + k)
+        for i in (0, 1):
+            if len(taken[i]) + k < 2 * sums.steps:
+                sums.advance(i, len(taken[i]) + k)
         for i in (5, 4, 2, 3):
             sums.advance(i, k)
-        if k < sums.steps:
-            lax.fori_loop(k * chunks // sums.steps, (k + 1) * chunks // sums.steps, blend, 0)
-            lax.fori_loop(k * chunks // sums.steps, (k + 1) * chunks // sums.steps, finish_chunk, 0)
-        else:
-            first_chunk = (k - sums.steps) * chunks // sums.steps
-            lax.fori_loop(first_chunk, (k - sums.steps + 1) * chunks // sums.steps, blend_end, 0)
+        if k < chunks:
+            blend(k, 0)
+        if k in ends:
+            finish_chunk(ends.index(k), 0)
         if k == sums.steps - 1:
-            for part in whole_stores[:2]:
-                part.start()
             lax.fori_loop(1, wide, take_pre, 0)
             pre_total[...] = sum(pre_tiles[w] for w in range(wide))
             pre_share.start()
-    for part in whole_stores[2:]:
+    for part in whole_stores:
         part.start()
+    lax.fori_loop(0, chunks, blend_end, 0)
     pre_share.wait()
     pre_tile[...] = pre_total[...] + pre_other[...]
     pre_out[0:1, :] = get_row(pre_tile, 0, model)
@@ -982,7 +1041,11 @@
     for source, picked in zip(ins[pairs:], layout):
         for r in picked:
             out = next(outs)
-            out[...] = source[r : r + out.shape[0], : out.shape[1]]
+            if out.shape[0] == 2:
+                out[0:1, :] = source[0:1, : out.shape[1]]
+                out[1:2, :] = source[0:1, 2 * out.shape[1] :]
+            else:
+                out[...] = source[r : r + out.shape[0], : out.shape[1]]
 
 
 def shards(
@@ -1049,10 +1112,11 @@
         room_for([(array.shape, array.dtype) for array in fetched] + kept
                  + [((8, tokens), jnp.int32), ((count, 128), F32), ((slots, model), BF16), ((slots, model), BF16),
                     ((width, model), BF16), ((tokens, width), BF16), ((tokens, model), BF16), ((tokens, model), BF16),
-                    ((tokens, half), BF16), ((slots, half), BF16), ((slots, half), BF16), ((slots, half), BF16),
+                    ((tokens, half), BF16), ((tokens, half), BF16), ((slots, half), BF16), ((slots, half), BF16),
+                    ((slots, half), BF16), ((slots, half), BF16),
                     ((slots, hidden), BF16), ((slots, hidden), BF16), ((slots, model), BF16), ((slots, half), F32),
                     ((slots, half), BF16), ((slots, half), BF16), ((slots, half), BF16)] + tables)
-        + [pltpu.SemaphoreType.DMA((2, 5 * wide + 3 * groups + 2 * chunks + 2)), pltpu.SemaphoreType.DMA((9,)),
+        + [pltpu.SemaphoreType.DMA((2, 6 * wide + 3 * groups + 2 * chunks + 2)), pltpu.SemaphoreType.DMA((9,)),
            pltpu.SemaphoreType.DMA((chunks,)), pltpu.SemaphoreType.DMA((5, chunks)), pltpu.SemaphoreType.DMA((groups + 1,))],
     )
 
@@ -1090,8 +1154,8 @@
     ]
     singles = [(0, 1), (0, 1, 2), (0, 1, 2), (0,), (0,), (0,), (0,), (0,)]
     sources = [sums[-1]] + list(sums[:-1]) + [in_bias, out_bias]
-    sizes = [(1, model)] * 8 + [(1, hidden), (1, lanes), (count, model), (1, hidden), (1, model)]
-    parts = 4
+    sizes = [(1, model)] * 8 + [(1, hidden), (2, width), (count, model), (1, hidden), (1, model)]
+    parts = 2
 
     def spec(shape):
         if len(shape) == 3:
@@ -1118,7 +1182,7 @@
     hidden_bias_g, qkv_bias_g, router_g, in_bias_g, out_bias_g = outs[16:]
     return (
         block_out, grad, pre_gain_g, pre_shift_g, qkv_g.transpose(1, 0, 2),
-        jnp.concatenate([qkv_bias_g[:, :width], qkv_bias_g[:, 2 * width :]]), proj_g, proj_bias_g, mid_gain_g,
+        qkv_bias_g, proj_g, proj_bias_g, mid_gain_g,
         mid_shift_g, hidden_g, hidden_bias_g.reshape(hidden), output_g, output_bias_g, moe_gain_g, moe_shift_g,
         router_g.T, in_grad[None], in_bias_g, out_grad[None], out_bias_g,
     )

time: 220 us -> 209 us (0.950)
  Pallas kernels: 218 us -> 208 us
    pallas_call x2, Pallas kernels: 209 us -> 200 us  [remote(): pl.pallas_call(kernel, out_shape=[jax.ShapeDtypeStruct(shape, dtype) for...]
where the time goes in v4:
time: 209 us
  Pallas kernels  208 us (100%)
    pallas_call x2, Pallas kernels, remote(): pl.pallas_call(kernel, out_shape=[jax.ShapeDtypeStruct(shape, dtype) for...  200 us
    pallas_call x1, Pallas kernels, shards(): pl.pallas_call(functools.partial(widen, len(pairs), singles), grid=(parts...  7.6 us

profile of v4, /device:TPU:0, one launch (start us, length us, event | category | flops | bytes accessed | tf_op | source)
XLA Modules:
  0.0 208.7 jit_solution(12122427969749276407)
XLA Ops:
  0.7 110.1 %front.1 = (bf16[1152,768]{1,0:T(8,128)(2,1)}, bf16[1152,256]{1,0:T(8,128)(2,1)}, f32[1152,512]{1,0:T(8,128)}, f32[1152,512]{1,0:T(8,128)}, f32[1152,128]{1,0:T(...) custom-call(bf16[1152,512]{1,0:T(8,128)(2,1)} %tokens_h.3, ...), custom_call_target="tpu_custom_call" | custom-call | tf_op jit(solution)/shard_map/front/pallas_call | solution.py:1077
  110.8 90.1 %backward.1 = (bf16[1152,512]{1,0:T(8,128)(2,1)}, f32[1152,512]{1,0:T(8,128)}, bf16[512,1024]{1,0:T(8,128)(2,1)}, bf16[1024,512]{1,0:T(8,128)(2,1)}, bf16[1536,2...) custom-call(f32[1152,512]{1,0:T(8,128)} %get-tuple-element.67.second, ...), custom_call_target="tpu_custom_call" | custom-call | tf_op jit(solution)/shard_map/backward/pallas_call | solution.py:1077
  200.9 7.6 %widen.1 = (bf16[1152,512]{1,0:T(8,128)(2,1)}, f32[1152,512]{1,0:T(8,128)}, f32[512,1024]{1,0:T(8,128)}, f32[1024,512]{1,0:T(8,128)}, f32[3,512,256]{2,1,0:T(8,1...) custom-call(bf16[1152,512]{1,0:T(8,128)(2,1)} %get-tuple-element.76., ...), custom_call_target="tpu_custom_call" | custom-call | tf_op jit(solution)/shard_map/widen/pallas_call | solution.py:1168

commit v5 on v4

--- a/solution.py
+++ b/solution.py
@@ -250,10 +250,10 @@
     tokens_h, cotangent_h, weight_qkv_h, projection_h, hidden_h, output_h, weight_in_h, weight_out_h,
     ids, priority, pre_gain, pre_shift, qv_bias, proj_bias, mid_gain, mid_shift, hidden_bias, output_bias,
     moe_gain, moe_shift, router, bias_in, bias_out,
-    qkv_h, context_h, first_h, second_h, info_h, result_h, in_grad_h, out_grad_h, own_home, peer_home,
+    qkv_h, context_h, first_h, second_h, info_h, result_h, in_grad_h, out_grad_h, fed_h, slope_h, lowered_h, own_home, peer_home,
     gate_home, in_bias_grad, out_bias_grad,
     tokens, cotangent, weight_qkv, projection, hidden, output, weight_in, weight_out,
-    qkv, context, first, second, info, result, in_grad, out_grad,
+    qkv, context, first, second, info, result, in_grad, out_grad, fed, slopes_kept, lowered_mid,
     targets, table, raised_placed, upstream, projection_peer, context_peer, partial_own, partial_peer,
     columns, other_columns, placed, other_placed, rows_own, rows_peer, act, inner_grad, slot_grad, grad_kept, grad_sent, grad_landed,
     grad_back, gate_sent, gate_arrived, gate_back, gate_own, gate_peer,
@@ -303,7 +303,8 @@
     def store(kind, source, target, c):
         return pltpu.make_async_copy(source.at[chunk_of(c)], target.at[chunk_of(c)], store_sems.at[kind, c])
 
-    stores = [(qkv, qkv_h), (context, context_h), (first, first_h), (second, second_h), (info, info_h)]
+    stores = [(qkv, qkv_h), (context, context_h), (first, first_h), (second, second_h), (info, info_h), (fed, fed_h), (slopes_kept, slope_h),
+              (lowered_mid, lowered_h)]
     greet(wide)
 
     def move(source, target, base, sent, landed, device):
@@ -370,9 +371,15 @@
         first[there, :] = value
         normed, _ = normalized(value)
         lowered = (normed * mid_gain[...] + mid_shift[...]).astype(BF16)
-        activated = gelu(dot(lowered, hidden[...]) + hidden_bias[...]).astype(BF16)
+        activated, slope = gelu_parts(dot(lowered, hidden[...]) + hidden_bias[...])
+        activated = activated.astype(BF16)
         partial_own[there, :] = dot(activated, output[...]).astype(BF16)
         across_chunk(partial_own, partial_peer, partial_at, c).start()
+        fed[there, :] = activated
+        slopes_kept[there, :] = slope.astype(BF16)
+        lowered_mid[there, :] = lowered
+        for kind in (5, 6, 7):
+            store(kind, *stores[kind], c).start()
         store(2, first, first_h, c).start()
 
     def route_chunk(c):
@@ -408,9 +415,10 @@
             loads[4].wait()
             find_slots()
 
-        @pl.when(c < groups)
+        @pl.when(c < chunks)
         def _():
-            raise_group(c)
+            for part in range(groups // chunks):
+                raise_group(c * (groups // chunks) + part)
 
         @pl.when(c == 1)
         def _():
@@ -438,10 +446,14 @@
     def other_copy(other, sender):
         return move(other_placed.at[rows_of(other)], rows_peer.at[rows_of(sender)], other_at, other, sender, (other, plane))
 
+    near_groups = groups // 2
+    sides = groups // 4
+
     def turned(k, sign):
-        pairs = groups // 2
-        pair = lax.rem(lax.div(mine, 2) + sign * lax.div(k, 2) + pairs, pairs)
-        return 2 * pair + lax.rem(mine + k, 2), k < 2
+        turn, side = lax.div(k, sides), lax.rem(mine + k, sides)
+        place = lax.div(mine, sides)
+        pair = lax.rem(lax.div(place, 2) + sign * lax.div(turn, 2) + 2, 2)
+        return sides * (2 * pair + lax.rem(place + turn, 2)) + side, k < near_groups
 
     def gate_copy(other, sender):
         return move(gate_sent.at[other], gate_arrived.at[sender], gate_at, other, sender, (other, plane))
@@ -551,12 +563,16 @@
         grad_sent[there, :] = dot_rows(inward, weight_in[peer_half, :]).astype(BF16)
         across(grad_sent, grad_landed, grad_at, p).start()
         grad_kept[there, :] = dot_rows(inward, weight_in[own_half, :])
-        value = dot(acted, weight_out[...]) + bias_out[...] * jnp.where(first_plane, 1.0, 0.0)
+
+    def result_group(k, carry):
+        p, _ = turned(k, -1)
+        there = rows_of_group(p)
+        value = dot(act[there, :], weight_out[...]) + bias_out[...] * jnp.where(first_plane, 1.0, 0.0)
         result[there, :] = value.astype(BF16)
         store_result(p).start()
-        out_bias_grad[0:1, :] += jnp.sum(slot.astype(F32), axis=0, keepdims=True)
-        in_bias_grad[0:1, :] += jnp.sum(inward.astype(F32), axis=0, keepdims=True)
-        slopes = jnp.sum(raised * value, axis=1, keepdims=True)
+        out_bias_grad[0:1, :] += jnp.sum(slot_grad[there, :].astype(F32), axis=0, keepdims=True)
+        in_bias_grad[0:1, :] += jnp.sum(inner_grad[there, :].astype(F32), axis=0, keepdims=True)
+        slopes = jnp.sum(upstream[there, :].astype(F32) * value, axis=1, keepdims=True)
         for j in range(group):
             w = p * group + j
             row = jnp.sum(
@@ -571,6 +587,8 @@
             @pl.when(w == me)
             def _(w=w):
                 gate_own[w] = gate_back[w]
+
+        return carry
 
     own_rows = pltpu.make_async_copy(grad_back.at[rows_of(me)], own_home.at[rows_of(me)], group_sems.at[groups])
 
@@ -590,48 +608,54 @@
             def _(w=w):
                 own_rows.start()
 
+    def share_group(k, carry):
+        q, _ = turned(k, 1)
+        for j in range(group):
+            e = q * group + j
+
+            @pl.when(e != me)
+            def _(e=e):
+                home_copy(e, e).wait_recv()
+
+            @pl.when(e == me)
+            def _():
+                own_rows.wait()
+
+        across(own_home, peer_home, share_at, q).start()
+        return carry
+
     def expert_turn(s, carry):
         @pl.when(s < groups)
         def _():
             join_group(s)
 
-        @pl.when(s < 2)
+        @pl.when(s < near_groups)
         def _():
             expert_group(s)
 
-        @pl.when((s >= 3) & (s <= groups))
+        @pl.when((s > near_groups) & (s <= groups))
         def _():
             expert_group(s - 1)
 
-        @pl.when((s >= 1) & (s <= 2))
+        @pl.when((s >= 1) & (s <= near_groups))
         def _():
             give_back(s - 1)
 
-        @pl.when(s >= 4)
+        @pl.when(s >= near_groups + 2)
         def _():
             give_back(s - 2)
+            share_group(s - near_groups - 2, 0)
 
         return carry
 
     lax.fori_loop(0, groups + 2, expert_turn, 0)
-    own_rows.wait()
-    tile = act.shape[1] // groups
-
-    def share_group(k, carry):
-        at = pl.multiple_of(k * tile, 128)
-        out_grad[pl.ds(at, tile), :] = dot_columns(act[:, pl.ds(at, tile)], slot_grad[...]).astype(BF16)
-        q, _ = turned(k, 1)
-        for j in range(group):
-            e = q * group + j
-
-            @pl.when(e != me)
-            def _(e=e):
-                home_copy(e, e).wait_recv()
-
-        across(own_home, peer_home, share_at, q).start()
-        return carry
-
-    lax.fori_loop(0, groups, share_group, 0)
+    lax.fori_loop(0, groups, result_group, 0)
+    lax.fori_loop(near_groups, groups, share_group, 0)
+
+    def put_out(at, tile, value):
+        out_grad[pl.ds(at, tile), :] = value.astype(BF16)
+
+    column_dots(act, slot_grad, put_out)
     out_store = pltpu.make_async_copy(out_grad, out_grad_h, load_sems.at[7])
     out_store.start()
 
@@ -670,7 +694,7 @@
 
         return carry
 
-    lax.fori_loop(0, 2, end_others, 0)
+    lax.fori_loop(0, near_groups, end_others, 0)
 
     def end_stores(c, carry):
         for kind, (source, target) in enumerate(stores):
@@ -695,19 +719,19 @@
 def backward(
     wide, room, heads, layout, orders, rows,
     second_h, cotangent_h, info_h, first_h, tokens_h, qkv_h, context_h, hidden_h, output_h, projection_h, weight_qkv_h,
-    row_own_h, row_peer_h, result,
-    moe_gain, moe_shift, router, gate_grads, mid_gain, mid_shift, pre_gain, pre_shift, hidden_bias,
+    row_own_h, row_peer_h, act_h, slope_h, lowered_h, result,
+    moe_gain, moe_shift, router, gate_grads, mid_gain, pre_gain, pre_shift,
     block_h, grad_h, hidden_out_h, output_out_h, qkv_out_h, proj_out_h, *rest,
 ):
     vectors_out, pre_out, rest = rest[: len(layout)], rest[len(layout)], rest[len(layout) + 1 :]
     (second, cotangent, info, first, tokens, qkv, context, hidden, output, projection, weight_qkv, row_own, row_peer,
-     block_out, grad_out, hidden_out, output_out, qkv_out, proj_out), rest = rest[:19], rest[19:]
+     act, slopes, lowered_mid, block_out, grad_out, hidden_out, output_out, qkv_out, proj_out), rest = rest[:22], rest[22:]
     load_sems, chunk_sems, store_sems, rest = rest[-3], rest[-2], rest[-1], rest[:-3]
-    (lowered_mid, act, inner_grad, mid_own, mid_peer, branch, qkv_grad, lowered_pre, pre_peer, result_own, blend_peer,
-     pre_tile, pre_tiles, pre_total, pre_other, moe_sums, router_sums, mid_sums, hidden_sums, qkv_sums, pre_sums, small_sums) = rest[:22]
-    hidden_total, output_total, qkv_total, proj_total, small = rest[22:27]
-    sends, lands = rest[27:33], rest[33:39]
-    mid_sems, pre_sems, blend_sems, result_sems, send_sems, recv_sems = rest[39:]
+    (inner_grad, mid_own, mid_peer, branch, qkv_grad, lowered_pre, pre_peer, result_own, blend_peer,
+     pre_tile, pre_tiles, pre_total, pre_other, moe_sums, router_sums, mid_sums, hidden_sums, qkv_sums, pre_sums, small_sums) = rest[:20]
+    hidden_total, output_total, qkv_total, proj_total, small = rest[20:25]
+    sends, lands = rest[25:31], rest[31:37]
+    mid_sems, pre_sems, blend_sems, result_sems, send_sems, recv_sems = rest[37:]
     blend_own = lowered_mid
     me, plane = lax.axis_index("wide"), lax.axis_index("tensor")
     chunks = tokens.shape[0] // rows
@@ -724,8 +748,9 @@
     def chunk_of(index):
         return pl.ds(pl.multiple_of(index * rows, 16), rows)
 
-    early = [(info_h, info), (second_h, second), (cotangent_h, cotangent), (first_h, first)]
-    late = [(tokens_h, tokens), (qkv_h, qkv)]
+    early = [(info_h, info), (second_h, second), (cotangent_h, cotangent), (slope_h, slopes)]
+    late = [(tokens_h, tokens), (qkv_h, qkv), (first_h, first)]
+    middle = [(lowered_h, lowered_mid), (act_h, act)]
 
     def load(kind, pair, c):
         return pltpu.make_async_copy(pair[0].at[chunk_of(c)], pair[1].at[chunk_of(c)], chunk_sems.at[kind, c])
@@ -740,6 +765,9 @@
             load(len(early) + kind, pair, c).start()
         return carry
 
+    middle_loads = [
+        pltpu.make_async_copy(source, target, load_sems.at[12 + i]) for i, (source, target) in enumerate(middle)
+    ]
     loads = [
         pltpu.make_async_copy(source, target, load_sems.at[i])
         for i, (source, target) in enumerate(
@@ -754,6 +782,8 @@
         part.start()
     lax.fori_loop(1, chunks, start_early, 0)
     for part in loads[4:]:
+        part.start()
+    for part in middle_loads:
         part.start()
     lax.fori_loop(0, chunks, start_late, 0)
     whole_stores = [
@@ -837,12 +867,7 @@
             loads[2].wait()
             loads[3].wait()
 
-        normed, _ = normalized(first[here, :])
-        lowered = (normed * mid_gain[...] + mid_shift[...]).astype(BF16)
-        lowered_mid[here, :] = lowered
-        acted, slope = gelu_parts(dot(lowered, hidden[...]) + hidden_bias[...])
-        act[here, :] = acted.astype(BF16)
-        inward = (dot_rows(branch[here, :], output[...]) * slope).astype(BF16)
+        inward = (dot_rows(branch[here, :], output[...]) * slopes[here, :].astype(F32)).astype(BF16)
         inner_grad[here, :] = inward
         hidden_sums[0:1, :] += jnp.sum(inward.astype(F32), axis=0, keepdims=True)
         mid_own[here, :] = dot_rows(inward, hidden[...]).astype(BF16)
@@ -859,6 +884,8 @@
 
         return put
 
+    for part in middle_loads:
+        part.wait()
     column_dots(lowered_mid, inner_grad, put_in(hidden_total))
     sums.begin(0, 0)
     column_dots(act, branch, put_in(output_total))
@@ -1066,7 +1093,7 @@
     lanes = 3 * width
     rows = 2 * PATCHES
     chunks = tokens // rows
-    group = 4
+    group = 2
     steps = wide.bit_length() - 1
 
     def row(vector):
@@ -1098,11 +1125,13 @@
     kept = [
         ((tokens, lanes), BF16), ((tokens, width), BF16), ((tokens, model), F32), ((tokens, model), F32),
         ((tokens, 128), F32), ((slots, model), BF16), ((model, hidden), BF16), ((hidden, model), BF16),
+        ((tokens, hidden), BF16), ((tokens, hidden), BF16), ((tokens, model), BF16),
     ]
     homes = [((slots, half), BF16), ((slots, half), BF16)]
     fetched = [tokens_in, cotangent, weight_qkv, proj_weight, hidden_weight, output_weight, expert_in[0], expert_out[0]]
     tables = [((count, 8, 128), F32)] * 5
-    qkv, context, first, second, info, result, in_grad, out_grad, row_own, row_peer, gate_grads, in_bias, out_bias = remote(
+    (qkv, context, first, second, info, result, in_grad, out_grad, fed, slopes, lowered, row_own, row_peer, gate_grads,
+     in_bias, out_bias) = remote(
         functools.partial(front, wide, room, group, heads, rows, count), "front", 1,
         fetched,
         [expert_ids.T, priority, pre_gain, pre_shift, qv_bias, proj_bias, mid_gain, mid_shift, hidden_bias, output_bias,
@@ -1117,14 +1146,15 @@
                     ((slots, hidden), BF16), ((slots, hidden), BF16), ((slots, model), BF16), ((slots, half), F32),
                     ((slots, half), BF16), ((slots, half), BF16), ((slots, half), BF16)] + tables)
         + [pltpu.SemaphoreType.DMA((2, 6 * wide + 3 * groups + 2 * chunks + 2)), pltpu.SemaphoreType.DMA((9,)),
-           pltpu.SemaphoreType.DMA((chunks,)), pltpu.SemaphoreType.DMA((5, chunks)), pltpu.SemaphoreType.DMA((groups + 1,))],
+           pltpu.SemaphoreType.DMA((chunks,)), pltpu.SemaphoreType.DMA((8, chunks)), pltpu.SemaphoreType.DMA((groups + 1,))],
     )
 
     layout = [(0, 1, 2), (0, 1, 2), (0,), (0,), tuple(range(count))]
     vectors = [((8, model), F32), ((8, model), F32), ((8, hidden), F32), ((8, lanes), F32), ((count, model), F32)]
     near, far = tuple(range(steps)), (0,) + tuple(range(2, steps)) + (1,)
     summed = [(model, hidden), (hidden, model), (3 * model // 2, width), (3 * model // 2, width), (width, model), (16 * wide, 128)]
-    fetched = [second, cotangent, info, first, tokens_in, qkv, context, hidden_weight, output_weight, proj_weight, weight_qkv, row_own, row_peer]
+    fetched = [second, cotangent, info, first, tokens_in, qkv, context, hidden_weight, output_weight, proj_weight, weight_qkv, row_own, row_peer,
+               fed, slopes, lowered]
     given = [
         ((tokens, model), BF16), ((tokens, model), F32), ((model, hidden), BF16), ((hidden, model), BF16),
         ((3 * model, width), BF16), ((width, model), BF16),
@@ -1133,10 +1163,10 @@
     block_out, grad, hidden_g, output_g, qkv_g, proj_g, *sums = remote(
         functools.partial(backward, wide, room, heads, layout, (near, far, near, far, near, far), rows), "backward", 2,
         fetched + [result],
-        [moe_gain, moe_shift, router, gate_grads, mid_gain, mid_shift, pre_gain, pre_shift, hidden_bias],
+        [moe_gain, moe_shift, router, gate_grads, mid_gain, pre_gain, pre_shift],
         given, vectors + [((8, model), F32)],
         room_for([(array.shape, array.dtype) for array in fetched] + given
-                 + [((tokens, model), BF16), ((tokens, hidden), BF16), ((tokens, hidden), BF16), ((tokens, model), BF16),
+                 + [((tokens, hidden), BF16), ((tokens, model), BF16),
                     ((tokens, model), BF16), ((tokens, model), BF16), ((tokens, lanes), BF16), ((tokens, model), BF16),
                     ((tokens, model), BF16), ((slots, model), BF16), ((tokens, model), BF16),
                     (tile, F32), ((wide,) + tile, F32), (tile, F32), (tile, F32), ((8, model), F32), ((count, model), F32),
@@ -1145,7 +1175,7 @@
                  + [(shape, BF16) for shape in summed] * 2)
         + [pltpu.SemaphoreType.DMA((2, chunks))] * 3 + [pltpu.SemaphoreType.DMA((2, 2 * wide + 1))]
         + [pltpu.SemaphoreType.DMA((len(summed), 2 * steps))] * 2
-        + [pltpu.SemaphoreType.DMA((12,)), pltpu.SemaphoreType.DMA((6, chunks)), pltpu.SemaphoreType.DMA((2, chunks))],
+        + [pltpu.SemaphoreType.DMA((14,)), pltpu.SemaphoreType.DMA((7, chunks)), pltpu.SemaphoreType.DMA((2, chunks))],
     )
 
     pairs = [

time: 209 us -> 208 us (level)
  no operation moved by 1% of the time
where the time goes in v5:
time: 208 us; the launch traced here: 207 us
  Pallas kernels  207 us (100%)
    pallas_call x2, Pallas kernels, remote(): pl.pallas_call(kernel, out_shape=[jax.ShapeDtypeStruct(shape, dtype) for...  199 us
    pallas_call x1, Pallas kernels, shards(): pl.pallas_call(functools.partial(widen, len(pairs), singles), grid=(parts...  7.6 us

profile of v5, /device:TPU:0, one launch (start us, length us, event | category | flops | bytes accessed | tf_op | source)
XLA Modules:
  0.0 207.4 jit_solution(13938890748463663641)
XLA Ops:
  0.7 110.9 %front.1 = (bf16[1152,768]{1,0:T(8,128)(2,1)}, bf16[1152,256]{1,0:T(8,128)(2,1)}, f32[1152,512]{1,0:T(8,128)}, f32[1152,512]{1,0:T(8,128)}, f32[1152,128]{1,0:T(...) custom-call(bf16[1152,512]{1,0:T(8,128)(2,1)} %tokens_h.3, ...), custom_call_target="tpu_custom_call" | custom-call | tf_op jit(solution)/shard_map/front/pallas_call | solution.py:1104
  111.6 88.1 %backward.1 = (bf16[1152,512]{1,0:T(8,128)(2,1)}, f32[1152,512]{1,0:T(8,128)}, bf16[512,1024]{1,0:T(8,128)(2,1)}, bf16[1024,512]{1,0:T(8,128)(2,1)}, bf16[1536,2...) custom-call(f32[1152,512]{1,0:T(8,128)} %get-tuple-element.70.second, ...), custom_call_target="tpu_custom_call" | custom-call | tf_op jit(solution)/shard_map/backward/pallas_call | solution.py:1104
  199.7 7.6 %widen.1 = (bf16[1152,512]{1,0:T(8,128)(2,1)}, f32[1152,512]{1,0:T(8,128)}, f32[512,1024]{1,0:T(8,128)}, f32[1024,512]{1,0:T(8,128)}, f32[3,512,256]{2,1,0:T(8,1...) custom-call(bf16[1152,512]{1,0:T(8,128)(2,1)} %get-tuple-element.82., ...), custom_call_target="tpu_custom_call" | custom-call | tf_op jit(solution)/shard_map/widen/pallas_call | solution.py:1198

commit v6 on v5

--- a/solution.py
+++ b/solution.py
@@ -1022,7 +1022,7 @@
         pre_total, pre_other, result_sems.at[0, 2 * wide], result_sems.at[1, 2 * wide],
         device_id=(me, 1 - plane), device_id_type=MESH,
     )
-    ends = (1, 3, 5, 7)
+    ends = (4, 5, 6, 7)
     for k in range(2 * sums.steps):
         for i in (0, 1):
             if len(taken[i]) + k < 2 * sums.steps:
@@ -1128,11 +1128,12 @@
         ((tokens, hidden), BF16), ((tokens, hidden), BF16), ((tokens, model), BF16),
     ]
     homes = [((slots, half), BF16), ((slots, half), BF16)]
+    images = tokens // PATCHES
     fetched = [tokens_in, cotangent, weight_qkv, proj_weight, hidden_weight, output_weight, expert_in[0], expert_out[0]]
     tables = [((count, 8, 128), F32)] * 5
     (qkv, context, first, second, info, result, in_grad, out_grad, fed, slopes, lowered, row_own, row_peer, gate_grads,
      in_bias, out_bias) = remote(
-        functools.partial(front, wide, room, group, heads, rows, count), "front", 1,
+        functools.partial(front, wide, room, group, heads, PATCHES, count), "front", 1,
         fetched,
         [expert_ids.T, priority, pre_gain, pre_shift, qv_bias, proj_bias, mid_gain, mid_shift, hidden_bias, output_bias,
          moe_gain, moe_shift, router, expert_in_bias, expert_out_bias],
@@ -1145,8 +1146,8 @@
                     ((slots, half), BF16), ((slots, half), BF16),
                     ((slots, hidden), BF16), ((slots, hidden), BF16), ((slots, model), BF16), ((slots, half), F32),
                     ((slots, half), BF16), ((slots, half), BF16), ((slots, half), BF16)] + tables)
-        + [pltpu.SemaphoreType.DMA((2, 6 * wide + 3 * groups + 2 * chunks + 2)), pltpu.SemaphoreType.DMA((9,)),
-           pltpu.SemaphoreType.DMA((chunks,)), pltpu.SemaphoreType.DMA((8, chunks)), pltpu.SemaphoreType.DMA((groups + 1,))],
+        + [pltpu.SemaphoreType.DMA((2, 6 * wide + 3 * groups + 2 * images + 2)), pltpu.SemaphoreType.DMA((9,)),
+           pltpu.SemaphoreType.DMA((images,)), pltpu.SemaphoreType.DMA((8, images)), pltpu.SemaphoreType.DMA((groups + 1,))],
     )
 
     layout = [(0, 1, 2), (0, 1, 2), (0,), (0,), tuple(range(count))]

time: 208 us -> 208 us (level)
  no operation moved by 1% of the time
where the time goes in v6:
time: 208 us; the launch traced here: 207 us
  Pallas kernels  206 us (99%)
    pallas_call x2, Pallas kernels, remote(): pl.pallas_call(kernel, out_shape=[jax.ShapeDtypeStruct(shape, dtype) for...  199 us
    pallas_call x1, Pallas kernels, shards(): pl.pallas_call(functools.partial(widen, len(pairs), singles), grid=(parts...  7.6 us

profile of v6, /device:TPU:0, one launch (start us, length us, event | category | flops | bytes accessed | tf_op | source)
XLA Modules:
  0.0 207.2 jit_solution(7131000317599717419)
XLA Ops:
  0.7 108.7 %front.1 = (bf16[1152,768]{1,0:T(8,128)(2,1)}, bf16[1152,256]{1,0:T(8,128)(2,1)}, f32[1152,512]{1,0:T(8,128)}, f32[1152,512]{1,0:T(8,128)}, f32[1152,128]{1,0:T(...) custom-call(bf16[1152,512]{1,0:T(8,128)(2,1)} %tokens_h.3, ...), custom_call_target="tpu_custom_call" | custom-call | tf_op jit(solution)/shard_map/front/pallas_call | solution.py:1104
  109.4 90.0 %backward.1 = (bf16[1152,512]{1,0:T(8,128)(2,1)}, f32[1152,512]{1,0:T(8,128)}, bf16[512,1024]{1,0:T(8,128)(2,1)}, bf16[1024,512]{1,0:T(8,128)(2,1)}, bf16[1536,2...) custom-call(f32[1152,512]{1,0:T(8,128)} %get-tuple-element.70.second, ...), custom_call_target="tpu_custom_call" | custom-call | tf_op jit(solution)/shard_map/backward/pallas_call | solution.py:1104
  199.5 7.6 %widen.1 = (bf16[1152,512]{1,0:T(8,128)(2,1)}, f32[1152,512]{1,0:T(8,128)}, f32[512,1024]{1,0:T(8,128)}, f32[1024,512]{1,0:T(8,128)}, f32[3,512,256]{2,1,0:T(8,1...) custom-call(bf16[1152,512]{1,0:T(8,128)(2,1)} %get-tuple-element.82., ...), custom_call_target="tpu_custom_call" | custom-call | tf_op jit(solution)/shard_map/widen/pallas_call | solution.py:1199
